TPU v7x, 32 devices: a whole 2x2x4 slice. The times are simulated.
32 devices in a mesh: dp: 8 (over y, x, core), mp: 4 (over z).
Axes of the slice: x: 2, y: 2, z: 4, core: 2. Of those that a mesh axis runs over, the one named last changes fastest.
Arguments:
- encoder_input: bfloat16 [4096, 768], P(('dp', 'mp')), may hold values from -6 to 6
- encoder_upstream: bfloat16 [4096, 768], P(('dp', 'mp')), may hold values from -6 to 6
- memory_index: int32 [64, 10], P('dp'), may hold values from 0 to 1023
- memory_table: bfloat16 [1024, 2, 768], replicated, may hold values from -6 to 6
- encoder_bucket: int32 [64, 64], replicated, may hold values from 0 to 31
- encoder_bias: float32 [32, 12], replicated, may hold values from -4 to 4
- encoder_gain: float32 [768], replicated, may hold values from 0.5 to 1.5
- encoder_query: bfloat16 [768, 768], P(None, 'mp'), may hold values from -0.0546875 to 0.0546875
- encoder_key: bfloat16 [768, 768], P(None, 'mp'), may hold values from -0.21875 to 0.21875
- encoder_value: bfloat16 [768, 768], P(None, 'mp'), may hold values from -0.21875 to 0.21875
- encoder_merge: bfloat16 [768, 768], P('mp'), may hold values from -0.4375 to 0.4375
- encoder_later_gain: float32 [768], replicated, may hold values from 0.5 to 1.5
- encoder_widen: bfloat16 [768, 3072], P(None, 'mp'), may hold values from -0.21875 to 0.21875
- encoder_narrow: bfloat16 [3072, 768], P('mp'), may hold values from -0.15625 to 0.15625
- decoder_input: bfloat16 [4096, 768], P(('dp', 'mp')), may hold values from -6 to 6
- decoder_upstream: bfloat16 [4096, 768], P(('dp', 'mp')), may hold values from -6 to 6
- encoder_states: bfloat16 [4096, 768], P(('dp', 'mp')), may hold values from -6 to 6
- decoder_bucket: int32 [64, 64], replicated, may hold values from 0 to 31
- decoder_bias: float32 [32, 12], replicated, may hold values from -4 to 4
- decoder_gain: float32 [768], replicated, may hold values from 0.5 to 1.5
- decoder_query: bfloat16 [768, 768], P(None, 'mp'), may hold values from -0.0546875 to 0.0546875
- decoder_key: bfloat16 [768, 768], P(None, 'mp'), may hold values from -0.21875 to 0.21875
- decoder_value: bfloat16 [768, 768], P(None, 'mp'), may hold values from -0.21875 to 0.21875
- decoder_merge: bfloat16 [768, 768], P('mp'), may hold values from -0.4375 to 0.4375
- cross_gain: float32 [768], replicated, may hold values from 0.5 to 1.5
- cross_query: bfloat16 [768, 768], P(None, 'mp'), may hold values from -0.0546875 to 0.0546875
- cross_key: bfloat16 [768, 768], P(None, 'mp'), may hold values from -0.21875 to 0.21875
- cross_value: bfloat16 [768, 768], P(None, 'mp'), may hold values from -0.21875 to 0.21875
- cross_merge: bfloat16 [768, 768], P('mp'), may hold values from -0.4375 to 0.4375
- decoder_later_gain: float32 [768], replicated, may hold values from 0.5 to 1.5
- decoder_widen: bfloat16 [768, 3072], P(None, 'mp'), may hold values from -0.21875 to 0.21875
- decoder_narrow: bfloat16 [3072, 768], P('mp'), may hold values from -0.15625 to 0.15625
Outputs:
- encoder_output: bfloat16 [4096, 768], P(('dp', 'mp'))
- encoder_input_grad: float32 [4096, 768], P(('dp', 'mp'))
- memory_table_grad: float32 [1024, 2, 768], P(('dp', 'mp'))
- encoder_bias_grad: float32 [32, 12], replicated
- encoder_gain_grad: float32 [768], replicated
- encoder_query_grad: float32 [768, 768], P('dp', 'mp')
- encoder_key_grad: float32 [768, 768], P('dp', 'mp')
- encoder_value_grad: float32 [768, 768], P('dp', 'mp')
- encoder_merge_grad: float32 [768, 768], P('mp', 'dp')
- encoder_later_gain_grad: float32 [768], replicated
- encoder_widen_grad: float32 [768, 3072], P('dp', 'mp')
- encoder_narrow_grad: float32 [3072, 768], P('mp', 'dp')
- decoder_output: bfloat16 [4096, 768], P(('dp', 'mp'))
- decoder_input_grad: float32 [4096, 768], P(('dp', 'mp'))
- encoder_states_grad: float32 [4096, 768], P(('dp', 'mp'))
- decoder_bias_grad: float32 [32, 12], replicated
- decoder_gain_grad: float32 [768], replicated
- decoder_query_grad: float32 [768, 768], P('dp', 'mp')
- decoder_key_grad: float32 [768, 768], P('dp', 'mp')
- decoder_value_grad: float32 [768, 768], P('dp', 'mp')
- decoder_merge_grad: float32 [768, 768], P('mp', 'dp')
- cross_gain_grad: float32 [768], replicated
- cross_query_grad: float32 [768, 768], P('dp', 'mp')
- cross_key_grad: float32 [768, 768], P('dp', 'mp')
- cross_value_grad: float32 [768, 768], P('dp', 'mp')
- cross_merge_grad: float32 [768, 768], P('mp', 'dp')
- decoder_later_gain_grad: float32 [768], replicated
- decoder_widen_grad: float32 [768, 3072], P('dp', 'mp')
- decoder_narrow_grad: float32 [3072, 768], P('mp', 'dp')
All inputs are finite; a program needn't handle non-finite values.
Results may differ from a plain program's by a relative error of at most 0.024.
The roundings to bfloat16 on the way count: a program that leaves them out, or rounds other values in their place, can miss the bound.
Values may be sent and summed in bfloat16 or wider, within the bound.
No kernel may reach another device: no remote copies, remote signals or barrier semaphores. Data moves between devices by JAX's collectives and lax.ppermute only.
A program may use at most 192 MiB of HBM per device.

v0:
```python
import jax
import jax.numpy as jnp
from jax import lax
from jax.sharding import PartitionSpec as P

DH = 64
SEQ = 64
MEMK = 10
PREFIX = 2


epsilon = 1e-06


def matmul_plain(left, right):
    return jnp.dot(left, right, preferred_element_type=jnp.float32)


def matmul_rows(left, right):
    return lax.dot_general(
        left, right, (((0,), (0,)), ((), ())), preferred_element_type=jnp.float32
    )


def matmul_cols(left, right):
    return lax.dot_general(
        left, right, (((1,), (1,)), ((), ())), preferred_element_type=jnp.float32
    )


def smooth_unit(value):
    return jax.nn.gelu(value, approximate=True)


def norm_apply(residual, norm_gain):
    return (
        residual
        * lax.rsqrt(jnp.mean(residual * residual, axis=-1, keepdims=True) + epsilon)
        * norm_gain
    )


def to_heads(rows, length, heads_here):
    return rows.astype(jnp.bfloat16).reshape(-1, length, heads_here, DH)


def to_flat(grads, heads_here):
    return grads.reshape(-1, heads_here * DH).astype(jnp.bfloat16)


def gather_rows(shard):
    return lax.all_gather(shard, "mp", axis=0, tiled=True)


def sum_rows(partial_rows):
    return lax.psum_scatter(partial_rows, "mp", scatter_dimension=0, tiled=True)


def spread_grad(grad_rows):
    return lax.all_gather(grad_rows.astype(jnp.bfloat16), "mp", axis=0, tiled=True)


def collect_grad(partial_rows):
    return lax.psum_scatter(
        partial_rows.astype(jnp.bfloat16), "mp", scatter_dimension=0, tiled=True
    ).astype(jnp.float32)


def bucket_bias(bucket, bias_table, heads_here):
    offset = lax.axis_index("mp") * heads_here
    local_part = lax.dynamic_slice_in_dim(bias_table, offset, heads_here, 1)
    onehot = (
        bucket.reshape(-1, 1) == lax.broadcasted_iota(jnp.int32, (1, bias_table.shape[0]), 1)
    ).astype(jnp.float32)
    looked = jnp.dot(onehot, local_part, precision=lax.Precision.HIGHEST)
    return (jnp.transpose(looked.reshape(SEQ, SEQ, heads_here), (2, 0, 1)), onehot)


def bucket_grad(onehot, grad_bias, bias_table):
    heads_here = grad_bias.shape[0]
    flat_grads = jnp.transpose(grad_bias, (1, 2, 0)).reshape(-1, heads_here)
    local_part = jnp.dot(onehot.T, flat_grads, precision=lax.Precision.HIGHEST)
    return lax.dynamic_update_slice_in_dim(
        jnp.zeros(bias_table.shape, jnp.float32), local_part, lax.axis_index("mp") * heads_here, 1
    )


def attention_core(queries, key_heads, value_heads, score_bias):
    scores = (
        jnp.einsum("slhd,smhd->shlm", queries, key_heads, preferred_element_type=jnp.float32)
        + score_bias
    )
    row_peak = jnp.max(scores, axis=-1, keepdims=True)
    shifted = jnp.exp(scores - row_peak)
    row_total = jnp.sum(shifted, axis=-1, keepdims=True)
    softmax_rows = (shifted / row_total).astype(jnp.bfloat16)
    mixture = jnp.einsum(
        "shlm,smhd->slhd", softmax_rows, value_heads, preferred_element_type=jnp.float32
    )
    return (mixture, row_peak + jnp.log(row_total))


def attention_grads(queries, key_heads, value_heads, score_bias, log_total, grad_mixture):
    scores = (
        jnp.einsum("slhd,smhd->shlm", queries, key_heads, preferred_element_type=jnp.float32)
        + score_bias
    )
    softmax_rows = jnp.exp(scores - log_total)
    grad_values = jnp.einsum(
        "shlm,slhd->smhd",
        softmax_rows.astype(jnp.bfloat16),
        grad_mixture,
        preferred_element_type=jnp.float32,
    )
    grad_chances = jnp.einsum(
        "slhd,smhd->shlm", grad_mixture, value_heads, preferred_element_type=jnp.float32
    )
    inner = jnp.sum(grad_chances * softmax_rows, axis=-1, keepdims=True)
    grad_scores = (softmax_rows * (grad_chances - inner)).astype(jnp.bfloat16)
    grad_queries = jnp.einsum(
        "shlm,smhd->slhd", grad_scores, key_heads, preferred_element_type=jnp.float32
    )
    grad_keys = jnp.einsum(
        "shlm,slhd->smhd", grad_scores, queries, preferred_element_type=jnp.float32
    )
    return (grad_queries, grad_keys, grad_values, grad_scores)


def attention_forward(
    residual, norm_gain, w_query, w_key, w_value, w_merge, score_bias, source, prefix
):
    heads_here = w_query.shape[1] // DH
    normed = norm_apply(residual, norm_gain).astype(jnp.bfloat16)
    gathered = gather_rows(normed)
    key_source = gathered if source is None else source[1]
    queries = to_heads(matmul_plain(gathered, w_query), SEQ, heads_here)
    key_heads = to_heads(matmul_plain(key_source, w_key), SEQ, heads_here)
    value_heads = to_heads(matmul_plain(key_source, w_value), SEQ, heads_here)
    if prefix is not None:
        count = MEMK * PREFIX
        key_heads = jnp.concatenate(
            [to_heads(matmul_plain(prefix, w_key), count, heads_here), key_heads], axis=1
        )
        value_heads = jnp.concatenate(
            [to_heads(matmul_plain(prefix, w_value), count, heads_here), value_heads], axis=1
        )
    mixture, log_total = attention_core(queries, key_heads, value_heads, score_bias)
    mixture = to_flat(mixture, heads_here)
    output = residual + sum_rows(matmul_plain(mixture, w_merge))
    return (
        output,
        (residual, normed, gathered, queries, key_heads, value_heads, log_total, mixture),
    )


def attention_backward(
    stored, norm_gain, w_query, w_key, w_value, w_merge, score_bias, source, prefix, grad_output
):
    residual, normed, gathered, queries, key_heads, value_heads, log_total, mixture = stored
    heads_here = w_query.shape[1] // DH
    grad_rows = spread_grad(grad_output)
    grad_merge = matmul_rows(mixture, grad_rows)
    grad_mixture = to_heads(matmul_cols(grad_rows, w_merge), SEQ, heads_here)
    grad_queries, grad_keys, grad_values, grad_scores = attention_grads(
        queries, key_heads, value_heads, score_bias, log_total, grad_mixture
    )
    offset = 0 if prefix is None else MEMK * PREFIX
    query_part = to_flat(grad_queries, heads_here)
    key_part = to_flat(grad_keys[:, offset:], heads_here)
    value_part = to_flat(grad_values[:, offset:], heads_here)
    key_source = gathered if source is None else source[1]
    grad_query_w = matmul_rows(gathered, query_part)
    grad_key_w = matmul_rows(key_source, key_part)
    grad_value_w = matmul_rows(key_source, value_part)
    grad_inputs = matmul_cols(query_part, w_query)
    grad_sources = matmul_cols(key_part, w_key) + matmul_cols(value_part, w_value)
    grad_prefix = None
    if prefix is not None:
        key_memory = to_flat(grad_keys[:, :offset], heads_here)
        value_memory = to_flat(grad_values[:, :offset], heads_here)
        grad_key_w = grad_key_w + matmul_rows(prefix, key_memory)
        grad_value_w = grad_value_w + matmul_rows(prefix, value_memory)
        grad_prefix = matmul_cols(key_memory, w_key) + matmul_cols(value_memory, w_value)
    grad_source = None
    if source is None:
        grad_inputs = grad_inputs + grad_sources
    else:
        grad_source = collect_grad(grad_sources)
    grad_normed = collect_grad(grad_inputs)
    forward_value, norm_pull = jax.vjp(norm_apply, residual, norm_gain)
    grad_residual, grad_gain = norm_pull(grad_normed)
    grad_bias = jnp.sum(grad_scores[..., offset:].astype(jnp.float32), axis=0)
    return (
        grad_output + grad_residual,
        grad_gain,
        (grad_query_w, grad_key_w, grad_value_w, grad_merge),
        grad_prefix,
        grad_source,
        grad_bias,
    )


def ffn_forward(residual, norm_gain, widen, narrow):
    normed = norm_apply(residual, norm_gain).astype(jnp.bfloat16)
    gathered = gather_rows(normed)
    before_unit = matmul_plain(gathered, widen)
    hidden = smooth_unit(before_unit).astype(jnp.bfloat16)
    output = residual + sum_rows(matmul_plain(hidden, narrow))
    return (output, (residual, normed, gathered, before_unit, hidden))


def ffn_backward(stored, norm_gain, widen, narrow, grad_output):
    residual, normed, gathered, before_unit, hidden = stored
    grad_rows = spread_grad(grad_output)
    grad_narrow = matmul_rows(hidden, grad_rows)
    unit_value, unit_pull = jax.vjp(smooth_unit, before_unit)
    grad_before = unit_pull(matmul_cols(grad_rows, narrow))[0].astype(jnp.bfloat16)
    grad_widen = matmul_rows(gathered, grad_before)
    grad_normed = collect_grad(matmul_cols(grad_before, widen))
    forward_value, norm_pull = jax.vjp(norm_apply, residual, norm_gain)
    grad_residual, grad_gain = norm_pull(grad_normed)
    return (grad_output + grad_residual, grad_gain, grad_widen, grad_narrow)


def shards(
    encoder_input,
    encoder_upstream,
    memory_index,
    memory_table,
    encoder_bucket,
    encoder_bias,
    encoder_gain,
    encoder_query,
    encoder_key,
    encoder_value,
    encoder_merge,
    encoder_later_gain,
    encoder_widen,
    encoder_narrow,
    decoder_input,
    decoder_upstream,
    encoder_states,
    decoder_bucket,
    decoder_bias,
    decoder_gain,
    decoder_query,
    decoder_key,
    decoder_value,
    decoder_merge,
    cross_gain,
    cross_query,
    cross_key,
    cross_value,
    cross_merge,
    decoder_later_gain,
    decoder_widen,
    decoder_narrow,
):
    heads_here = encoder_query.shape[1] // DH
    value_rows = memory_table.reshape(memory_table.shape[0], -1)
    flat_index = memory_index.reshape(-1)
    prefix = jnp.take(value_rows, flat_index, axis=0).reshape(-1, memory_table.shape[2])
    encoder_relative, encoder_onehot = bucket_bias(encoder_bucket, encoder_bias, heads_here)
    encoder_mask = jnp.concatenate(
        [jnp.zeros((heads_here, SEQ, MEMK * PREFIX), jnp.float32), encoder_relative], axis=2
    )[None]
    middle, encoder_attention = attention_forward(
        encoder_input.astype(jnp.float32),
        encoder_gain,
        encoder_query,
        encoder_key,
        encoder_value,
        encoder_merge,
        encoder_mask,
        None,
        prefix,
    )
    encoder_final, encoder_ffn = ffn_forward(
        middle, encoder_later_gain, encoder_widen, encoder_narrow
    )
    grad_middle, encoder_later_grad, encoder_widen_grad, encoder_narrow_grad = ffn_backward(
        encoder_ffn,
        encoder_later_gain,
        encoder_widen,
        encoder_narrow,
        encoder_upstream.astype(jnp.float32),
    )
    (
        encoder_input_grad,
        encoder_gain_grad,
        encoder_mats,
        prefix_grad,
        encoder_nothing,
        encoder_scores,
    ) = attention_backward(
        encoder_attention,
        encoder_gain,
        encoder_query,
        encoder_key,
        encoder_value,
        encoder_merge,
        encoder_mask,
        None,
        prefix,
        grad_middle,
    )
    encoder_bias_grad = bucket_grad(encoder_onehot, encoder_scores, encoder_bias)
    table_local = (
        jnp.zeros(value_rows.shape, jnp.float32)
        .at[flat_index]
        .add(prefix_grad.reshape(flat_index.shape[0], -1))
    )
    table_grad = lax.psum_scatter(
        table_local.reshape(memory_table.shape), ("dp", "mp"), scatter_dimension=0, tiled=True
    )
    decoder_relative, decoder_onehot = bucket_bias(decoder_bucket, decoder_bias, heads_here)
    row_place = lax.broadcasted_iota(jnp.int32, (SEQ, SEQ), 0)
    col_place = lax.broadcasted_iota(jnp.int32, (SEQ, SEQ), 1)
    causal_mask = jnp.where(col_place <= row_place, decoder_relative, -1000000000.0)[None]
    plain_mask = jnp.zeros((1, 1, 1, 1), jnp.float32)
    states_full = gather_rows(encoder_states)
    source = (encoder_states, states_full)
    after_self, self_stored = attention_forward(
        decoder_input.astype(jnp.float32),
        decoder_gain,
        decoder_query,
        decoder_key,
        decoder_value,
        decoder_merge,
        causal_mask,
        None,
        None,
    )
    after_cross, cross_stored = attention_forward(
        after_self,
        cross_gain,
        cross_query,
        cross_key,
        cross_value,
        cross_merge,
        plain_mask,
        source,
        None,
    )
    decoder_final, decoder_ffn = ffn_forward(
        after_cross, decoder_later_gain, decoder_widen, decoder_narrow
    )
    grad_cross, decoder_later_grad, decoder_widen_grad, decoder_narrow_grad = ffn_backward(
        decoder_ffn,
        decoder_later_gain,
        decoder_widen,
        decoder_narrow,
        decoder_upstream.astype(jnp.float32),
    )
    grad_self, cross_gain_grad, cross_mats, cross_nothing, states_grad, cross_scores = (
        attention_backward(
            cross_stored,
            cross_gain,
            cross_query,
            cross_key,
            cross_value,
            cross_merge,
            plain_mask,
            source,
            None,
            grad_cross,
        )
    )
    decoder_input_grad, decoder_gain_grad, self_mats, self_nothing, self_empty, self_scores = (
        attention_backward(
            self_stored,
            decoder_gain,
            decoder_query,
            decoder_key,
            decoder_value,
            decoder_merge,
            causal_mask,
            None,
            None,
            grad_self,
        )
    )
    decoder_bias_grad = bucket_grad(decoder_onehot, self_scores, decoder_bias)
    every_sum = (
        lax.psum_scatter(encoder_mats[0], "dp", scatter_dimension=0, tiled=True),
        lax.psum_scatter(encoder_mats[1], "dp", scatter_dimension=0, tiled=True),
        lax.psum_scatter(encoder_mats[2], "dp", scatter_dimension=0, tiled=True),
        lax.psum_scatter(encoder_mats[3], "dp", scatter_dimension=1, tiled=True),
        lax.psum_scatter(encoder_widen_grad, "dp", scatter_dimension=0, tiled=True),
        lax.psum_scatter(encoder_narrow_grad, "dp", scatter_dimension=1, tiled=True),
        lax.psum_scatter(self_mats[0], "dp", scatter_dimension=0, tiled=True),
        lax.psum_scatter(self_mats[1], "dp", scatter_dimension=0, tiled=True),
        lax.psum_scatter(self_mats[2], "dp", scatter_dimension=0, tiled=True),
        lax.psum_scatter(self_mats[3], "dp", scatter_dimension=1, tiled=True),
        lax.psum_scatter(cross_mats[0], "dp", scatter_dimension=0, tiled=True),
        lax.psum_scatter(cross_mats[1], "dp", scatter_dimension=0, tiled=True),
        lax.psum_scatter(cross_mats[2], "dp", scatter_dimension=0, tiled=True),
        lax.psum_scatter(cross_mats[3], "dp", scatter_dimension=1, tiled=True),
        lax.psum_scatter(decoder_widen_grad, "dp", scatter_dimension=0, tiled=True),
        lax.psum_scatter(decoder_narrow_grad, "dp", scatter_dimension=1, tiled=True),
    )
    encoder_sums = every_sum[:6]
    decoder_sums = every_sum[6:]
    small_sums = lax.psum(
        (
            encoder_gain_grad,
            encoder_later_grad,
            encoder_bias_grad,
            decoder_gain_grad,
            cross_gain_grad,
            decoder_later_grad,
            decoder_bias_grad,
        ),
        ("dp", "mp"),
    )
    return (
        encoder_final.astype(jnp.bfloat16),
        encoder_input_grad,
        table_grad,
        small_sums[2],
        small_sums[0],
        encoder_sums[0],
        encoder_sums[1],
        encoder_sums[2],
        encoder_sums[3],
        small_sums[1],
        encoder_sums[4],
        encoder_sums[5],
        decoder_final.astype(jnp.bfloat16),
        decoder_input_grad,
        states_grad,
        small_sums[6],
        small_sums[3],
        decoder_sums[0],
        decoder_sums[1],
        decoder_sums[2],
        decoder_sums[3],
        small_sums[4],
        decoder_sums[4],
        decoder_sums[5],
        decoder_sums[6],
        decoder_sums[7],
        small_sums[5],
        decoder_sums[8],
        decoder_sums[9],
    )


def solution(mesh):
    in_specs = (
        P(("dp", "mp"), None),
        P(("dp", "mp"), None),
        P("dp", None),
        P(),
        P(),
        P(),
        P(),
        P(None, "mp"),
        P(None, "mp"),
        P(None, "mp"),
        P("mp", None),
        P(),
        P(None, "mp"),
        P("mp", None),
        P(("dp", "mp"), None),
        P(("dp", "mp"), None),
        P(("dp", "mp"), None),
        P(),
        P(),
        P(),
        P(None, "mp"),
        P(None, "mp"),
        P(None, "mp"),
        P("mp", None),
        P(),
        P(None, "mp"),
        P(None, "mp"),
        P(None, "mp"),
        P("mp", None),
        P(),
        P(None, "mp"),
        P("mp", None),
    )
    out_specs = (
        P(("dp", "mp"), None),
        P(("dp", "mp"), None),
        P(("dp", "mp"), None, None),
        P(),
        P(),
        P("dp", "mp"),
        P("dp", "mp"),
        P("dp", "mp"),
        P("mp", "dp"),
        P(),
        P("dp", "mp"),
        P("mp", "dp"),
        P(("dp", "mp"), None),
        P(("dp", "mp"), None),
        P(("dp", "mp"), None),
        P(),
        P(),
        P("dp", "mp"),
        P("dp", "mp"),
        P("dp", "mp"),
        P("mp", "dp"),
        P(),
        P("dp", "mp"),
        P("dp", "mp"),
        P("dp", "mp"),
        P("mp", "dp"),
        P(),
        P("dp", "mp"),
        P("mp", "dp"),
    )
    return jax.shard_map(shards, mesh=mesh, in_specs=in_specs, out_specs=out_specs, check_vma=False)
```

profile of v0, /device:TPU:0, one launch (start us, length us, event | category | flops | bytes accessed | tf_op | source)
XLA Modules:
  0.0 1350.0 jit_solution(12668517473321497400)
XLA Ops:
  12.8 21.3 %all_gather.37 = bf16[512,768]{1,0:T(8,128)(2,1)S(1)} all-gather(bf16[128,768]{1,0:T(8,128)(2,1)S(1)} %fusion.46), channel_id=1, replica_groups=mesh['dp'=8,'mp'=4] {'mp'}, dimensions={0}, use_global_device_ids=true | all-gather | bytes 983040 | tf_op jit(solution)/shard_map/all_gather | solution.py:52
  43.9 27.8 %all_gather.33 = bf16[512,768]{1,0:T(8,128)(2,1)S(1)} all-gather(bf16[128,768]{1,0:T(8,128)(2,1)S(1)} %fusion.47), channel_id=1, replica_groups=mesh['dp'=8,'mp'=4] {'mp'}, dimensions={0}, use_global_device_ids=true | all-gather | bytes 983040 | tf_op jit(solution)/shard_map/all_gather | solution.py:52
  80.6 4.2 copy.414
  84.8 4.0 gather_fusion
  103.8 2.6 fusion.130
  106.4 25.8 %all_gather.38 = bf16[512,768]{1,0:T(8,128)(2,1)S(1)} all-gather(bf16[128,768]{1,0:T(8,128)(2,1)} %param.48), channel_id=1, replica_groups=mesh['dp'=8,'mp'=4] {'mp'}, dimensions={0}, use_global_device_ids=true | all-gather | bytes 983040 | tf_op jit(solution)/shard_map/all_gather | solution.py:52
  145.0 17.4 %all_gather.39 = bf16[512,768]{1,0:T(8,128)(2,1)S(1)} all-gather(bf16[128,768]{1,0:T(8,128)(2,1)S(1)} %multiply_convert_fusion.6), channel_id=1, replica_groups=mesh['dp'=8,'mp'=4] {'mp'}, dimensions={0}, use_global_device_ids=true | all-gather | bytes 983040 | tf_op jit(solution)/shard_map/all_gather | solution.py:52
  171.7 2.6 fusion.140
  174.5 27.6 %all_gather.35 = bf16[512,768]{1,0:T(8,128)(2,1)S(1)} all-gather(bf16[128,768]{1,0:T(8,128)(2,1)} %param.33), channel_id=1, replica_groups=mesh['dp'=8,'mp'=4] {'mp'}, dimensions={0}, use_global_device_ids=true | all-gather | bytes 983040 | tf_op jit(solution)/shard_map/all_gather | solution.py:60
  202.0 26.9 %all_gather.41 = bf16[512,768]{1,0:T(8,128)(2,1)S(1)} all-gather(bf16[128,768]{1,0:T(8,128)(2,1)} %param.47), channel_id=1, replica_groups=mesh['dp'=8,'mp'=4] {'mp'}, dimensions={0}, use_global_device_ids=true | all-gather | bytes 983040 | tf_op jit(solution)/shard_map/all_gather | solution.py:60
  235.8 17.3 %all_gather.34 = bf16[512,768]{1,0:T(8,128)(2,1)S(1)} all-gather(bf16[128,768]{1,0:T(8,128)(2,1)S(1)} %multiply_convert_fusion.7), channel_id=1, replica_groups=mesh['dp'=8,'mp'=4] {'mp'}, dimensions={0}, use_global_device_ids=true | all-gather | bytes 983040 | tf_op jit(solution)/shard_map/all_gather | solution.py:52
  253.2 2.6 fusion.8
  260.1 23.6 %all_gather.40 = bf16[512,768]{1,0:T(8,128)(2,1)S(1)} all-gather(bf16[128,768]{1,0:T(8,128)(2,1)S(1)} %multiply_convert_fusion.5), channel_id=1, replica_groups=mesh['dp'=8,'mp'=4] {'mp'}, dimensions={0}, use_global_device_ids=true | all-gather | bytes 983040 | tf_op jit(solution)/shard_map/all_gather | solution.py:52
  283.7 2.6 fusion.15
  289.0 4.0 fusion.124
  297.8 24.2 %all_gather.36 = bf16[512,768]{1,0:T(8,128)(2,1)S(1)} all-gather(bf16[128,768]{1,0:T(8,128)(2,1)S(1)} %fusion.120), channel_id=1, replica_groups=mesh['dp'=8,'mp'=4] {'mp'}, dimensions={0}, use_global_device_ids=true | all-gather | bytes 983040 | tf_op jit(solution)/shard_map/all_gather | solution.py:60
  326.6 29.8 %reduce-scatter.60.cloned.1.call-done = f32[128,768]{1,0:T(8,128)} async-done(((f32[512,768]{1,0:T(8,128)}), f32[128,768]{1,0:T(8,128)}) %reduce-scatter.60.cloned.1.call-update) | async-done | bytes 393232 | tf_op jit(solution)/shard_map/reduce_scatter | solution.py:56
  358.4 18.3 %all_gather.42 = bf16[512,768]{1,0:T(8,128)(2,1)S(1)} all-gather(bf16[128,768]{1,0:T(8,128)(2,1)S(1)} %get-tuple-element.260), channel_id=1, replica_groups=mesh['dp'=8,'mp'=4] {'mp'}, dimensions={0}, use_global_device_ids=true | all-gather | bytes 983040 | tf_op jit(solution)/shard_map/all_gather | solution.py:60
  386.7 2.4 convolution_convert_fusion.2
  406.2 2.4 fusion.63
  416.5 2.7 convolution_bitcast_fusion.2
  422.7 4.1 fusion.122
  440.5 4.9 scatter_custom_fusion
  445.5 8.3 reshape.381
  455.2 2.6 convolution_bitcast_fusion
  472.2 19.8 %all_gather.43 = bf16[512,768]{1,0:T(8,128)(2,1)S(1)} all-gather(bf16[128,768]{1,0:T(8,128)(2,1)S(1)} %get-tuple-element.251), channel_id=1, replica_groups=mesh['dp'=8,'mp'=4] {'mp'}, dimensions={0}, use_global_device_ids=true | all-gather | bytes 983040 | tf_op jit(solution)/shard_map/all_gather | solution.py:60
  524.0 2.3 convolution_add_fusion.3
  526.4 3.3 fusion.138
  530.9 3.8 fusion.121
  539.5 3.9 fusion.123
  559.3 120.1 %all-reduce.5.cloned.1.call-done = f32[1024,2,768]{2,1,0:T(2,128)} async-done(((f32[1024,2,768]{2,1,0:T(2,128)}), f32[1024,2,768]{2,1,0:T(2,128)}) %all-reduce.5.cloned.1.call-update) | async-done | bytes 6291472
  681.0 36.4 %reduce-scatter.90.cloned.1.call-done = f32[96,192]{1,0:T(8,128)} async-done(((f32[768,192]{1,0:T(8,128)}), f32[96,192]{1,0:T(8,128)}) %reduce-scatter.90.cloned.1.call-update) | async-done | bytes 73744
  719.9 23.3 %reduce-scatter.68.cloned.1.call-done = bf16[128,768]{1,0:T(8,128)(2,1)} async-done(((bf16[512,768]{1,0:T(8,128)(2,1)}), bf16[128,768]{1,0:T(8,128)(2,1)}) %reduce-scatter.68.cloned.1.call-update) | async-done | bytes 196624 | tf_op jit(solution)/shard_map/reduce_scatter | solution.py:64
  744.9 35.9 %reduce-scatter.84.cloned.1.call-done = f32[96,192]{1,0:T(8,128)} async-done(((f32[768,192]{1,0:T(8,128)}), f32[96,192]{1,0:T(8,128)}) %reduce-scatter.84.cloned.1.call-update) | async-done | bytes 73744
  782.4 24.0 %reduce-scatter.66.cloned.1.call-done = bf16[128,768]{1,0:T(8,128)(2,1)} async-done(((bf16[512,768]{1,0:T(8,128)(2,1)}), bf16[128,768]{1,0:T(8,128)(2,1)}) %reduce-scatter.66.cloned.1.call-update) | async-done | bytes 196624 | tf_op jit(solution)/shard_map/reduce_scatter | solution.py:64
  807.6 39.8 %all-reduce.2 = (f32[32,12]{0,1:T(8,128)}, f32[768]{0:T(1024)}, f32[768]{0:T(1024)}, f32[32,12]{0,1:T(8,128)}, f32[768]{0:T(1024)}, /*index=5*/f32[768]{0:T(1024)}, f32[768]{0:T(1024)}) all-reduce(f32[32,12]{0,1:T(8,128)S(1)} %dynamic_update_slice.6, f32[768]{0:T(1024)S(1)} %get-tuple-element.240, ...), channel_id=1, replica_groups=mesh['dp'=8,'mp'=4] {'dp','mp'}, use_global_device_ids=true, to_apply=%region_14.15 | all-reduce | flops 4608 | bytes 36864 | tf_op jit(solution)/shard_map/psum | solution.py:404
  849.2 34.4 %reduce-scatter.46.cloned.1.call-done = f32[96,192]{1,0:T(8,128)} async-done(((f32[768,192]{1,0:T(8,128)}), f32[96,192]{1,0:T(8,128)}) %reduce-scatter.46.cloned.1.call-update) | async-done | bytes 73744 | tf_op jit(solution)/shard_map/reduce_scatter | solution.py:385
  883.6 38.9 %reduce-scatter.48.cloned.1.call-done = f32[96,192]{1,0:T(8,128)} async-done(((f32[768,192]{1,0:T(8,128)}), f32[96,192]{1,0:T(8,128)}) %reduce-scatter.48.cloned.1.call-update) | async-done | bytes 73744 | tf_op jit(solution)/shard_map/reduce_scatter | solution.py:386
  922.5 46.8 %reduce-scatter.52.cloned.1.call-done = f32[96,768]{1,0:T(8,128)} async-done(((f32[768,768]{1,0:T(8,128)}), f32[96,768]{1,0:T(8,128)}) %reduce-scatter.52.cloned.1.call-update) | async-done | bytes 294928 | tf_op jit(solution)/shard_map/reduce_scatter | solution.py:389
  969.4 46.3 %reduce-scatter.54.cloned.1.call-done = f32[768,96]{0,1:T(8,128)} async-done(((f32[768,768]{0,1:T(8,128)}), f32[768,96]{0,1:T(8,128)}) %reduce-scatter.54.cloned.1.call-update) | async-done | bytes 294928 | tf_op jit(solution)/shard_map/reduce_scatter | solution.py:390
  1015.6 46.8 %reduce-scatter.78.cloned.1.call-done = f32[96,768]{1,0:T(8,128)} async-done(((f32[768,768]{1,0:T(8,128)}), f32[96,768]{1,0:T(8,128)}) %reduce-scatter.78.cloned.1.call-update) | async-done | bytes 294928 | tf_op jit(solution)/shard_map/reduce_scatter | solution.py:399
  1062.5 46.4 %reduce-scatter.80.cloned.1.call-done = f32[768,96]{0,1:T(8,128)} async-done(((f32[768,768]{0,1:T(8,128)}), f32[768,96]{0,1:T(8,128)}) %reduce-scatter.80.cloned.1.call-update) | async-done | bytes 294928 | tf_op jit(solution)/shard_map/reduce_scatter | solution.py:400
  1108.9 39.0 %reduce-scatter.76.cloned.1.call-done = f32[96,192]{1,0:T(8,128)} async-done(((f32[768,192]{1,0:T(8,128)}), f32[96,192]{1,0:T(8,128)}) %reduce-scatter.76.cloned.1.call-update) | async-done | bytes 73744 | tf_op jit(solution)/shard_map/reduce_scatter | solution.py:395
  1148.0 38.9 %reduce-scatter.88.cloned.1.call-done = f32[96,192]{1,0:T(8,128)} async-done(((f32[768,192]{1,0:T(8,128)}), f32[96,192]{1,0:T(8,128)}) %reduce-scatter.88.cloned.1.call-update) | async-done | bytes 73744
  1186.9 39.0 %reduce-scatter.86.cloned.1.call-done = f32[96,192]{1,0:T(8,128)} async-done(((f32[768,192]{1,0:T(8,128)}), f32[96,192]{1,0:T(8,128)}) %reduce-scatter.86.cloned.1.call-update) | async-done | bytes 73744
  1225.9 38.9 %reduce-scatter.72.cloned.1.call-done = f32[96,192]{1,0:T(8,128)} async-done(((f32[768,192]{1,0:T(8,128)}), f32[96,192]{1,0:T(8,128)}) %reduce-scatter.72.cloned.1.call-update) | async-done | bytes 73744 | tf_op jit(solution)/shard_map/reduce_scatter | solution.py:392
  1264.8 38.9 %reduce-scatter.74.cloned.1.call-done = f32[96,192]{1,0:T(8,128)} async-done(((f32[768,192]{1,0:T(8,128)}), f32[96,192]{1,0:T(8,128)}) %reduce-scatter.74.cloned.1.call-update) | async-done | bytes 73744 | tf_op jit(solution)/shard_map/reduce_scatter | solution.py:393
  1303.7 39.0 %reduce-scatter.70.cloned.1.call-done = f32[96,192]{1,0:T(8,128)} async-done(((f32[768,192]{1,0:T(8,128)}), f32[96,192]{1,0:T(8,128)}) %reduce-scatter.70.cloned.1.call-update) | async-done | bytes 73744 | tf_op jit(solution)/shard_map/reduce_scatter | solution.py:391
  (547 shorter events, 217.0 us)
Async XLA Ops:
  7.2 246.0 %copy-start = (bf16[768,768]{1,0:T(8,128)(2,1)S(1)}, bf16[768,768]{1,0:T(8,128)(2,1)}, u32[]{:S(2)}) copy-start(bf16[768,768]{1,0:T(8,128)(2,1)} %param.44) | copy-start | bytes 3538948
  7.2 135.0 %reduce-scatter.56.cloned.1.call-start = ((), (), s32[]{:S(2)}) async-start(), calls=%async_computation.36 | async-start | bytes 1966080 | tf_op jit(solution)/shard_map/reduce_scatter | solution.py:56
  41.0 30.7 %copy-start.41 = (bf16[768,192]{0,1:T(8,128)(2,1)S(1)}, bf16[768,192]{0,1:T(8,128)(2,1)}, u32[]{:S(2)}) copy-start(bf16[768,192]{0,1:T(8,128)(2,1)} %param.40) | copy-start | bytes 884740
  41.0 192.0 %reduce-scatter.38.cloned.1.call-start = ((), (), s32[]{:S(2)}) async-start(), calls=%async_computation.27 | async-start | bytes 1966080 | tf_op jit(solution)/shard_map/reduce_scatter | solution.py:56
  41.2 30.5 %copy-start.123 = (f32[128]{0:T(128)}, f32[128]{0:T(128)S(1)}, u32[]{:S(2)}) copy-start(f32[128]{0:T(128)S(1)} %fusion.109) | copy-start | bytes 1540
  42.7 29.0 %copy-start.130 = (pred[80]{0:T(512)(128)(4,1)}, pred[80]{0:T(512)(128)(4,1)S(1)}, u32[]{:S(2)}) copy-start(pred[80]{0:T(512)(128)(4,1)S(1)} %compare_and_fusion) | copy-start | bytes 244
  106.4 152.1 %reduce-scatter.58.cloned.1.call-start = ((), (), s32[]{:S(2)}) async-start(), calls=%async_computation.37 | async-start | bytes 1966080 | tf_op jit(solution)/shard_map/reduce_scatter | solution.py:56
  174.4 119.9 %reduce-scatter.42.cloned.1.call-start = ((), (), s32[]{:S(2)}) async-start(), calls=%async_computation.29 | async-start | bytes 983040 | tf_op jit(solution)/shard_map/reduce_scatter | solution.py:64
  174.5 54.5 %copy-start.142 = (bf16[768,768]{1,0:T(8,128)(2,1)S(1)}, bf16[768,768]{1,0:T(8,128)(2,1)}, u32[]{:S(2)}) copy-start(bf16[768,768]{1,0:T(8,128)(2,1)} %param.63) | copy-start | bytes 3538948
  202.0 28.9 %copy-start.80 = (bf16[512,768]{1,0:T(8,128)(2,1)}, bf16[512,768]{1,0:T(8,128)(2,1)S(1)}, u32[]{:S(2)}) copy-start(bf16[512,768]{1,0:T(8,128)(2,1)S(1)} %all_gather.35) | copy-start | bytes 2359300
  258.4 65.9 %reduce-scatter.62.cloned.1.call-start = ((), (), s32[]{:S(2)}) async-start(), calls=%async_computation.39 | async-start | bytes 983040 | tf_op jit(solution)/shard_map/reduce_scatter | solution.py:64
  259.9 96.5 %copy-start.12 = (f32[128,768]{1,0:T(8,128)}, f32[128,768]{1,0:T(8,128)S(1)}, u32[]{:S(2)}) copy-start(f32[128,768]{1,0:T(8,128)S(1)} %get-tuple-element.254) | copy-start | bytes 1179652
  288.9 67.6 %reduce-scatter.60.cloned.1.call-start = ((), (), s32[]{:S(2)}) async-start(), calls=%async_computation.38 | async-start | bytes 1966080 | tf_op jit(solution)/shard_map/reduce_scatter | solution.py:56
  293.0 174.6 %reduce-scatter.64.cloned.1.call-start = ((), (), s32[]{:S(2)}) async-start(), calls=%async_computation.40 | async-start | bytes 983040 | tf_op jit(solution)/shard_map/reduce_scatter | solution.py:64
  297.7 58.7 %copy-start.53 = (bf16[128,768]{1,0:T(8,128)(2,1)S(1)}, bf16[128,768]{1,0:T(8,128)(2,1)}, u32[]{:S(2)}) copy-start(bf16[128,768]{1,0:T(8,128)(2,1)} %param.47) | copy-start | bytes 589828
  326.6 29.8 %copy-start.129 = (f32[128]{0:T(128)}, f32[128]{0:T(128)S(1)}, u32[]{:S(2)}) copy-start(f32[128]{0:T(128)S(1)} %multiply_multiply_fusion.6) | copy-start | bytes 1540
  389.1 162.2 %reduce-scatter.82.cloned.1.call-start = ((), (), s32[]{:S(2)}) async-start(), calls=%async_computation.49 | async-start | bytes 884736
  419.2 135.3 %reduce-scatter.44.cloned.1.call-start = ((), (), s32[]{:S(2)}) async-start(), calls=%async_computation.30 | async-start | bytes 983040 | tf_op jit(solution)/shard_map/reduce_scatter | solution.py:64
  422.6 133.0 %reduce-scatter.40.cloned.1.call-start = ((), (), s32[]{:S(2)}) async-start(), calls=%async_computation.28 | async-start | bytes 1966080 | tf_op jit(solution)/shard_map/reduce_scatter | solution.py:56
  426.8 252.6 %all-reduce.5.cloned.1.call-start = ((), (), s32[]{:S(2)}) async-start(), calls=%async_computation.54 | async-start | bytes 12582912
  453.8 263.7 %reduce-scatter.90.cloned.1.call-start = ((), (), s32[]{:S(2)}) async-start(), calls=%async_computation.53 | async-start | bytes 884736
  457.8 285.4 %reduce-scatter.68.cloned.1.call-start = ((), (), s32[]{:S(2)}) async-start(), calls=%async_computation.42 | async-start | bytes 983040 | tf_op jit(solution)/shard_map/reduce_scatter | solution.py:64
  467.5 313.3 %reduce-scatter.84.cloned.1.call-start = ((), (), s32[]{:S(2)}) async-start(), calls=%async_computation.50 | async-start | bytes 884736
  513.0 293.4 %reduce-scatter.66.cloned.1.call-start = ((), (), s32[]{:S(2)}) async-start(), calls=%async_computation.41 | async-start | bytes 983040 | tf_op jit(solution)/shard_map/reduce_scatter | solution.py:64
  516.4 332.8 %reduce-scatter.50.cloned.1.call-start = ((), (), s32[]{:S(2)}) async-start(), calls=%async_computation.33 | async-start | bytes 884736 | tf_op jit(solution)/shard_map/reduce_scatter | solution.py:387
  521.2 362.5 %reduce-scatter.46.cloned.1.call-start = ((), (), s32[]{:S(2)}) async-start(), calls=%async_computation.31 | async-start | bytes 884736 | tf_op jit(solution)/shard_map/reduce_scatter | solution.py:385
  523.6 399.0 %reduce-scatter.48.cloned.1.call-start = ((), (), s32[]{:S(2)}) async-start(), calls=%async_computation.32 | async-start | bytes 884736 | tf_op jit(solution)/shard_map/reduce_scatter | solution.py:386
  526.3 443.0 %reduce-scatter.52.cloned.1.call-start = ((), (), s32[]{:S(2)}) async-start(), calls=%async_computation.34 | async-start | bytes 2654208 | tf_op jit(solution)/shard_map/reduce_scatter | solution.py:389
  529.7 485.9 %reduce-scatter.54.cloned.1.call-start = ((), (), s32[]{:S(2)}) async-start(), calls=%async_computation.35 | async-start | bytes 2654208 | tf_op jit(solution)/shard_map/reduce_scatter | solution.py:390
  534.7 527.7 %reduce-scatter.78.cloned.1.call-start = ((), (), s32[]{:S(2)}) async-start(), calls=%async_computation.47 | async-start | bytes 2654208 | tf_op jit(solution)/shard_map/reduce_scatter | solution.py:399
  538.4 570.6 %reduce-scatter.80.cloned.1.call-start = ((), (), s32[]{:S(2)}) async-start(), calls=%async_computation.48 | async-start | bytes 2654208 | tf_op jit(solution)/shard_map/reduce_scatter | solution.py:400
  543.4 604.6 %reduce-scatter.76.cloned.1.call-start = ((), (), s32[]{:S(2)}) async-start(), calls=%async_computation.46 | async-start | bytes 884736 | tf_op jit(solution)/shard_map/reduce_scatter | solution.py:395
  545.9 641.0 %reduce-scatter.88.cloned.1.call-start = ((), (), s32[]{:S(2)}) async-start(), calls=%async_computation.52 | async-start | bytes 884736
  547.5 678.4 %reduce-scatter.86.cloned.1.call-start = ((), (), s32[]{:S(2)}) async-start(), calls=%async_computation.51 | async-start | bytes 884736
  549.1 715.7 %reduce-scatter.72.cloned.1.call-start = ((), (), s32[]{:S(2)}) async-start(), calls=%async_computation.44 | async-start | bytes 884736 | tf_op jit(solution)/shard_map/reduce_scatter | solution.py:392
  550.4 753.2 %reduce-scatter.74.cloned.1.call-start = ((), (), s32[]{:S(2)}) async-start(), calls=%async_computation.45 | async-start | bytes 884736 | tf_op jit(solution)/shard_map/reduce_scatter | solution.py:393
  554.4 788.3 %reduce-scatter.70.cloned.1.call-start = ((), (), s32[]{:S(2)}) async-start(), calls=%async_computation.43 | async-start | bytes 884736 | tf_op jit(solution)/shard_map/reduce_scatter | solution.py:391
  557.9 161.4 %copy-start.86 = (f32[3,64,64]{1,2,0:T(8,128)S(1)}, f32[3,64,64]{1,2,0:T(8,128)}, u32[]{:S(2)}) copy-start(f32[3,64,64]{1,2,0:T(8,128)} %get-tuple-element.249) | copy-start | bytes 147460
  557.9 161.6 %copy-start.112 = (s32[4096]{0:T(1024)S(1)}, s32[4096]{0:T(1024)}, u32[]{:S(2)}) copy-start(s32[4096]{0:T(1024)} %copy-done.111) | copy-start | bytes 49156
  559.2 247.2 %copy-start.28 = (bf16[128,768]{1,0:T(8,128)(2,1)S(1)}, bf16[128,768]{1,0:T(8,128)(2,1)}, u32[]{:S(2)}) copy-start(bf16[128,768]{1,0:T(8,128)(2,1)} %param.46) | copy-start | bytes 589828
  559.2 247.2 %copy-start.106 = (f32[768]{0:T(1024)S(1)}, f32[768]{0:T(1024)}, u32[]{:S(2)}) copy-start(f32[768]{0:T(1024)} %param.51) | copy-start | bytes 9220
  559.2 247.2 %copy-start.122 = (f32[128]{0:T(128)S(1)}, f32[128]{0:T(128)}, u32[]{:S(2)}) copy-start(f32[128]{0:T(128)} %copy-done.121) | copy-start | bytes 1540
  559.2 248.3 %copy-start.108 = (f32[768]{0:T(1024)S(1)}, f32[768]{0:T(1024)}, u32[]{:S(2)}) copy-start(f32[768]{0:T(1024)} %get-tuple-element.236) | copy-start | bytes 9220
  559.2 248.3 %copy-start.109 = (f32[768]{0:T(1024)S(1)}, f32[768]{0:T(1024)}, u32[]{:S(2)}) copy-start(f32[768]{0:T(1024)} %get-tuple-element.232) | copy-start | bytes 9220
  559.2 248.3 %copy-start.110 = (f32[768]{0:T(1024)S(1)}, f32[768]{0:T(1024)}, u32[]{:S(2)}) copy-start(f32[768]{0:T(1024)} %get-tuple-element.234) | copy-start | bytes 9220
  559.3 288.1 %copy-start.136 = (f32[128]{0:T(128)S(1)}, f32[128]{0:T(128)}, u32[]{:S(2)}) copy-start(f32[128]{0:T(128)} %copy-done.135) | copy-start | bytes 1540
  559.3 288.1 %copy-start.64 = (f32[128,768]{1,0:T(8,128)S(1)}, f32[128,768]{1,0:T(8,128)}, u32[]{:S(2)}) copy-start(f32[128,768]{1,0:T(8,128)} %get-tuple-element.252) | copy-start | bytes 1179652
  717.5 625.2 %copy-start.1 = (bf16[768,768]{1,0:T(8,128)(2,1)S(1)}, bf16[768,768]{1,0:T(8,128)(2,1)}, u32[]{:S(2)}) copy-start(bf16[768,768]{1,0:T(8,128)(2,1)} %param.44) | copy-start | bytes 3538948
  (126 other events, 571.3 us)
Sparse Core Ops, SparseCore 0:
  41.1 44.7 reduce-scatter.55
  106.5 44.7 reduce-scatter.37
  174.5 54.8 reduce-scatter.57
  258.6 26.9 reduce-scatter.41
  289.0 30.7 reduce-scatter.61
  322.0 34.4 reduce-scatter.59
  389.2 22.5 reduce-scatter.63
  419.3 34.2 reduce-scatter.81
  456.0 25.8 reduce-scatter.43
  484.0 34.7 reduce-scatter.39
  524.5 154.8 all-reduce.4
  682.7 34.6 reduce-scatter.89
  719.9 23.2 reduce-scatter.67
  746.5 34.2 reduce-scatter.83
  783.0 23.3 reduce-scatter.65
  810.3 34.2 reduce-scatter.49
  848.5 35.0 reduce-scatter.45
  887.5 34.9 reduce-scatter.47
  926.8 42.4 reduce-scatter.51
  973.1 42.4 reduce-scatter.53
  1019.9 42.4 reduce-scatter.77
  1066.4 42.4 reduce-scatter.79
  1113.0 34.9 reduce-scatter.75
  1151.9 34.9 reduce-scatter.87
  1190.9 34.9 reduce-scatter.85
  1229.8 34.9 reduce-scatter.71
  1268.7 34.9 reduce-scatter.73
  1307.7 34.9 reduce-scatter.69
where the time goes:
time: 1360 us; the launch traced here: 1350 us
  waiting for transfers between devices  764 us (56%)
  blocking collectives  290 us (21%)
  local copies, waits for them, and re-layouts  125 us (9%)
  matrix products  116 us (9%)
  other arithmetic  37.2 us (3%)
  between operations  16.7 us (1%)
    unnamed x34, waiting for transfers between devices  271 us
    all_gather x6, blocking collectives, gather_rows(): return lax.all_gather(shard, 'mp', axis=0, tiled=True)  133 us
    all_gather x5, blocking collectives, spread_grad(): lax.all_gather(grad_rows.astype(jnp.bfloat16), 'mp', axis=0, tiled=True)  117 us
    reduce_scatter x6, waiting for transfers between devices, collect_grad(): lax.psum_scatter(partial_rows.astype(jnp.bfloat16), 'mp', scatter_dimensi...  47.4 us
    reduce_scatter x1, waiting for transfers between devices, shards(): lax.psum_scatter(decoder_widen_grad, 'dp', scatter_dimension=0, tiled=True)  46.8 us
    reduce_scatter x1, waiting for transfers between devices, shards(): lax.psum_scatter(encoder_widen_grad, 'dp', scatter_dimension=0, tiled=True)  46.8 us
    reduce_scatter x1, waiting for transfers between devices, shards(): lax.psum_scatter(decoder_narrow_grad, 'dp', scatter_dimension=1, tiled=True)  46.4 us
    reduce_scatter x1, waiting for transfers between devices, shards(): lax.psum_scatter(encoder_narrow_grad, 'dp', scatter_dimension=1, tiled=True)  46.3 us
  transfers between devices with their start and end apart: 28, of which 18 were waited for; matrix products, arithmetic and copies ran while one was open for 18% of the time, Pallas kernels for 0%

commit v1 on v0

v1 whole, which is shorter than its diff:
```python
import functools

import jax
import jax.numpy as jnp
from jax import lax
from jax.experimental import pallas as pl
from jax.experimental.pallas import tpu as pltpu
from jax.sharding import PartitionSpec as P

DH = 64
SEQ = 64
MEMK = 10
PREFIX = 2
EPS = 1e-06
NEG = -1e30
BLOCKS = 8
bf16 = jnp.bfloat16
f32 = jnp.float32
VMEM_LIMIT = 56 * 1024 * 1024


def nn(left, right):
    return lax.dot_general(left, right, (((1,), (0,)), ((), ())), preferred_element_type=f32)


def nt(left, right):
    return lax.dot_general(left, right, (((1,), (1,)), ((), ())), preferred_element_type=f32)


def tn(left, right):
    return lax.dot_general(left, right, (((0,), (0,)), ((), ())), preferred_element_type=f32)


def from_mp(array, step):
    size = lax.axis_size("mp")
    return lax.ppermute(array, "mp", [(i, (i - step) % size) for i in range(size)])


def to_mp(array, step):
    size = lax.axis_size("mp")
    return lax.ppermute(array, "mp", [(i, (i + step) % size) for i in range(size)])


def swap_mp(array, bit):
    return lax.ppermute(array, "mp", [(i, i ^ bit) for i in range(lax.axis_size("mp"))])


def swap_dp(array, bit):
    return lax.ppermute(array, "dp", [(i, i ^ bit) for i in range(lax.axis_size("dp"))])


def high_bits():
    low = lax.axis_size("dp") // BLOCKS
    return low, 2 * low, 4 * low


def gather_weights(block):
    core, along, across = high_bits()
    slots = [block] + [from_mp(block, step) for step in range(1, lax.axis_size("mp"))]
    first = jnp.stack(slots[:2])
    second = jnp.stack(slots[2:])
    first_x = swap_dp(first, along)
    first_y = swap_dp(first, across)
    second_y = swap_dp(second, across)
    second_x = swap_dp(second, along)
    first_xy = swap_dp(first_x, across)
    second_xy = swap_dp(second_y, along)
    own = jnp.stack(
        [
            jnp.concatenate([first, second]),
            jnp.concatenate([first_x, second_x]),
            jnp.concatenate([first_y, second_y]),
            jnp.concatenate([first_xy, second_xy]),
        ]
    )
    return own, swap_dp(own, core)


def rounded_sum(left, right):
    return (left.astype(f32) + right.astype(f32)).astype(bf16)


def reduce_dp(keep, send):
    core, along, across = high_bits()
    half = keep.shape[1] // 2
    got = swap_dp(send, core)

    def pick(places, first):
        part = slice(None, half) if first else slice(half, None)
        return jnp.stack([rounded_sum(keep[j, part], got[j, part]) for j in places])

    first_got = swap_dp(pick((1, 3), True), along)
    second_got = swap_dp(pick((2, 3), False), across)
    first_keep = pick((0, 2), True)
    second_keep = pick((0, 1), False)
    first_last = swap_dp(rounded_sum(first_keep[1], first_got[1]), across)
    second_last = swap_dp(rounded_sum(second_keep[1], second_got[1]), along)
    first_sum = first_keep[0].astype(f32) + first_got[0].astype(f32) + first_last.astype(f32)
    second_sum = second_keep[0].astype(f32) + second_got[0].astype(f32) + second_last.astype(f32)
    return jnp.concatenate([first_sum, second_sum])


def scatter_rest(rows):
    size = lax.axis_size("dp")
    low = size // BLOCKS
    if low == 1:
        return rows
    groups = [[high * low + i for i in range(low)] for high in range(BLOCKS)]
    return lax.psum_scatter(
        rows, "dp", scatter_dimension=0, axis_index_groups=groups, tiled=True
    )


def reduce_attention(keep, send):
    slots = reduce_dp(keep, send)
    total = slots[0]
    for step in range(1, lax.axis_size("mp")):
        total = total + to_mp(slots[step].astype(bf16), step).astype(f32)
    total = scatter_rest(total)
    width = total.shape[1] // 4
    parts = [total[:, i * width : (i + 1) * width] for i in range(4)]
    return parts[0], parts[1], parts[2], parts[3].T


def reduce_ffn(keep, send):
    both = reduce_dp(keep, send)
    return scatter_rest(both[0]), scatter_rest(both[1]).T


def sum_everywhere(array):
    bit = 1
    while bit < lax.axis_size("dp"):
        array = array + swap_dp(array, bit)
        bit *= 2
    bit = 1
    while bit < lax.axis_size("mp"):
        array = array + swap_mp(array, bit)
        bit *= 2
    return array


def fetch_weights(own_ref, rest_ref, held, sems, place):
    copies = []
    for slot in range(4):
        row = []
        for j in range(4):
            for side in range(2):
                source = (own_ref if side == 0 else rest_ref).at[j, slot]
                copy = pltpu.make_async_copy(
                    source, held.at[slot, place ^ (2 * j + side)], sems.at[slot, 2 * j + side]
                )
                copy.start()
                row.append(copy)
        copies.append(row)
    return copies


def slot_weights(copies, held, slot):
    for copy in copies[slot]:
        copy.wait()


def all_rows(held, slot, lanes):
    part = held[slot, :, :, lanes]
    return part.reshape(part.shape[0] * part.shape[1], part.shape[2])


def inverse_rms(rows):
    return lax.rsqrt(jnp.mean(rows * rows, axis=-1, keepdims=True) + EPS)


def column_head(shape):
    return lax.broadcasted_iota(jnp.int32, shape, 1) // DH


def softmax_rows(scores):
    shifted = jnp.exp(scores - jnp.max(scores, axis=-1, keepdims=True))
    return shifted / jnp.sum(shifted, axis=-1, keepdims=True)


def same_sequence(rows):
    row = lax.broadcasted_iota(jnp.int32, (rows, rows), 0)
    col = lax.broadcasted_iota(jnp.int32, (rows, rows), 1)
    return row // SEQ == col // SEQ, col <= row


def score_bias(kind, rel_ref, head, rows, keys):
    same, before = same_sequence(rows)
    if kind == "cross":
        return jnp.where(same, 0.0, NEG)
    wide = jnp.concatenate([rel_ref[head]] * (rows // SEQ), axis=0)
    if kind == "self":
        return jnp.where(jnp.logical_and(same, before), wide, NEG)
    row = lax.broadcasted_iota(jnp.int32, (rows, keys - rows), 0)
    col = lax.broadcasted_iota(jnp.int32, (rows, keys - rows), 1)
    first = (row // SEQ) * (MEMK * PREFIX)
    valid = jnp.logical_and(col >= first, col < first + MEMK * PREFIX)
    return jnp.concatenate([jnp.where(same, wide, NEG), jnp.where(valid, 0.0, NEG)], axis=1)


def attention_forward_kernel(kind, later, *refs):
    if kind == "encoder":
        place, x_ref, pre_ref, gain_ref, later_ref, rel_ref, own, rest = refs[:8]
        refs = refs[8:]
    elif kind == "self":
        place, x_ref, gain_ref, later_ref, rel_ref, own, rest = refs[:7]
        refs = refs[7:]
    else:
        place, x_ref, pre_ref, gain_ref, later_ref, own, rest = refs[:7]
        rel_ref = None
        refs = refs[7:]
    r1_ref, next_ref, a_ref, q_ref, kv_ref, o_ref, held, sems = refs
    copies = fetch_weights(own, rest, held, sems, place[0])
    r = x_ref[...].astype(f32)
    rows = r.shape[0]
    a = (r * inverse_rms(r) * gain_ref[...]).astype(bf16)
    if kind == "encoder":
        a_ref[0:rows, :] = a
        a_ref[rows:, :] = pre_ref[...]
        a_all = a_ref[...]
    else:
        a_ref[...] = a
        a_all = a
    acc = r
    for slot in range(4):
        slot_weights(copies, held, slot)
        w_in = all_rows(held, slot, slice(0, 576))
        if kind == "cross":
            q = nn(a, w_in[:, :192]).astype(bf16)
            kv = nn(pre_ref[...], w_in[:, 192:]).astype(bf16)
        else:
            qkv = nn(a_all, w_in).astype(bf16)
            q = qkv[:rows, :192]
            kv = qkv[:, 192:]
        q_ref[slot] = q
        kv_ref[slot] = kv
        k = kv[:, :192]
        v = kv[:, 192:]
        head_of = column_head(q.shape)
        o = jnp.zeros(q.shape, f32)
        for j in range(3):
            q_head = jnp.where(head_of == j, q, jnp.zeros_like(q))
            scores = nt(q_head, k) + score_bias(kind, rel_ref, 3 * slot + j, rows, k.shape[0])
            o = jnp.where(head_of == j, nn(softmax_rows(scores).astype(bf16), v), o)
        o = o.astype(bf16)
        o_ref[slot] = o
        acc = acc + nt(o, all_rows(held, slot, slice(576, 768)))
    r1_ref[...] = acc
    next_ref[...] = (acc * inverse_rms(acc) * later_ref[...]).astype(bf16)


def norm_back(dn, r, gain, dgain_ref):
    t = inverse_rms(r)
    dgain_ref[...] = jnp.sum(dn * r * t, axis=0, keepdims=True)
    scaled = dn * gain
    return t * (scaled - r * (t * t) * jnp.mean(scaled * r, axis=-1, keepdims=True))


def store_blocks(keep_ref, send_ref, place, part, value):
    size = value.shape[0] // BLOCKS
    side = place % 2
    for pair in range(BLOCKS // 2):
        where = pair ^ (place // 2)
        even = value[2 * pair * size : (2 * pair + 1) * size]
        odd = value[(2 * pair + 1) * size : (2 * pair + 2) * size]

        @pl.when(side == 0)
        def _():
            keep_ref[where, part] = even
            send_ref[where, part] = odd

        @pl.when(side == 1)
        def _():
            keep_ref[where, part] = odd
            send_ref[where, part] = even


def attention_backward_kernel(kind, after_ffn, *refs):
    refs = list(refs)
    place = refs.pop(0)[0]
    if after_ffn:
        dc_own, dc_rest, up_ref, r1_ref, later_ref = refs[:5]
        refs = refs[5:]
    else:
        up_ref = refs.pop(0)
    x_ref, gain_ref, a_ref = refs[:3]
    refs = refs[3:]
    source_ref = refs.pop(0) if kind == "cross" else None
    q_ref, kv_ref, o_ref, own, rest = refs[:5]
    refs = refs[5:]
    rel_ref, bucket_ref = (refs.pop(0), refs.pop(0)) if kind != "cross" else (None, None)
    dx_ref, dgain_ref, keep_ref, send_ref = refs[:4]
    refs = refs[4:]
    later_grad = refs.pop(0) if after_ffn else None
    if kind == "encoder":
        dpre_ref = refs.pop(0)
    elif kind == "cross":
        dsource_ref = refs.pop(0)
    bias_grad = refs.pop(0) if kind != "cross" else None
    held, sems, total, source_total, weight_grad = refs[:5]
    ds_sum = refs[5] if kind != "cross" else None

    copies = fetch_weights(own, rest, held, sems, place)
    d_out = up_ref[...].astype(f32)
    if after_ffn:
        dn = dc_own[...]
        for i in range(3):
            dn = dn + dc_rest[i].astype(f32)
        d_out = d_out + norm_back(dn, r1_ref[...], later_ref[...], later_grad)
    g = d_out.astype(bf16)
    rows = g.shape[0]
    a = a_ref[...]
    keys = kv_ref.shape[1]
    for slot in range(4):
        slot_weights(copies, held, slot)
        w_in = all_rows(held, slot, slice(0, 576))
        w_out = all_rows(held, slot, slice(576, 768))
        do = nn(g, w_out).astype(bf16)
        q = q_ref[slot]
        kv = kv_ref[slot]
        k = kv[:, :192]
        v = kv[:, 192:]
        head_q = column_head(q.shape)
        head_k = column_head(k.shape)
        dq = jnp.zeros(q.shape, f32)
        dk = jnp.zeros(k.shape, f32)
        dv = jnp.zeros(k.shape, f32)
        for j in range(3):
            q_head = jnp.where(head_q == j, q, jnp.zeros_like(q))
            do_head = jnp.where(head_q == j, do, jnp.zeros_like(do))
            scores = nt(q_head, k) + score_bias(kind, rel_ref, 3 * slot + j, rows, keys)
            p = softmax_rows(scores)
            dv = jnp.where(head_k == j, tn(p.astype(bf16), do), dv)
            dp = nt(do_head, v)
            ds = (p * (dp - jnp.sum(dp * p, axis=-1, keepdims=True))).astype(bf16)
            dq = jnp.where(head_q == j, nn(ds, k), dq)
            dk = jnp.where(head_k == j, tn(ds, q), dk)
            if kind != "cross":
                wide = ds[:, :rows].astype(f32)
                ds_sum[3 * slot + j] = wide[:SEQ] + wide[SEQ:]
        dq = dq.astype(bf16)
        dkv = jnp.concatenate([dk, dv], axis=1).astype(bf16)
        part_total = nt(dq, w_in[:, :192])
        part_source = nt(dkv, w_in[:, 192:])
        if kind == "cross":
            source = source_ref[...]
        else:
            source = a
        if slot == 0:
            total[...] = part_total
            source_total[...] = part_source
        else:
            total[...] += part_total
            source_total[...] += part_source
        weight_grad[:, 0:192] = tn(a[:rows], dq).astype(bf16)
        weight_grad[:, 192:576] = tn(source, dkv).astype(bf16)
        weight_grad[:, 576:768] = tn(g, o_ref[slot]).astype(bf16)
        store_blocks(keep_ref, send_ref, place, slot, weight_grad)
    da = total[...]
    if kind == "cross":
        dsource_ref[...] = source_total[...]
    else:
        da = da + source_total[0:rows]
    if kind == "encoder":
        dpre_ref[...] = source_total[rows:].astype(bf16)
    dx_ref[...] = d_out + norm_back(da, x_ref[...].astype(f32), gain_ref[...], dgain_ref)
    if kind != "cross":
        bucket = bucket_ref[...]
        for b in range(bias_grad.shape[1]):
            chosen = bucket == b
            for head in range(bias_grad.shape[0]):
                bias_grad[head, b : b + 1, :] = jnp.sum(
                    jnp.where(chosen, ds_sum[head], 0.0), axis=0, keepdims=True
                )


def ffn_first_kernel(c0, c1, c2, c3, g0, g1, g2, g3, widen, narrow, c_all, g_all, h_ref, du_ref, dc_own, dc_rest):
    tokens = c0.shape[0]
    for i, (c, g) in enumerate(((c0, g0), (c1, g1), (c2, g2), (c3, g3))):
        c_all[i * tokens : (i + 1) * tokens, :] = c[...]
        g_all[i * tokens : (i + 1) * tokens, :] = g[...]
    inner = 0.7978845608028654
    for n in range(widen.shape[1] // 256):
        at = slice(n * 256, (n + 1) * 256)
        u = nn(c_all[...], widen[:, at])
        u2 = u * u
        th = jnp.tanh(inner * (u + 0.044715 * u * u2))
        h_ref[:, at] = (0.5 * u * (1.0 + th)).astype(bf16)
        slope = 0.5 * (1.0 + th) + (0.5 * inner) * u * (1.0 - th * th) * (1.0 + 3 * 0.044715 * u2)
        dh = nt(g_all[...], narrow[at, :])
        du_ref[:, at] = (dh * slope).astype(bf16)
    for n in range(widen.shape[0] // 256):
        at = slice(n * 256, (n + 1) * 256)
        dc = nt(du_ref[...], widen[at, :])
        dc_own[:, at] = dc[:tokens]
        for i in range(3):
            dc_rest[i, :, at] = dc[(i + 1) * tokens : (i + 2) * tokens].astype(bf16)


def ffn_second_kernel(place, c_all, g_all, h_ref, du_ref, narrow, out_own, out_rest, keep_ref, send_ref, grad):
    tokens = out_own.shape[0]
    for n in range(narrow.shape[1] // 256):
        at = slice(n * 256, (n + 1) * 256)
        out = nn(h_ref[...], narrow[:, at])
        out_own[:, at] = out[:tokens]
        for i in range(3):
            out_rest[i, :, at] = out[(i + 1) * tokens : (i + 2) * tokens].astype(bf16)
    grad[...] = tn(c_all[...], du_ref[...]).astype(bf16)
    store_blocks(keep_ref, send_ref, place[0], 0, grad)
    grad[...] = tn(g_all[...], h_ref[...]).astype(bf16)
    store_blocks(keep_ref, send_ref, place[0], 1, grad)


def call(kernel, name, operands, smem, hbm, outs, scratch, flops):
    specs = []
    for i in range(len(operands)):
        if i in smem:
            specs.append(pl.BlockSpec(memory_space=pltpu.SMEM))
        elif i in hbm:
            specs.append(pl.BlockSpec(memory_space=pl.ANY))
        else:
            specs.append(pl.BlockSpec(memory_space=pltpu.VMEM))
    moved = sum(x.size * x.dtype.itemsize for x in operands)
    return pl.pallas_call(
        kernel,
        out_shape=[jax.ShapeDtypeStruct(shape, kind) for shape, kind in outs],
        in_specs=specs,
        out_specs=[pl.BlockSpec(memory_space=pltpu.VMEM)] * len(outs),
        scratch_shapes=scratch,
        compiler_params=pltpu.CompilerParams(vmem_limit_bytes=VMEM_LIMIT),
        cost_estimate=pl.CostEstimate(flops=flops, bytes_accessed=moved, transcendentals=0),
        name=name,
    )(*operands)


def attention_forward(kind, place, x, extra, gain, later, rel, weights):
    own, rest = weights
    rows, width = x.shape
    extra_rows = extra.shape[0] if kind == "encoder" else 0
    keys = rows + extra_rows
    operands = [place, x]
    if extra is not None:
        operands.append(extra)
    operands += [gain, later]
    if rel is not None:
        operands.append(rel)
    operands += [own, rest]
    count = len(operands)
    return call(
        functools.partial(attention_forward_kernel, kind, True),
        kind + "_forward",
        operands,
        (0,),
        (count - 2, count - 1),
        [
            ((rows, width), f32),
            ((rows, width), bf16),
            ((keys, width), bf16),
            ((4, rows, 192), bf16),
            ((4, keys, 384), bf16),
            ((4, rows, 192), bf16),
        ],
        [pltpu.VMEM((4, BLOCKS, own.shape[2], width), bf16), pltpu.SemaphoreType.DMA((4, 8))],
        8 * rows * width * width,
    )


def attention_backward(kind, place, ffn, upstream, x, gain, stored, source, weights, rel, bucket, buckets):
    own, rest = weights
    rows, width = upstream.shape
    a, q, kv, o = stored
    keys = kv.shape[1]
    operands = [place]
    if ffn is not None:
        dc_own, dc_rest, r1, later = ffn
        operands += [dc_own, dc_rest, upstream, r1, later]
    else:
        operands += [upstream]
    operands += [x, gain, a]
    if source is not None:
        operands.append(source)
    operands += [q, kv, o]
    hbm = (len(operands), len(operands) + 1)
    operands += [own, rest]
    if kind != "cross":
        operands += [rel, bucket]
    block = own.shape[2]
    outs = [
        ((rows, width), f32),
        ((1, width), f32),
        ((4, 4, block, width), bf16),
        ((4, 4, block, width), bf16),
    ]
    if ffn is not None:
        outs.append(((1, width), f32))
    if kind == "encoder":
        outs.append(((keys - rows, width), bf16))
    elif kind == "cross":
        outs.append(((rows, width), f32))
    if kind != "cross":
        outs.append(((rel.shape[0], buckets, 2 * SEQ), f32))
    scratch = [
        pltpu.VMEM((4, BLOCKS, block, width), bf16),
        pltpu.SemaphoreType.DMA((4, 8)),
        pltpu.VMEM((rows, width), f32),
        pltpu.VMEM((keys, width), f32),
        pltpu.VMEM((width, width), bf16),
    ]
    if kind != "cross":
        scratch.append(pltpu.VMEM((rel.shape[0], SEQ, 2 * SEQ), f32))
    return call(
        functools.partial(attention_backward_kernel, kind, ffn is not None),
        kind + "_backward",
        operands,
        (0,),
        hbm,
        outs,
        scratch,
        16 * rows * width * width,
    )


def ffn_both(name, place, c_parts, g_parts, widen, narrow):
    tokens, width = c_parts[0].shape
    hidden = widen.shape[1]
    every = 4 * tokens
    block = width // BLOCKS
    c_all, g_all, h, du, dc_own, dc_rest = call(
        ffn_first_kernel,
        name + "_first",
        [*c_parts, *g_parts, widen, narrow],
        (),
        (),
        [
            ((every, width), bf16),
            ((every, width), bf16),
            ((every, hidden), bf16),
            ((every, hidden), bf16),
            ((tokens, width), f32),
            ((3, tokens, width), bf16),
        ],
        [],
        6 * every * width * hidden,
    )
    out_own, out_rest, keep, send = call(
        ffn_second_kernel,
        name + "_second",
        [place, c_all, g_all, h, du, narrow],
        (0,),
        (),
        [
            ((tokens, width), f32),
            ((3, tokens, width), bf16),
            ((4, 2, block, hidden), bf16),
            ((4, 2, block, hidden), bf16),
        ],
        [pltpu.VMEM((width, hidden), bf16)],
        6 * every * width * hidden,
    )
    return dc_own, dc_rest, out_own, out_rest, keep, send


def gather_tokens(part):
    return [part] + [from_mp(part, step) for step in range(1, 4)]


def return_tokens(rest):
    return jnp.stack([to_mp(rest[step - 1], step) for step in range(1, 4)])


def weight_block(place, query, key, value, merge):
    size = query.shape[0] // BLOCKS
    start = place * size
    parts = [lax.dynamic_slice_in_dim(w, start, size, 0) for w in (query, key, value)]
    parts.append(lax.dynamic_slice_in_dim(merge, start, size, 1).T)
    return jnp.concatenate(parts, axis=1)


def relative_bias(bucket, table, heads_here):
    twice = jnp.concatenate([bucket, bucket], axis=1)
    onehot = (
        lax.broadcasted_iota(jnp.int32, (table.shape[0], 1), 0) == twice.reshape(1, -1)
    ).astype(f32)
    start = lax.axis_index("mp") * heads_here
    columns = jnp.concatenate([table.T, table.T], axis=0)
    ordered = lax.dynamic_slice_in_dim(columns, start, table.shape[1], 0)
    looked = jnp.dot(ordered, onehot, precision=lax.Precision.HIGHEST)
    return looked.reshape(table.shape[1], SEQ, 2 * SEQ), twice


def bias_sums(raw, heads_here):
    by_head = jnp.sum(raw, axis=-1)
    heads = by_head.shape[0]
    start = heads - lax.axis_index("mp") * heads_here
    twice = jnp.concatenate([by_head, by_head], axis=0)
    return lax.dynamic_slice_in_dim(twice, start, heads, 0)


def shards(
    encoder_input,
    encoder_upstream,
    memory_index,
    memory_table,
    encoder_bucket,
    encoder_bias,
    encoder_gain,
    encoder_query,
    encoder_key,
    encoder_value,
    encoder_merge,
    encoder_later_gain,
    encoder_widen,
    encoder_narrow,
    decoder_input,
    decoder_upstream,
    encoder_states,
    decoder_bucket,
    decoder_bias,
    decoder_gain,
    decoder_query,
    decoder_key,
    decoder_value,
    decoder_merge,
    cross_gain,
    cross_query,
    cross_key,
    cross_value,
    cross_merge,
    decoder_later_gain,
    decoder_widen,
    decoder_narrow,
):
    heads_here = encoder_query.shape[1] // DH
    width = encoder_input.shape[1]
    dp_at = lax.axis_index("dp")
    mp_at = lax.axis_index("mp")
    place = dp_at // (lax.axis_size("dp") // BLOCKS)
    place_in = place.reshape(1).astype(jnp.int32)

    def flat(gain):
        return gain.reshape(1, -1)

    encoder_weights = gather_weights(
        weight_block(place, encoder_query, encoder_key, encoder_value, encoder_merge)
    )
    self_weights = gather_weights(
        weight_block(place, decoder_query, decoder_key, decoder_value, decoder_merge)
    )
    cross_weights = gather_weights(
        weight_block(place, cross_query, cross_key, cross_value, cross_merge)
    )
    encoder_g = gather_tokens(encoder_upstream)
    decoder_g = gather_tokens(decoder_upstream)

    own_questions = memory_index.shape[0] // lax.axis_size("mp")
    entries = lax.dynamic_slice_in_dim(
        memory_index, mp_at * own_questions, own_questions, 0
    ).reshape(-1)
    prefix = jnp.take(memory_table, entries, axis=0).reshape(-1, width)
    prefix_rows = prefix.shape[0]
    prefix = jnp.pad(prefix, ((0, -prefix_rows % 64), (0, 0)))

    encoder_rel, encoder_twice = relative_bias(encoder_bucket, encoder_bias, heads_here)
    decoder_rel, decoder_twice = relative_bias(decoder_bucket, decoder_bias, heads_here)

    encoder_r1, encoder_c, *encoder_stored = attention_forward(
        "encoder",
        place_in,
        encoder_input,
        prefix,
        flat(encoder_gain),
        flat(encoder_later_gain),
        encoder_rel,
        encoder_weights,
    )
    dc_own, dc_rest, out_own, out_rest, keep, send = ffn_both(
        "encoder_ffn",
        place_in,
        gather_tokens(encoder_c),
        encoder_g,
        encoder_widen,
        encoder_narrow,
    )
    dc_rest = return_tokens(dc_rest)
    out_rest = return_tokens(out_rest)
    encoder_output = (
        encoder_r1 + out_own + jnp.sum(out_rest.astype(f32), axis=0)
    ).astype(bf16)
    encoder_widen_grad, encoder_narrow_grad = reduce_ffn(keep, send)
    (
        encoder_input_grad,
        encoder_gain_grad,
        keep,
        send,
        encoder_later_grad,
        prefix_grad,
        encoder_bias_raw,
    ) = attention_backward(
        "encoder",
        place_in,
        (dc_own, dc_rest, encoder_r1, flat(encoder_later_gain)),
        encoder_upstream,
        encoder_input,
        flat(encoder_gain),
        encoder_stored,
        None,
        encoder_weights,
        encoder_rel,
        encoder_twice,
        encoder_bias.shape[0],
    )
    encoder_mats = reduce_attention(keep, send)

    entry_rows = jnp.repeat(entries, PREFIX)
    numbers = jnp.stack([entry_rows // 32, entry_rows % 32], axis=1).astype(bf16)
    numbers = jnp.pad(numbers, ((0, 0), (0, 126)))
    packed = jnp.concatenate([prefix_grad[:prefix_rows], numbers], axis=1)
    used = lax.all_gather(packed, ("dp", "mp"), axis=0, tiled=True)
    used_entry = used[:, width].astype(jnp.int32) * 32 + used[:, width + 1].astype(jnp.int32)
    used_row = used_entry * PREFIX + jnp.arange(used.shape[0]) % PREFIX
    devices = lax.axis_size("dp") * lax.axis_size("mp")
    table_rows = memory_table.shape[0] * PREFIX // devices
    first_row = (dp_at * lax.axis_size("mp") + mp_at) * table_rows
    onehot = (
        first_row + lax.broadcasted_iota(jnp.int32, (table_rows, 1), 0) == used_row[None, :]
    ).astype(bf16)
    table_grad = nn(onehot, used[:, :width]).reshape(-1, PREFIX, width)

    self_r1, _, *self_stored = attention_forward(
        "self",
        place_in,
        decoder_input,
        None,
        flat(decoder_gain),
        flat(cross_gain),
        decoder_rel,
        self_weights,
    )
    cross_r2, decoder_c, *cross_stored = attention_forward(
        "cross",
        place_in,
        self_r1,
        encoder_states,
        flat(cross_gain),
        flat(decoder_later_gain),
        None,
        cross_weights,
    )
    dc_own, dc_rest, out_own, out_rest, keep, send = ffn_both(
        "decoder_ffn",
        place_in,
        gather_tokens(decoder_c),
        decoder_g,
        decoder_widen,
        decoder_narrow,
    )
    dc_rest = return_tokens(dc_rest)
    out_rest = return_tokens(out_rest)
    decoder_output = (cross_r2 + out_own + jnp.sum(out_rest.astype(f32), axis=0)).astype(bf16)
    decoder_widen_grad, decoder_narrow_grad = reduce_ffn(keep, send)
    cross_dx, cross_gain_grad, keep, send, decoder_later_grad, states_grad = attention_backward(
        "cross",
        place_in,
        (dc_own, dc_rest, cross_r2, flat(decoder_later_gain)),
        decoder_upstream,
        self_r1,
        flat(cross_gain),
        cross_stored,
        encoder_states,
        cross_weights,
        None,
        None,
        None,
    )
    cross_mats = reduce_attention(keep, send)
    decoder_input_grad, decoder_gain_grad, keep, send, decoder_bias_raw = attention_backward(
        "self",
        place_in,
        None,
        cross_dx,
        decoder_input,
        flat(decoder_gain),
        self_stored,
        None,
        self_weights,
        decoder_rel,
        decoder_twice,
        decoder_bias.shape[0],
    )
    self_mats = reduce_attention(keep, send)

    gains = [
        encoder_gain_grad,
        encoder_later_grad,
        decoder_gain_grad,
        cross_gain_grad,
        decoder_later_grad,
    ]
    tables = [bias_sums(encoder_bias_raw, heads_here), bias_sums(decoder_bias_raw, heads_here)]
    small = jnp.concatenate([x.reshape(-1) for x in gains + tables]).reshape(-1, 128)
    small = sum_everywhere(small).reshape(-1)
    gain_sums = [small[i * width : (i + 1) * width] for i in range(5)]
    heads, buckets = tables[0].shape
    table_at = 5 * width
    bias_grads = [
        small[table_at + i * heads * buckets : table_at + (i + 1) * heads * buckets]
        .reshape(heads, buckets)
        .T
        for i in range(2)
    ]
    return (
        encoder_output,
        encoder_input_grad,
        table_grad,
        bias_grads[0],
        gain_sums[0],
        *encoder_mats,
        gain_sums[1],
        encoder_widen_grad,
        encoder_narrow_grad,
        decoder_output,
        decoder_input_grad,
        states_grad,
        bias_grads[1],
        gain_sums[2],
        *self_mats,
        gain_sums[3],
        *cross_mats,
        gain_sums[4],
        decoder_widen_grad,
        decoder_narrow_grad,
    )


def solution(mesh):
    rows = P(("dp", "mp"), None)
    columns = P(None, "mp")
    lines = P("mp", None)
    attention = (columns, columns, columns, lines)
    in_specs = (
        (rows, rows, P("dp", None), P(), P(), P(), P())
        + attention
        + (P(), columns, lines, rows, rows, rows, P(), P(), P())
        + attention
        + (P(),)
        + attention
        + (P(), columns, lines)
    )
    both = P("dp", "mp")
    turned = P("mp", "dp")
    grads = (both, both, both, turned)
    out_specs = (
        (rows, rows, P(("dp", "mp"), None, None), P(), P())
        + grads
        + (P(), both, turned, rows, rows, rows, P(), P())
        + grads
        + (P(),)
        + grads
        + (P(), both, turned)
    )
    return jax.shard_map(shards, mesh=mesh, in_specs=in_specs, out_specs=out_specs, check_vma=False)
```

time: 1360 us -> 461 us (0.34)
  waiting for transfers between devices: 764 us -> 115 us
  blocking collectives: 290 us -> 0 us
  starting transfers between devices: 1.63 us -> 130 us
  matrix products: 116 us -> 2.97 us
  Pallas kernels: 0 us -> 99.9 us
  local copies, waits for them, and re-layouts: 125 us -> 37.8 us
  other arithmetic: 37.2 us -> 52.3 us
    reduce_scatter x22 -> x0, waiting for transfers between devices: 493 us -> none  [the longest x6 47.4 us: collect_grad(): lax.psum_scatter(partial_rows.astype(jnp.bfloat16), 'mp', scatter_dimensi...]
    unnamed x34 -> x1, waiting for transfers between devices: 271 us -> 0.02 us
    all_gather x11 -> x0, blocking collectives: 250 us -> none  [the longest x6 133 us: gather_rows(): return lax.all_gather(shard, 'mp', axis=0, tiled=True)]
    ppermute x0 -> x93, starting transfers between devices: none -> 130 us  [the longest x49 44.7 us: swap_dp(): lax.ppermute(array, 'dp', [(i, i ^ bit) for i in range(lax.axis_size('dp'...]
    ppermute x0 -> x93, waiting for transfers between devices: none -> 115 us  [the longest x49 78 us: swap_dp(): lax.ppermute(array, 'dp', [(i, i ^ bit) for i in range(lax.axis_size('dp'...]
    dot_general x73 -> x3, matrix products: 109 us -> 2.97 us  [the longest x1 2.06 us: nn(): lax.dot_general(left, right, (((1,), (0,)), ((), ())), preferred_element_...]
    pallas_call x0 -> x10, Pallas kernels: none -> 99.9 us  [call(): pl.pallas_call(kernel, out_shape=[jax.ShapeDtypeStruct(shape, kind) for s...]
    psum x1 -> x0, blocking collectives: 39.8 us -> none  [shards(): lax.psum((encoder_gain_grad, encoder_later_grad, encoder_bias_grad, decod...]
  transfers between devices with their start and end apart: 28 -> 94, of which waited for: 18 -> 31; matrix products, arithmetic and copies ran while one was open for 18% -> 18% of each run, Pallas kernels for 0% -> 22%
where the time goes in v1:
time: 461 us; the launch traced here: 453 us
  starting transfers between devices  130 us (28%)
  waiting for transfers between devices  115 us (25%)
  Pallas kernels  99.9 us (22%)
  other arithmetic  52.3 us (11%)
  local copies, waits for them, and re-layouts  37.8 us (8%)
  between operations  15.8 us (3%)
    pallas_call x10, Pallas kernels, call(): pl.pallas_call(kernel, out_shape=[jax.ShapeDtypeStruct(shape, kind) for s...  99.9 us
    ppermute x49, waiting for transfers between devices, swap_dp(): lax.ppermute(array, 'dp', [(i, i ^ bit) for i in range(lax.axis_size('dp'...  78 us
    ppermute x49, starting transfers between devices, swap_dp(): lax.ppermute(array, 'dp', [(i, i ^ bit) for i in range(lax.axis_size('dp'...  44.7 us
    ppermute x21, starting transfers between devices, from_mp(): lax.ppermute(array, 'mp', [(i, (i - step) % size) for i in range(size)])  41.5 us
    ppermute x21, starting transfers between devices, to_mp(): lax.ppermute(array, 'mp', [(i, (i + step) % size) for i in range(size)])  37.4 us
    ppermute x21, waiting for transfers between devices, to_mp(): lax.ppermute(array, 'mp', [(i, (i + step) % size) for i in range(size)])  17.2 us
    ppermute x21, waiting for transfers between devices, from_mp(): lax.ppermute(array, 'mp', [(i, (i - step) % size) for i in range(size)])  15.1 us
    convert_element_type x10, other arithmetic, rounded_sum(): return (left.astype(f32) + right.astype(f32)).astype(bf16)  12.7 us
  transfers between devices with their start and end apart: 94, of which 31 were waited for; matrix products, arithmetic and copies ran while one was open for 18% of the time, Pallas kernels for 22%

profile of v1, /device:TPU:0, one launch (start us, length us, event | category | flops | bytes accessed | tf_op | source)
XLA Modules:
  0.0 453.3 jit_solution(8810474447656165573)
XLA Ops:
  11.8 4.0 collective-permute-start.23
  17.4 2.2 collective-permute-start.22
  35.8 3.3 collective-permute-start.32
  42.4 3.9 collective-permute-start
  51.3 2.3 collective-permute-done.1
  59.0 5.5 %collective-permute-done.25 = bf16[2,96,768]{2,1,0:T(8,128)(2,1)S(1)} collective-permute-done((bf16[2,96,768]{2,1,0:T(8,128)(2,1)S(1)}, bf16[2,96,768]{2,1,0:T(8,128)(2,1)S(1)}, u32[]{:S(2)}, u32[]{:S(2)}) %collective-permute-start.25) | collective-permute-done | bytes 294944 | tf_op jit(solution)/shard_map/ppermute | solution.py:49
  68.2 3.2 collective-permute-done.38
  73.6 4.1 collective-permute-done.37
  79.9 4.2 collective-permute-done.6
  84.9 5.5 %collective-permute-done.5 = bf16[2,96,768]{2,1,0:T(8,128)(2,1)S(1)} collective-permute-done((bf16[2,96,768]{2,1,0:T(8,128)(2,1)S(1)}, bf16[2,96,768]{2,1,0:T(8,128)(2,1)S(1)}, u32[]{:S(2)}, u32[]{:S(2)}) %collective-permute-start.5) | collective-permute-done | bytes 294944 | tf_op jit(solution)/shard_map/ppermute | solution.py:49
  93.3 2.7 collective-permute-done.30
  98.5 3.9 collective-permute-done.40
  107.9 2.8 collective-permute-start.45
  119.4 2.1 collective-permute-start.47
  121.5 7.8 %self_forward.1 = (f32[128,768]{1,0:T(8,128)}, bf16[128,768]{1,0:T(8,128)(2,1)}, bf16[128,768]{1,0:T(8,128)(2,1)}, bf16[4,128,192]{2,1,0:T(8,128)(2,1)}, bf16[4,...) custom-call(s32[1]{0:T(128)} %bitcast.refs_0_.place, bf16[128,768]{1,0:T(8,128)(2,1)} %refs_2_.3, ...), custom_call_target="tpu_custom_call" | custom-call | flops 603979776 | bytes 5314564 | tf_op jit(solution)/shard_map/self_forward/pallas_call | solution.py:424
  129.3 7.7 %cross_forward.1 = (f32[128,768]{1,0:T(8,128)}, bf16[128,768]{1,0:T(8,128)(2,1)}, bf16[128,768]{1,0:T(8,128)(2,1)}, bf16[4,128,192]{2,1,0:T(8,128)(2,1)}, bf16[4...) custom-call(s32[1]{0:T(128)} %bitcast.refs_0_.place, f32[128,768]{1,0:T(8,128)} %get-tuple-element.102.refs_1_.refs_6_, ...), custom_call_target="tpu_custom_call" | custom-call | flops 603979776 | bytes 5314564 | tf_op jit(solution)/shard_map/cross_forward/pallas_call | solution.py:424
  142.5 8.9 %encoder_forward.1 = (f32[128,768]{1,0:T(8,128)}, bf16[128,768]{1,0:T(8,128)(2,1)}, bf16[192,768]{1,0:T(8,128)(2,1)}, bf16[4,128,192]{2,1,0:T(8,128)(2,1)}, bf16...) custom-call(s32[1]{0:T(128)} %bitcast.refs_0_.place, bf16[128,768]{1,0:T(8,128)(2,1)} %refs_6_.1, ...), custom_call_target="tpu_custom_call" | custom-call | flops 603979776 | bytes 5412868 | tf_op jit(solution)/shard_map/encoder_forward/pallas_call | solution.py:424
  151.4 3.3 collective-permute-start.13
  156.8 3.0 collective-permute-start.10
  159.8 8.1 %collective-permute-start.11 = (bf16[128,768]{1,0:T(8,128)(2,1)}, bf16[128,768]{1,0:T(8,128)(2,1)S(1)}, u32[]{:S(2)}, u32[]{:S(2)}) collective-permute-start(bf16[128,768]{1,0:T(8,128)(2,1)} %get-tuple-element.85.c0), channel_id=1, source_target_pairs={{0,2},{1,3},{2,0},{3,1},{4,6},{5,7},{6,4},{7,5},{8,10},{9,11},{10,... | collective-permute-start | bytes 589832 | tf_op jit(solution)/shard_map/ppermute | solution.py:36
  167.9 5.5 %decoder_ffn_first.1 = (bf16[512,768]{1,0:T(8,128)(2,1)}, bf16[512,768]{1,0:T(8,128)(2,1)}, bf16[512,768]{1,0:T(8,128)(2,1)}, bf16[512,768]{1,0:T(8,128)(2,1)}, ...) custom-call(bf16[128,768]{1,0:T(8,128)(2,1)} %get-tuple-element.103.c0, bf16[128,768]{1,0:T(8,128)(2,1)} %copy-done.42, ...), custom_call_target="tpu_custom_call" | custom-call | flops 1811939328 | bytes 3932160 | tf_op jit(solution)/shard_map/decoder_ffn_first/pallas_call | solution.py:424
  174.6 6.8 %decoder_ffn_second.1 = (f32[128,768]{1,0:T(8,128)}, bf16[3,128,768]{2,1,0:T(8,128)(2,1)}, bf16[4,2,96,768]{3,2,1,0:T(8,128)(2,1)}, bf16[4,2,96,768]{3,2,1,0:T(8,128)(2,1)}) custom-call(s32[1]{0:T(128)} %bitcast.refs_0_.place, bf16[512,768]{1,0:T(8,128)(2,1)} %get-tuple-element.125.c_all, bf16[512,768]{1,0:T(8,128)(2,1)} %get-tuple-element.126.g_all, ...), custom_call_target="tpu_custom_call" | custom-call | flops 1811939328 | bytes 4325380 | tf_op jit(solution)/shard_map/decoder_ffn_second/pallas_call | solution.py:424
  184.0 3.2 collective-permute-start.49
  187.1 11.8 %collective-permute-done.11.c2 = bf16[128,768]{1,0:T(8,128)(2,1)S(1)} collective-permute-done((bf16[128,768]{1,0:T(8,128)(2,1)}, bf16[128,768]{1,0:T(8,128)(2,1)S(1)}, u32[]{:S(2)}, u32[]{:S(2)}) %collective-permute-start.11) | collective-permute-done | bytes 196640 | tf_op jit(solution)/shard_map/ppermute | solution.py:36
  201.0 5.6 %encoder_ffn_first.1 = (bf16[512,768]{1,0:T(8,128)(2,1)}, bf16[512,768]{1,0:T(8,128)(2,1)}, bf16[512,768]{1,0:T(8,128)(2,1)}, bf16[512,768]{1,0:T(8,128)(2,1)}, ...) custom-call(bf16[128,768]{1,0:T(8,128)(2,1)} %get-tuple-element.85.c0, bf16[128,768]{1,0:T(8,128)(2,1)} %copy-done.45, ...), custom_call_target="tpu_custom_call" | custom-call | flops 1811939328 | bytes 3932160 | tf_op jit(solution)/shard_map/encoder_ffn_first/pallas_call | solution.py:424
  207.8 6.7 %encoder_ffn_second.1 = (f32[128,768]{1,0:T(8,128)}, bf16[3,128,768]{2,1,0:T(8,128)(2,1)}, bf16[4,2,96,768]{3,2,1,0:T(8,128)(2,1)}, bf16[4,2,96,768]{3,2,1,0:T(8,128)(2,1)}) custom-call(s32[1]{0:T(128)} %bitcast.refs_0_.place, bf16[512,768]{1,0:T(8,128)(2,1)} %get-tuple-element.86.c_all, bf16[512,768]{1,0:T(8,128)(2,1)} %get-tuple-element.87.g_all, ...), custom_call_target="tpu_custom_call" | custom-call | flops 1811939328 | bytes 4325380 | tf_op jit(solution)/shard_map/encoder_ffn_second/pallas_call | solution.py:424
  219.7 17.0 %cross_backward.1 = (f32[128,768]{1,0:T(8,128)}, f32[1,768]{1,0:T(1,128)}, bf16[4,4,96,768]{3,2,1,0:T(8,128)(2,1)}, bf16[4,4,96,768]{3,2,1,0:T(8,128)(2,1)}, f32[1,768]{1,0:T(1,128)}, /*index=5*/f32[128,768]{1,0:T(8,128)}) custom-call(s32[1]{0:T(128)} %bitcast.refs_0_.place, f32[128,768]{1,0:T(8,128)} %get-tuple-element.104.refs_1_, ...), custom_call_target="tpu_custom_call" | custom-call | flops 1207959552 | bytes 7870468 | tf_op jit(solution)/shard_map/cross_backward/pallas_call | solution.py:424
  236.7 16.3 %self_backward.1 = (f32[128,768]{1,0:T(8,128)}, f32[1,768]{1,0:T(1,128)}, bf16[4,4,96,768]{3,2,1,0:T(8,128)(2,1)}, bf16[4,4,96,768]{3,2,1,0:T(8,128)(2,1)}, f32[12,32,128]{2,1,0:T(8,128)}) custom-call(s32[1]{0:T(128)} %bitcast.refs_0_.place, f32[128,768]{1,0:T(8,128)} %get-tuple-element.111.refs_1_, bf16[128,768]{1,0:T(8,128)(2,1)} %refs_2_.3, ...), custom_call_target="tpu_custom_call" | custom-call | flops 1207959552 | bytes 6720516 | tf_op jit(solution)/shard_map/self_backward/pallas_call | solution.py:424
  257.6 17.6 %encoder_backward.1 = (f32[128,768]{1,0:T(8,128)}, f32[1,768]{1,0:T(1,128)}, bf16[4,4,96,768]{3,2,1,0:T(8,128)(2,1)}, bf16[4,4,96,768]{3,2,1,0:T(8,128)(2,1)}, f...) custom-call(s32[1]{0:T(128)} %bitcast.refs_0_.place, f32[128,768]{1,0:T(8,128)} %get-tuple-element.92.refs_1_, ...), custom_call_target="tpu_custom_call" | custom-call | flops 1207959552 | bytes 8198148 | tf_op jit(solution)/shard_map/encoder_backward/pallas_call | solution.py:424
  289.8 2.1 collective-permute-start.18
  293.8 9.2 %collective-permute-done.17 = bf16[128,768]{1,0:T(8,128)(2,1)S(1)} collective-permute-done((bf16[128,768]{1,0:T(8,128)(2,1)}, bf16[128,768]{1,0:T(8,128)(2,1)S(1)}, u32[]{:S(2)}, u32[]{:S(2)}) %collective-permute-start.17) | collective-permute-done | bytes 196640 | tf_op jit(solution)/shard_map/ppermute | solution.py:41
  303.0 4.9 %collective-permute-start.54 = (f32[36,128]{1,0:T(8,128)S(1)}, f32[36,128]{1,0:T(8,128)S(1)}, u32[]{:S(2)}, u32[]{:S(2)}) collective-permute-start(f32[36,128]{1,0:T(8,128)S(1)} %add.571), channel_id=1, source_target_pairs={{0,1},{1,0},{2,3},{3,2},{4,5},{5,4},{6,7},{7,6},{8,9},{9,8},{10,11... | collective-permute-start | bytes 55304 | tf_op jit(solution)/shard_map/ppermute | solution.py:45
  311.5 2.8 collective-permute-done.55
  320.8 5.0 %collective-permute-done.89 = bf16[2,1,96,768]{3,2,1,0:T(8,128)(2,1)S(1)} collective-permute-done((bf16[2,1,96,768]{3,2,1,0:T(8,128)(2,1)S(1)}, bf16[2,1,96,768]{3,2,1,0:T(8,128)(2,1)S(1)}, u32[]{:S(2)}, u32[]{:S(2)}) %collective-permute-start.89) | collective-permute-done | bytes 294944 | tf_op jit(solution)/shard_map/ppermute | solution.py:49
  332.0 6.3 %collective-permute-done.65 = bf16[2,1,96,768]{3,2,1,0:T(8,128)(2,1)S(1)} collective-permute-done((bf16[2,1,96,768]{3,2,1,0:T(8,128)(2,1)}, bf16[2,1,96,768]{3,2,1,0:T(8,128)(2,1)S(1)}, u32[]{:S(2)}, u32[]{:S(2)}) %collective-permute-start.65) | collective-permute-done | bytes 294944 | tf_op jit(solution)/shard_map/ppermute | solution.py:49
  339.8 2.3 collective-permute-done.67
  345.5 3.2 collective-permute-done.92
  348.7 2.1 fusion.25
  362.5 6.4 %collective-permute-done.81 = bf16[2,2,96,768]{3,2,1,0:T(8,128)(2,1)S(1)} collective-permute-done((bf16[2,2,96,768]{3,2,1,0:T(8,128)(2,1)S(1)}, bf16[2,2,96,768]{3,2,1,0:T(8,128)(2,1)S(1)}, u32[]{:S(2)}, u32[]{:S(2)}) %collective-permute-start.81) | collective-permute-done | bytes 589856 | tf_op jit(solution)/shard_map/ppermute | solution.py:49
  374.3 7.2 %collective-permute-done.73 = bf16[2,2,96,768]{3,2,1,0:T(8,128)(2,1)S(1)} collective-permute-done((bf16[2,2,96,768]{3,2,1,0:T(8,128)(2,1)S(1)}, bf16[2,2,96,768]{3,2,1,0:T(8,128)(2,1)S(1)}, u32[]{:S(2)}, u32[]{:S(2)}) %collective-permute-start.73) | collective-permute-done | bytes 589856 | tf_op jit(solution)/shard_map/ppermute | solution.py:49
  385.0 9.2 %collective-permute-done.57 = bf16[2,2,96,768]{3,2,1,0:T(8,128)(2,1)S(1)} collective-permute-done((bf16[2,2,96,768]{3,2,1,0:T(8,128)(2,1)S(1)}, bf16[2,2,96,768]{3,2,1,0:T(8,128)(2,1)S(1)}, u32[]{:S(2)}, u32[]{:S(2)}) %collective-permute-start.57) | collective-permute-done | bytes 589856 | tf_op jit(solution)/shard_map/ppermute | solution.py:49
  397.6 4.6 %collective-permute-done.82 = bf16[2,96,768]{2,1,0:T(8,128)(2,1)S(1)} collective-permute-done((bf16[2,96,768]{2,1,0:T(8,128)(2,1)S(1)}, bf16[2,96,768]{2,1,0:T(8,128)(2,1)S(1)}, u32[]{:S(2)}, u32[]{:S(2)}) %collective-permute-start.82) | collective-permute-done | bytes 294944 | tf_op jit(solution)/shard_map/ppermute | solution.py:49
  405.4 3.0 collective-permute-start.87
  410.7 3.1 collective-permute-start.79
  416.5 7.1 %collective-permute-start.62 = (bf16[96,768]{1,0:T(8,128)(2,1)}, bf16[96,768]{1,0:T(8,128)(2,1)S(1)}, u32[]{:S(2)}, u32[]{:S(2)}) collective-permute-start(bf16[96,768]{1,0:T(8,128)(2,1)} %get-tuple-element.323), channel_id=1, source_target_pairs={{0,2},{1,3},{2,0},{3,1},{4,6},{5,7},{6,4},{7,5},{8,10},{9,11},{10,... | collective-permute-start | bytes 442376 | tf_op jit(solution)/shard_map/ppermute | solution.py:41
  423.6 3.7 collective-permute-start.63
  428.8 3.1 collective-permute-done.78
  436.1 2.8 collective-permute-done.59
  (410 shorter events, 170.5 us)
Async XLA Ops:
  7.2 434.5 %all-gather.2.cloned.1.call-start = ((), (), s32[]{:S(2)}) async-start(), calls=%async_computation | async-start | bytes 2365440 | tf_op jit(solution)/shard_map/all_gather | solution.py:718
  11.8 24.0 %collective-permute-start.23 = (bf16[96,768]{1,0:T(8,128)(2,1)}, bf16[96,768]{1,0:T(8,128)(2,1)}, u32[]{:S(2)}, u32[]{:S(2)}) collective-permute-start(bf16[96,768]{1,0:T(8,128)(2,1)} %pad_maximum_fusion.22), channel_id=1, source_target_pairs={{0,2},{1,3},{2,0},{3,1},{4,6},{5,7},{6,4},{7,5},{8,10},{9,11},{10,... | collective-permute-start | bytes 442376 | tf_op jit(solution)/shard_map/ppermute | solution.py:36
  15.8 23.3 %collective-permute-start.24 = (bf16[96,768]{1,0:T(8,128)(2,1)}, bf16[96,768]{1,0:T(8,128)(2,1)}, u32[]{:S(2)}, u32[]{:S(2)}) collective-permute-start(bf16[96,768]{1,0:T(8,128)(2,1)} %pad_maximum_fusion.22), channel_id=1, source_target_pairs={{0,1},{1,2},{2,3},{3,0},{4,5},{5,6},{6,7},{7,4},{8,9},{9,10},{10,1... | collective-permute-start | bytes 442376 | tf_op jit(solution)/shard_map/ppermute | solution.py:36
  17.4 22.8 %collective-permute-start.22 = (bf16[96,768]{1,0:T(8,128)(2,1)}, bf16[96,768]{1,0:T(8,128)(2,1)}, u32[]{:S(2)}, u32[]{:S(2)}) collective-permute-start(bf16[96,768]{1,0:T(8,128)(2,1)} %pad_maximum_fusion.22), channel_id=1, source_target_pairs={{0,3},{1,0},{2,1},{3,2},{4,7},{5,4},{6,5},{7,6},{8,11},{9,8},{10,9... | collective-permute-start | bytes 442376 | tf_op jit(solution)/shard_map/ppermute | solution.py:36
  23.3 19.1 %collective-permute-start.33 = (bf16[96,768]{1,0:T(8,128)(2,1)}, bf16[96,768]{1,0:T(8,128)(2,1)}, u32[]{:S(2)}, u32[]{:S(2)}) collective-permute-start(bf16[96,768]{1,0:T(8,128)(2,1)} %pad_maximum_fusion.23), channel_id=1, source_target_pairs={{0,2},{1,3},{2,0},{3,1},{4,6},{5,7},{6,4},{7,5},{8,10},{9,11},{10,... | collective-permute-start | bytes 442376 | tf_op jit(solution)/shard_map/ppermute | solution.py:36
  23.3 23.9 %collective-permute-start.34 = (bf16[96,768]{1,0:T(8,128)(2,1)}, bf16[96,768]{1,0:T(8,128)(2,1)}, u32[]{:S(2)}, u32[]{:S(2)}) collective-permute-start(bf16[96,768]{1,0:T(8,128)(2,1)} %pad_maximum_fusion.23), channel_id=1, source_target_pairs={{0,1},{1,2},{2,3},{3,0},{4,5},{5,6},{6,7},{7,4},{8,9},{9,10},{10,1... | collective-permute-start | bytes 442376 | tf_op jit(solution)/shard_map/ppermute | solution.py:36
  71.4 19.0 %collective-permute-start.5 = (bf16[2,96,768]{2,1,0:T(8,128)(2,1)S(1)}, bf16[2,96,768]{2,1,0:T(8,128)(2,1)S(1)}, u32[]{:S(2)}, u32[]{:S(2)}) collective-permute-start(bf16[2,96,768]{2,1,0:T(8,128)(2,1)S(1)} %pad_maximum_fusion.11), channel_id=1, source_target_pairs={{0,16},{4,20},{8,24},{12,28},{16,0},{20,4},{24,8},{28,12},{1,17},{... | collective-permute-start | bytes 884744 | tf_op jit(solution)/shard_map/ppermute | solution.py:49
  72.2 18.7 %collective-permute-start.3 = (bf16[2,96,768]{2,1,0:T(8,128)(2,1)S(1)}, bf16[2,96,768]{2,1,0:T(8,128)(2,1)S(1)}, u32[]{:S(2)}, u32[]{:S(2)}) collective-permute-start(bf16[2,96,768]{2,1,0:T(8,128)(2,1)S(1)} %pad_maximum_fusion.11), channel_id=1, source_target_pairs={{0,8},{4,12},{8,0},{12,4},{16,24},{20,28},{24,16},{28,20},{1,9},{5... | collective-permute-start | bytes 884744 | tf_op jit(solution)/shard_map/ppermute | solution.py:49
  98.5 20.9 %collective-permute-start.31 = (bf16[4,4,96,768]{3,2,1,0:T(8,128)(2,1)}, bf16[4,4,96,768]{3,2,1,0:T(8,128)(2,1)}, u32[]{:S(2)}, u32[]{:S(2)}) collective-permute-start(bf16[4,4,96,768]{3,2,1,0:T(8,128)(2,1)} %pad_maximum_fusion.1.refs_5_.refs_8_), channel_id=1, source_target_pairs={{0,4},{4,0},{8,12},{12,8},{16,20},{20,16},{24,28},{28,24},{1,5},{5... | collective-permute-start | bytes 7077896 | tf_op jit(solution)/shard_map/ppermute | solution.py:49
  104.2 25.0 %collective-permute-start.41 = (bf16[4,4,96,768]{3,2,1,0:T(8,128)(2,1)}, bf16[4,4,96,768]{3,2,1,0:T(8,128)(2,1)}, u32[]{:S(2)}, u32[]{:S(2)}) collective-permute-start(bf16[4,4,96,768]{3,2,1,0:T(8,128)(2,1)} %pad_maximum_fusion.2.refs_5_.refs_13_), channel_id=1, source_target_pairs={{0,4},{4,0},{8,12},{12,8},{16,20},{20,16},{24,28},{28,24},{1,5},{5... | collective-permute-start | bytes 7077896 | tf_op jit(solution)/shard_map/ppermute | solution.py:49
  107.9 31.1 %collective-permute-start.9 = (bf16[4,4,96,768]{3,2,1,0:T(8,128)(2,1)}, bf16[4,4,96,768]{3,2,1,0:T(8,128)(2,1)}, u32[]{:S(2)}, u32[]{:S(2)}) collective-permute-start(bf16[4,4,96,768]{3,2,1,0:T(8,128)(2,1)} %pad_maximum_fusion.refs_6_.refs_12_), channel_id=1, source_target_pairs={{0,4},{4,0},{8,12},{12,8},{16,20},{20,16},{24,28},{28,24},{1,5},{5... | collective-permute-start | bytes 7077896 | tf_op jit(solution)/shard_map/ppermute | solution.py:49
  107.9 31.0 %collective-permute-start.45 = (bf16[128,768]{1,0:T(8,128)(2,1)S(1)}, bf16[128,768]{1,0:T(8,128)(2,1)}, u32[]{:S(2)}, u32[]{:S(2)}) collective-permute-start(bf16[128,768]{1,0:T(8,128)(2,1)S(1)} %copy-done.24), channel_id=1, source_target_pairs={{0,3},{1,0},{2,1},{3,2},{4,7},{5,4},{6,5},{7,6},{8,11},{9,8},{10,9... | collective-permute-start | bytes 589832 | tf_op jit(solution)/shard_map/ppermute | solution.py:36
  110.7 40.7 %collective-permute-start.46 = (bf16[128,768]{1,0:T(8,128)(2,1)S(1)}, bf16[128,768]{1,0:T(8,128)(2,1)}, u32[]{:S(2)}, u32[]{:S(2)}) collective-permute-start(bf16[128,768]{1,0:T(8,128)(2,1)S(1)} %copy-done.24), channel_id=1, source_target_pairs={{0,2},{1,3},{2,0},{3,1},{4,6},{5,7},{6,4},{7,5},{8,10},{9,11},{10,... | collective-permute-start | bytes 589832 | tf_op jit(solution)/shard_map/ppermute | solution.py:36
  119.4 35.3 %collective-permute-start.47 = (bf16[128,768]{1,0:T(8,128)(2,1)S(1)}, bf16[128,768]{1,0:T(8,128)(2,1)S(1)}, u32[]{:S(2)}, u32[]{:S(2)}) collective-permute-start(bf16[128,768]{1,0:T(8,128)(2,1)S(1)} %copy-done.24), channel_id=1, source_target_pairs={{0,1},{1,2},{2,3},{3,0},{4,5},{5,6},{6,7},{7,4},{8,9},{9,10},{10,1... | collective-permute-start | bytes 589832 | tf_op jit(solution)/shard_map/ppermute | solution.py:36
  137.0 18.7 %collective-permute-start.42 = (bf16[128,768]{1,0:T(8,128)(2,1)}, bf16[128,768]{1,0:T(8,128)(2,1)S(1)}, u32[]{:S(2)}, u32[]{:S(2)}) collective-permute-start(bf16[128,768]{1,0:T(8,128)(2,1)} %get-tuple-element.103.c0), channel_id=1, source_target_pairs={{0,3},{1,0},{2,1},{3,2},{4,7},{5,4},{6,5},{7,6},{8,11},{9,8},{10,9... | collective-permute-start | bytes 589832 | tf_op jit(solution)/shard_map/ppermute | solution.py:36
  139.0 17.8 %collective-permute-start.43 = (bf16[128,768]{1,0:T(8,128)(2,1)}, bf16[128,768]{1,0:T(8,128)(2,1)S(1)}, u32[]{:S(2)}, u32[]{:S(2)}) collective-permute-start(bf16[128,768]{1,0:T(8,128)(2,1)} %get-tuple-element.103.c0), channel_id=1, source_target_pairs={{0,2},{1,3},{2,0},{3,1},{4,6},{5,7},{6,4},{7,5},{8,10},{9,11},{10,... | collective-permute-start | bytes 589832 | tf_op jit(solution)/shard_map/ppermute | solution.py:36
  139.0 20.8 %collective-permute-start.44 = (bf16[128,768]{1,0:T(8,128)(2,1)}, bf16[128,768]{1,0:T(8,128)(2,1)S(1)}, u32[]{:S(2)}, u32[]{:S(2)}) collective-permute-start(bf16[128,768]{1,0:T(8,128)(2,1)} %get-tuple-element.103.c0), channel_id=1, source_target_pairs={{0,1},{1,2},{2,3},{3,0},{4,5},{5,6},{6,7},{7,4},{8,9},{9,10},{10,1... | collective-permute-start | bytes 589832 | tf_op jit(solution)/shard_map/ppermute | solution.py:36
  151.4 30.0 %collective-permute-start.13 = (bf16[128,768]{1,0:T(8,128)(2,1)S(1)}, bf16[128,768]{1,0:T(8,128)(2,1)S(1)}, u32[]{:S(2)}, u32[]{:S(2)}) collective-permute-start(bf16[128,768]{1,0:T(8,128)(2,1)S(1)} %copy-done.25), channel_id=1, source_target_pairs={{0,3},{1,0},{2,1},{3,2},{4,7},{5,4},{6,5},{7,6},{8,11},{9,8},{10,9... | collective-permute-start | bytes 589832 | tf_op jit(solution)/shard_map/ppermute | solution.py:36
  154.7 27.9 %collective-permute-start.14 = (bf16[128,768]{1,0:T(8,128)(2,1)S(1)}, bf16[128,768]{1,0:T(8,128)(2,1)S(1)}, u32[]{:S(2)}, u32[]{:S(2)}) collective-permute-start(bf16[128,768]{1,0:T(8,128)(2,1)S(1)} %copy-done.25), channel_id=1, source_target_pairs={{0,2},{1,3},{2,0},{3,1},{4,6},{5,7},{6,4},{7,5},{8,10},{9,11},{10,... | collective-permute-start | bytes 589832 | tf_op jit(solution)/shard_map/ppermute | solution.py:36
  155.8 26.9 %collective-permute-start.15 = (bf16[128,768]{1,0:T(8,128)(2,1)S(1)}, bf16[128,768]{1,0:T(8,128)(2,1)S(1)}, u32[]{:S(2)}, u32[]{:S(2)}) collective-permute-start(bf16[128,768]{1,0:T(8,128)(2,1)S(1)} %copy-done.25), channel_id=1, source_target_pairs={{0,1},{1,2},{2,3},{3,0},{4,5},{5,6},{6,7},{7,4},{8,9},{9,10},{10,1... | collective-permute-start | bytes 589832 | tf_op jit(solution)/shard_map/ppermute | solution.py:36
  156.8 27.1 %collective-permute-start.10 = (bf16[128,768]{1,0:T(8,128)(2,1)}, bf16[128,768]{1,0:T(8,128)(2,1)S(1)}, u32[]{:S(2)}, u32[]{:S(2)}) collective-permute-start(bf16[128,768]{1,0:T(8,128)(2,1)} %get-tuple-element.85.c0), channel_id=1, source_target_pairs={{0,3},{1,0},{2,1},{3,2},{4,7},{5,4},{6,5},{7,6},{8,11},{9,8},{10,9... | collective-permute-start | bytes 589832 | tf_op jit(solution)/shard_map/ppermute | solution.py:36
  159.8 39.2 %collective-permute-start.11 = (bf16[128,768]{1,0:T(8,128)(2,1)}, bf16[128,768]{1,0:T(8,128)(2,1)S(1)}, u32[]{:S(2)}, u32[]{:S(2)}) collective-permute-start(bf16[128,768]{1,0:T(8,128)(2,1)} %get-tuple-element.85.c0), channel_id=1, source_target_pairs={{0,2},{1,3},{2,0},{3,1},{4,6},{5,7},{6,4},{7,5},{8,10},{9,11},{10,... | collective-permute-start | bytes 589832 | tf_op jit(solution)/shard_map/ppermute | solution.py:36
  182.6 132.3 %collective-permute-start.88 = (bf16[4,2,96,768]{3,2,1,0:T(8,128)(2,1)}, bf16[4,2,96,768]{3,2,1,0:T(8,128)(2,1)}, u32[]{:S(2)}, u32[]{:S(2)}) collective-permute-start(bf16[4,2,96,768]{3,2,1,0:T(8,128)(2,1)} %get-tuple-element.138), channel_id=1, source_target_pairs={{0,4},{4,0},{8,12},{12,8},{16,20},{20,16},{24,28},{28,24},{1,5},{5... | collective-permute-start | bytes 3538952 | tf_op jit(solution)/shard_map/ppermute | solution.py:49
  182.7 31.8 %collective-permute-start.48 = (bf16[128,768]{1,0:T(8,128)(2,1)S(1)}, bf16[128,768]{1,0:T(8,128)(2,1)S(1)}, u32[]{:S(2)}, u32[]{:S(2)}) collective-permute-start(bf16[128,768]{1,0:T(8,128)(2,1)S(1)} %get-tuple-element.298), channel_id=1, source_target_pairs={{0,1},{1,2},{2,3},{3,0},{4,5},{5,6},{6,7},{7,4},{8,9},{9,10},{10,1... | collective-permute-start | bytes 589832 | tf_op jit(solution)/shard_map/ppermute | solution.py:41
  184.0 31.2 %collective-permute-start.49 = (bf16[128,768]{1,0:T(8,128)(2,1)S(1)}, bf16[128,768]{1,0:T(8,128)(2,1)S(1)}, u32[]{:S(2)}, u32[]{:S(2)}) collective-permute-start(bf16[128,768]{1,0:T(8,128)(2,1)S(1)} %get-tuple-element.300), channel_id=1, source_target_pairs={{0,2},{1,3},{2,0},{3,1},{4,6},{5,7},{6,4},{7,5},{8,10},{9,11},{10,... | collective-permute-start | bytes 589832 | tf_op jit(solution)/shard_map/ppermute | solution.py:41
  199.0 18.0 %collective-permute-start.50 = (bf16[128,768]{1,0:T(8,128)(2,1)S(1)}, bf16[128,768]{1,0:T(8,128)(2,1)S(1)}, u32[]{:S(2)}, u32[]{:S(2)}) collective-permute-start(bf16[128,768]{1,0:T(8,128)(2,1)S(1)} %get-tuple-element.299), channel_id=1, source_target_pairs={{0,3},{1,0},{2,1},{3,2},{4,7},{5,4},{6,5},{7,6},{8,11},{9,8},{10,9... | collective-permute-start | bytes 589832 | tf_op jit(solution)/shard_map/ppermute | solution.py:41
  199.0 84.9 %collective-permute-start.69 = (bf16[128,768]{1,0:T(8,128)(2,1)S(1)}, bf16[128,768]{1,0:T(8,128)(2,1)}, u32[]{:S(2)}, u32[]{:S(2)}) collective-permute-start(bf16[128,768]{1,0:T(8,128)(2,1)S(1)} %get-tuple-element.295), channel_id=1, source_target_pairs={{0,1},{1,2},{2,3},{3,0},{4,5},{5,6},{6,7},{7,4},{8,9},{9,10},{10,1... | collective-permute-start | bytes 589832 | tf_op jit(solution)/shard_map/ppermute | solution.py:41
  214.5 39.2 %collective-permute-start.19 = (bf16[128,768]{1,0:T(8,128)(2,1)S(1)}, bf16[128,768]{1,0:T(8,128)(2,1)S(1)}, u32[]{:S(2)}, u32[]{:S(2)}) collective-permute-start(bf16[128,768]{1,0:T(8,128)(2,1)S(1)} %get-tuple-element.301), channel_id=1, source_target_pairs={{0,1},{1,2},{2,3},{3,0},{4,5},{5,6},{6,7},{7,4},{8,9},{9,10},{10,1... | collective-permute-start | bytes 589832 | tf_op jit(solution)/shard_map/ppermute | solution.py:41
  215.1 40.6 %collective-permute-start.20 = (bf16[128,768]{1,0:T(8,128)(2,1)S(1)}, bf16[128,768]{1,0:T(8,128)(2,1)S(1)}, u32[]{:S(2)}, u32[]{:S(2)}) collective-permute-start(bf16[128,768]{1,0:T(8,128)(2,1)S(1)} %get-tuple-element.303), channel_id=1, source_target_pairs={{0,2},{1,3},{2,0},{3,1},{4,6},{5,7},{6,4},{7,5},{8,10},{9,11},{10,... | collective-permute-start | bytes 589832 | tf_op jit(solution)/shard_map/ppermute | solution.py:41
  216.9 39.8 %collective-permute-start.21 = (bf16[128,768]{1,0:T(8,128)(2,1)S(1)}, bf16[128,768]{1,0:T(8,128)(2,1)S(1)}, u32[]{:S(2)}, u32[]{:S(2)}) collective-permute-start(bf16[128,768]{1,0:T(8,128)(2,1)S(1)} %get-tuple-element.302), channel_id=1, source_target_pairs={{0,3},{1,0},{2,1},{3,2},{4,7},{5,4},{6,5},{7,6},{8,11},{9,8},{10,9... | collective-permute-start | bytes 589832 | tf_op jit(solution)/shard_map/ppermute | solution.py:41
  253.7 31.3 %collective-permute-start.70 = (bf16[128,768]{1,0:T(8,128)(2,1)S(1)}, bf16[128,768]{1,0:T(8,128)(2,1)}, u32[]{:S(2)}, u32[]{:S(2)}) collective-permute-start(bf16[128,768]{1,0:T(8,128)(2,1)S(1)} %get-tuple-element.297), channel_id=1, source_target_pairs={{0,2},{1,3},{2,0},{3,1},{4,6},{5,7},{6,4},{7,5},{8,10},{9,11},{10,... | collective-permute-start | bytes 589832 | tf_op jit(solution)/shard_map/ppermute | solution.py:41
  255.7 30.3 %collective-permute-start.71 = (bf16[128,768]{1,0:T(8,128)(2,1)S(1)}, bf16[128,768]{1,0:T(8,128)(2,1)}, u32[]{:S(2)}, u32[]{:S(2)}) collective-permute-start(bf16[128,768]{1,0:T(8,128)(2,1)S(1)} %get-tuple-element.296), channel_id=1, source_target_pairs={{0,3},{1,0},{2,1},{3,2},{4,7},{5,4},{6,5},{7,6},{8,11},{9,8},{10,9... | collective-permute-start | bytes 589832 | tf_op jit(solution)/shard_map/ppermute | solution.py:41
  283.9 34.0 %collective-permute-start.64 = (bf16[4,2,96,768]{3,2,1,0:T(8,128)(2,1)}, bf16[4,2,96,768]{3,2,1,0:T(8,128)(2,1)S(1)}, u32[]{:S(2)}, u32[]{:S(2)}) collective-permute-start(bf16[4,2,96,768]{3,2,1,0:T(8,128)(2,1)} %get-tuple-element.124), channel_id=1, source_target_pairs={{0,4},{4,0},{8,12},{12,8},{16,20},{20,16},{24,28},{28,24},{1,5},{5... | collective-permute-start | bytes 3538952 | tf_op jit(solution)/shard_map/ppermute | solution.py:49
  285.0 18.0 %collective-permute-start.17 = (bf16[128,768]{1,0:T(8,128)(2,1)}, bf16[128,768]{1,0:T(8,128)(2,1)S(1)}, u32[]{:S(2)}, u32[]{:S(2)}) collective-permute-start(bf16[128,768]{1,0:T(8,128)(2,1)} %get-tuple-element.306), channel_id=1, source_target_pairs={{0,2},{1,3},{2,0},{3,1},{4,6},{5,7},{6,4},{7,5},{8,10},{9,11},{10,... | collective-permute-start | bytes 589832 | tf_op jit(solution)/shard_map/ppermute | solution.py:41
  293.8 57.0 %collective-permute-start.80 = (bf16[4,4,96,768]{3,2,1,0:T(8,128)(2,1)}, bf16[4,4,96,768]{3,2,1,0:T(8,128)(2,1)}, u32[]{:S(2)}, u32[]{:S(2)}) collective-permute-start(bf16[4,4,96,768]{3,2,1,0:T(8,128)(2,1)} %get-tuple-element.136), channel_id=1, source_target_pairs={{0,4},{4,0},{8,12},{12,8},{16,20},{20,16},{24,28},{28,24},{1,5},{5... | collective-permute-start | bytes 7077896 | tf_op jit(solution)/shard_map/ppermute | solution.py:49
  303.0 51.7 %collective-permute-start.72 = (bf16[4,4,96,768]{3,2,1,0:T(8,128)(2,1)}, bf16[4,4,96,768]{3,2,1,0:T(8,128)(2,1)}, u32[]{:S(2)}, u32[]{:S(2)}) collective-permute-start(bf16[4,4,96,768]{3,2,1,0:T(8,128)(2,1)} %get-tuple-element.134), channel_id=1, source_target_pairs={{0,4},{4,0},{8,12},{12,8},{16,20},{20,16},{24,28},{28,24},{1,5},{5... | collective-permute-start | bytes 7077896 | tf_op jit(solution)/shard_map/ppermute | solution.py:49
  314.3 42.2 %collective-permute-start.56 = (bf16[4,4,96,768]{3,2,1,0:T(8,128)(2,1)}, bf16[4,4,96,768]{3,2,1,0:T(8,128)(2,1)}, u32[]{:S(2)}, u32[]{:S(2)}) collective-permute-start(bf16[4,4,96,768]{3,2,1,0:T(8,128)(2,1)} %get-tuple-element.122), channel_id=1, source_target_pairs={{0,4},{4,0},{8,12},{12,8},{16,20},{20,16},{24,28},{28,24},{1,5},{5... | collective-permute-start | bytes 7077896 | tf_op jit(solution)/shard_map/ppermute | solution.py:49
  354.7 18.1 %collective-permute-start.84 = (bf16[2,2,96,768]{3,2,1,0:T(8,128)(2,1)S(1)}, bf16[2,2,96,768]{3,2,1,0:T(8,128)(2,1)S(1)}, u32[]{:S(2)}, u32[]{:S(2)}) collective-permute-start(bf16[2,2,96,768]{3,2,1,0:T(8,128)(2,1)S(1)} %pad_maximum_fusion.10), channel_id=1, source_target_pairs={{0,16},{4,20},{8,24},{12,28},{16,0},{20,4},{24,8},{28,12},{1,17},{... | collective-permute-start | bytes 1769480 | tf_op jit(solution)/shard_map/ppermute | solution.py:49
  356.5 25.0 %collective-permute-start.73 = (bf16[2,2,96,768]{3,2,1,0:T(8,128)(2,1)S(1)}, bf16[2,2,96,768]{3,2,1,0:T(8,128)(2,1)S(1)}, u32[]{:S(2)}, u32[]{:S(2)}) collective-permute-start(bf16[2,2,96,768]{3,2,1,0:T(8,128)(2,1)S(1)} %pad_maximum_fusion.7), channel_id=1, source_target_pairs={{0,8},{4,12},{8,0},{12,4},{16,24},{20,28},{24,16},{28,20},{1,9},{5... | collective-permute-start | bytes 1769480 | tf_op jit(solution)/shard_map/ppermute | solution.py:49
  360.2 23.5 %collective-permute-start.76 = (bf16[2,2,96,768]{3,2,1,0:T(8,128)(2,1)S(1)}, bf16[2,2,96,768]{3,2,1,0:T(8,128)(2,1)S(1)}, u32[]{:S(2)}, u32[]{:S(2)}) collective-permute-start(bf16[2,2,96,768]{3,2,1,0:T(8,128)(2,1)S(1)} %pad_maximum_fusion.8), channel_id=1, source_target_pairs={{0,16},{4,20},{8,24},{12,28},{16,0},{20,4},{24,8},{28,12},{1,17},{... | collective-permute-start | bytes 1769480 | tf_op jit(solution)/shard_map/ppermute | solution.py:49
  360.6 33.5 %collective-permute-start.57 = (bf16[2,2,96,768]{3,2,1,0:T(8,128)(2,1)S(1)}, bf16[2,2,96,768]{3,2,1,0:T(8,128)(2,1)S(1)}, u32[]{:S(2)}, u32[]{:S(2)}) collective-permute-start(bf16[2,2,96,768]{3,2,1,0:T(8,128)(2,1)S(1)} %pad_maximum_fusion.5), channel_id=1, source_target_pairs={{0,8},{4,12},{8,0},{12,4},{16,24},{20,28},{24,16},{28,20},{1,9},{5... | collective-permute-start | bytes 1769480 | tf_op jit(solution)/shard_map/ppermute | solution.py:49
  368.9 27.4 %collective-permute-start.60 = (bf16[2,2,96,768]{3,2,1,0:T(8,128)(2,1)S(1)}, bf16[2,2,96,768]{3,2,1,0:T(8,128)(2,1)S(1)}, u32[]{:S(2)}, u32[]{:S(2)}) collective-permute-start(bf16[2,2,96,768]{3,2,1,0:T(8,128)(2,1)S(1)} %pad_maximum_fusion.6), channel_id=1, source_target_pairs={{0,16},{4,20},{8,24},{12,28},{16,0},{20,4},{24,8},{28,12},{1,17},{... | collective-permute-start | bytes 1769480 | tf_op jit(solution)/shard_map/ppermute | solution.py:49
  374.1 28.2 %collective-permute-start.82 = (bf16[2,96,768]{2,1,0:T(8,128)(2,1)S(1)}, bf16[2,96,768]{2,1,0:T(8,128)(2,1)S(1)}, u32[]{:S(2)}, u32[]{:S(2)}) collective-permute-start(bf16[2,96,768]{2,1,0:T(8,128)(2,1)S(1)} %get-tuple-element.258), channel_id=1, source_target_pairs={{0,16},{4,20},{8,24},{12,28},{16,0},{20,4},{24,8},{28,12},{1,17},{... | collective-permute-start | bytes 884744 | tf_op jit(solution)/shard_map/ppermute | solution.py:49
  381.5 21.1 %collective-permute-start.85 = (bf16[2,96,768]{2,1,0:T(8,128)(2,1)S(1)}, bf16[2,96,768]{2,1,0:T(8,128)(2,1)S(1)}, u32[]{:S(2)}, u32[]{:S(2)}) collective-permute-start(bf16[2,96,768]{2,1,0:T(8,128)(2,1)S(1)} %get-tuple-element.257), channel_id=1, source_target_pairs={{0,8},{4,12},{8,0},{12,4},{16,24},{20,28},{24,16},{28,20},{1,9},{5... | collective-permute-start | bytes 884744 | tf_op jit(solution)/shard_map/ppermute | solution.py:49
  384.9 20.5 %collective-permute-start.74 = (bf16[2,96,768]{2,1,0:T(8,128)(2,1)S(1)}, bf16[2,96,768]{2,1,0:T(8,128)(2,1)S(1)}, u32[]{:S(2)}, u32[]{:S(2)}) collective-permute-start(bf16[2,96,768]{2,1,0:T(8,128)(2,1)S(1)} %get-tuple-element.266), channel_id=1, source_target_pairs={{0,16},{4,20},{8,24},{12,28},{16,0},{20,4},{24,8},{28,12},{1,17},{... | collective-permute-start | bytes 884744 | tf_op jit(solution)/shard_map/ppermute | solution.py:49
  409.8 22.1 %collective-permute-start.78 = (bf16[96,768]{1,0:T(8,128)(2,1)S(1)}, bf16[96,768]{1,0:T(8,128)(2,1)S(1)}, u32[]{:S(2)}, u32[]{:S(2)}) collective-permute-start(bf16[96,768]{1,0:T(8,128)(2,1)S(1)} %get-tuple-element.317), channel_id=1, source_target_pairs={{0,2},{1,3},{2,0},{3,1},{4,6},{5,7},{6,4},{7,5},{8,10},{9,11},{10,... | collective-permute-start | bytes 442376 | tf_op jit(solution)/shard_map/ppermute | solution.py:41
  410.7 21.3 %collective-permute-start.79 = (bf16[96,768]{1,0:T(8,128)(2,1)S(1)}, bf16[96,768]{1,0:T(8,128)(2,1)}, u32[]{:S(2)}, u32[]{:S(2)}) collective-permute-start(bf16[96,768]{1,0:T(8,128)(2,1)S(1)} %get-tuple-element.318), channel_id=1, source_target_pairs={{0,3},{1,0},{2,1},{3,2},{4,7},{5,4},{6,5},{7,6},{8,11},{9,8},{10,9... | collective-permute-start | bytes 442376 | tf_op jit(solution)/shard_map/ppermute | solution.py:41
  416.5 19.0 %collective-permute-start.62 = (bf16[96,768]{1,0:T(8,128)(2,1)}, bf16[96,768]{1,0:T(8,128)(2,1)S(1)}, u32[]{:S(2)}, u32[]{:S(2)}) collective-permute-start(bf16[96,768]{1,0:T(8,128)(2,1)} %get-tuple-element.323), channel_id=1, source_target_pairs={{0,2},{1,3},{2,0},{3,1},{4,6},{5,7},{6,4},{7,5},{8,10},{9,11},{10,... | collective-permute-start | bytes 442376 | tf_op jit(solution)/shard_map/ppermute | solution.py:41
  (95 other events, 1228.0 us)
Sparse Core Ops, SparseCore 0:
  282.4 65.8 all-gather.1

commit v2 on v1

v2 whole, which is shorter than its diff:
```python
import functools

import jax
import jax.numpy as jnp
from jax import lax
from jax.experimental import pallas as pl
from jax.experimental.pallas import tpu as pltpu
from jax.sharding import PartitionSpec as P

DH = 64
SEQ = 64
MEMK = 10
PREFIX = 2
EPS = 1e-06
NEG = -1e30
BLOCKS = 8
bf16 = jnp.bfloat16
f32 = jnp.float32


def nn(left, right):
    return lax.dot_general(left, right, (((1,), (0,)), ((), ())), preferred_element_type=f32)


def nt(left, right):
    return lax.dot_general(left, right, (((1,), (1,)), ((), ())), preferred_element_type=f32)


def tn(left, right):
    return lax.dot_general(left, right, (((0,), (0,)), ((), ())), preferred_element_type=f32)


def from_mp(array, step):
    size = lax.axis_size("mp")
    return lax.ppermute(array, "mp", [(i, (i - step) % size) for i in range(size)])


def to_mp(array, step):
    size = lax.axis_size("mp")
    return lax.ppermute(array, "mp", [(i, (i + step) % size) for i in range(size)])


def swap_mp(array, bit):
    return lax.ppermute(array, "mp", [(i, i ^ bit) for i in range(lax.axis_size("mp"))])


def swap_dp(array, bit):
    return lax.ppermute(array, "dp", [(i, i ^ bit) for i in range(lax.axis_size("dp"))])


def after(value, *earlier):
    leaves, shape = jax.tree.flatten(value)
    tied = lax.optimization_barrier((*leaves, *jax.tree.leaves(earlier)))
    return jax.tree.unflatten(shape, tied[: len(leaves)])


def high_bits():
    low = lax.axis_size("dp") // BLOCKS
    return low, 2 * low, 4 * low


def rounded_sum(left, right):
    return (left.astype(f32) + right.astype(f32)).astype(bf16)


def stack_slots(block, others):
    return jnp.stack([block, others[0]]), jnp.stack(others[1:])


def spread_once(first, second):
    core, along, across = high_bits()
    return swap_dp(first, along), swap_dp(second, across)


def spread_twice(first_two, second_two):
    core, along, across = high_bits()
    return swap_dp(first_two, across), swap_dp(second_two, along)


def join_places(first_two, second_two, first_far, second_far):
    return jnp.concatenate(
        [
            jnp.concatenate([first_two, first_far]),
            jnp.stack([second_two[0], second_far[0], second_two[1], second_far[1]]),
        ],
        axis=1,
    )


def swap_cores(array):
    return swap_dp(array, high_bits()[0])


def fold_cores(keep, got):
    return tuple(
        (rounded_sum(keep[i, :2], got[i, :2]), rounded_sum(keep[i, 2:], got[i, 2:])) for i in range(2)
    )


def send_once(halves):
    core, along, across = high_bits()
    return swap_dp(halves[0][1], along), swap_dp(halves[1][1], across)


def fold_once(halves, got):
    return tuple(rounded_sum(halves[i][0][1], got[i][1]) for i in range(2))


def send_twice(last):
    core, along, across = high_bits()
    return swap_dp(last[0], across), swap_dp(last[1], along)


def fold_twice(halves, got, last_got):
    sums = [
        halves[i][0][0].astype(f32) + got[i][0].astype(f32) + last_got[i].astype(f32) for i in range(2)
    ]
    return [sums[0][0], sums[0][1], sums[1][0], sums[1][1]]


def send_slots(slots):
    return [to_mp(slots[step].astype(bf16), step) for step in range(1, 4)]


def scatter_rest(rows):
    size = lax.axis_size("dp")
    low = size // BLOCKS
    if low == 1:
        return rows
    groups = [[high * low + i for i in range(low)] for high in range(BLOCKS)]
    return lax.psum_scatter(
        rows, "dp", scatter_dimension=0, axis_index_groups=groups, tiled=True
    )


def four_matrices(slots, got):
    total = slots[0]
    if lax.axis_size("dp") == BLOCKS:
        rows, width = total.shape
        part = width // 4
        return call(
            finish_kernel,
            "matrices",
            [total, *got],
            (),
            (),
            [((rows, part), f32)] * 3 + [((part, rows), f32)],
            [],
        )
    for other in got:
        total = total + other.astype(f32)
    total = scatter_rest(total)
    width = total.shape[1] // 4
    parts = [total[:, i * width : (i + 1) * width] for i in range(4)]
    return parts[0], parts[1], parts[2], parts[3].T


def reduce_ffn(grads):
    return lax.psum_scatter(grads, "dp", scatter_dimension=0, tiled=True)


def two_matrices(sums):
    rows, width = sums.shape
    if rows % 16:
        sums = sums.astype(f32)
        return sums[:, : width // 2], sums[:, width // 2 :].T
    return call(
        finish_ffn_kernel,
        "ffn_matrices",
        [sums],
        (),
        (),
        [((rows, width // 2), f32), ((width // 2, rows), f32)],
        [],
    )


def gather_blocks(blocks):
    low = lax.axis_size("dp") // BLOCKS
    if low == 1:
        every = lax.all_gather(blocks, ("dp", "mp"), axis=0, tiled=False)
        return every.reshape(BLOCKS, -1, *blocks.shape)
    groups = [[high * low + i for high in range(BLOCKS)] for i in range(low)]
    return lax.all_gather(
        lax.all_gather(blocks, "mp", axis=0, tiled=False),
        "dp",
        axis=0,
        axis_index_groups=groups,
        tiled=False,
    )


def sum_everywhere(array):
    bit = 1
    while bit < lax.axis_size("dp"):
        array = array + swap_dp(array, bit)
        bit *= 2
    bit = 1
    while bit < lax.axis_size("mp"):
        array = array + swap_mp(array, bit)
        bit *= 2
    return array


def fetch_weights(parts, group, held, sems, place, mp_at, order):
    copies = {(what, slot): [] for what in order for slot in range(4)}
    if len(parts) == 2:
        for slot in range(4):
            for j in range(4):
                for side in range(2):
                    held[slot, place ^ (2 * j + side)] = parts[side][j, slot]
        return copies
    for i, what in enumerate(order):
        blocks = pl.ds(6, 2) if what == "merge" else pl.ds(0, 6)
        for slot in range(4):
            copy = pltpu.make_async_copy(
                parts[0].at[blocks, (mp_at + slot) % 4, group],
                held.at[slot, blocks],
                sems.at[slot, i],
            )
            copy.start()
            copies[what, slot].append(copy)
    return copies


def wait_all(copies):
    for copy in copies:
        copy.wait()


def slot_rows(held, slot, first, last):
    part = held[slot, 2 * first : 2 * last]
    return part.reshape(part.shape[0] * part.shape[1], part.shape[2])


def blocks_kernel(groups, place_ref, *refs):
    inputs = refs[: 4 * groups]
    first, others, sems = refs[4 * groups :]
    outs = [first] + [others.at[i] for i in range(groups - 1)]
    size = first.shape[0]
    place = place_ref[0]
    start = pl.multiple_of((place % 2) * size, size)
    for j in range(4):

        @pl.when(place // 2 == j)
        def _():
            copies = [
                pltpu.make_async_copy(inputs[4 * i + j].at[pl.ds(start, size)], outs[i], sems.at[i])
                for i in range(groups)
            ]
            for copy in copies:
                copy.start()
            wait_all(copies)


def inverse_rms(rows):
    return lax.rsqrt(jnp.mean(rows * rows, axis=-1, keepdims=True) + EPS)


def gain_rows(kind, gains_ref):
    at = {"encoder": (0, 1), "self": (2, 3), "cross": (3, 4)}[kind]
    return tuple(gains_ref[i : i + 1, :] for i in at)


def column_head(shape):
    return lax.broadcasted_iota(jnp.int32, shape, 1) // DH


def softmax_rows(scores):
    shifted = jnp.exp(scores - jnp.max(scores, axis=-1, keepdims=True))
    return shifted / jnp.sum(shifted, axis=-1, keepdims=True)


def masks(kind, rows, keys):
    row = lax.broadcasted_iota(jnp.int32, (rows, rows), 0)
    col = lax.broadcasted_iota(jnp.int32, (rows, rows), 1)
    same = row // SEQ == col // SEQ
    if kind == "self":
        same = jnp.logical_and(same, col <= row)
    if kind != "encoder":
        return same, None
    row = lax.broadcasted_iota(jnp.int32, (rows, keys - rows), 0)
    col = lax.broadcasted_iota(jnp.int32, (rows, keys - rows), 1)
    first = (row // SEQ) * (MEMK * PREFIX)
    valid = jnp.logical_and(col >= first, col < first + MEMK * PREFIX)
    return same, jnp.where(valid, 0.0, NEG)


def add_bias(kind, scores, rel_ref, slot, same, before):
    rows = scores.shape[0] // 3
    parts = []
    for j in range(3):
        part = scores[j * rows : (j + 1) * rows]
        own = part[:, :rows]
        if kind != "cross":
            rel = rel_ref[3 * slot + j]
            own = own + jnp.concatenate([rel] * (rows // SEQ), axis=0)
        own = jnp.where(same, own, NEG)
        if before is not None:
            own = jnp.concatenate([own, part[:, rows:] + before], axis=1)
        parts.append(own)
    return jnp.concatenate(parts, axis=0)


def stack_heads(array):
    head = column_head(array.shape)
    return jnp.concatenate([jnp.where(head == j, array, jnp.zeros_like(array)) for j in range(3)], axis=0)


def join_heads(stacked):
    rows = stacked.shape[0] // 3
    head = column_head((rows, stacked.shape[1]))
    return jnp.where(
        head == 0,
        stacked[:rows],
        jnp.where(head == 1, stacked[rows : 2 * rows], stacked[2 * rows :]),
    )


def attention_forward_kernel(kind, parts, *refs):
    refs = list(refs)
    place_ref, x_ref = refs[:2]
    del refs[:2]
    pre_ref = refs.pop(0) if kind != "self" else None
    gains_ref = refs.pop(0)
    gain, later = gain_rows(kind, gains_ref)
    rel_ref = refs.pop(0) if kind != "cross" else None
    weights = refs[:parts]
    r1_ref, next_ref, a_ref, q_ref, kv_ref, o_ref, held, sems = refs[parts:]
    copies = fetch_weights(weights, int(kind == "cross"), held, sems, place_ref[0], place_ref[1], ("rest", "merge"))
    r = x_ref[...].astype(f32)
    rows = r.shape[0]
    a = (r * inverse_rms(r) * gain).astype(bf16)
    if kind == "encoder":
        a_ref[0:rows, :] = a
        a_ref[rows:, :] = pre_ref[...]
        a_all = a_ref[...]
    else:
        a_ref[...] = a
        a_all = a
    keys = kv_ref.shape[1]
    same, before = masks(kind, rows, keys)
    queries = []
    sources = []
    for slot in range(4):
        wait_all(copies["rest", slot])
        if kind == "cross":
            q = nt(a, slot_rows(held, slot, 0, 1)).astype(bf16)
            kv = nt(pre_ref[...], slot_rows(held, slot, 1, 3)).astype(bf16)
        else:
            qkv = nt(a_all, slot_rows(held, slot, 0, 3)).astype(bf16)
            q = qkv[:rows, :192]
            kv = qkv[:, 192:]
        q_ref[slot] = q
        kv_ref[slot] = kv
        queries.append(q)
        sources.append(kv)
    chances = []
    for slot in range(4):
        scores = nt(stack_heads(queries[slot]), sources[slot][:, :192])
        chances.append(softmax_rows(add_bias(kind, scores, rel_ref, slot, same, before)).astype(bf16))
    mixed = []
    for slot in range(4):
        o = join_heads(nn(chances[slot], sources[slot][:, 192:])).astype(bf16)
        o_ref[slot] = o
        mixed.append(o)
    acc = r
    for slot in range(4):
        wait_all(copies["merge", slot])
        acc = acc + nn(mixed[slot], slot_rows(held, slot, 3, 4))
    r1_ref[...] = acc
    next_ref[...] = (acc * inverse_rms(acc) * later).astype(bf16)


def norm_back(dn, r, gain, dgain_ref):
    t = inverse_rms(r)
    dgain_ref[...] = jnp.sum(dn * r * t, axis=0, keepdims=True)
    scaled = dn * gain
    return t * (scaled - r * (t * t) * jnp.mean(scaled * r, axis=-1, keepdims=True))


def store_blocks(keep_ref, send_ref, place, slot, value):
    size = value.shape[0] // BLOCKS
    side = place % 2
    for pair in range(BLOCKS // 2):
        where = pair ^ (place // 2)
        if slot // 2 == 0:
            where = (where % 2) * 2 + where // 2
        even = value[2 * pair * size : (2 * pair + 1) * size]
        odd = value[(2 * pair + 1) * size : (2 * pair + 2) * size]

        @pl.when(side == 0)
        def _():
            keep_ref[slot // 2, where, slot % 2] = even
            send_ref[slot // 2, where, slot % 2] = odd

        @pl.when(side == 1)
        def _():
            keep_ref[slot // 2, where, slot % 2] = odd
            send_ref[slot // 2, where, slot % 2] = even


def attention_backward_kernel(kind, parts, after_ffn, *refs):
    refs = list(refs)
    place_ref = refs.pop(0)
    place, mp_at = place_ref[0], place_ref[1]
    if after_ffn:
        dc_own, *dc_rest = refs[:4]
        up_ref, r1_ref = refs[4:6]
        refs = refs[6:]
    else:
        up_ref = refs.pop(0)
    x_ref, gains_ref, a_ref = refs[:3]
    gain, later = gain_rows(kind, gains_ref)
    refs = refs[3:]
    source_ref = refs.pop(0) if kind == "cross" else None
    q_ref, kv_ref, o_ref = refs[:3]
    weights = refs[3 : 3 + parts]
    refs = refs[3 + parts :]
    rel_ref, bucket_ref = (refs.pop(0), refs.pop(0)) if kind != "cross" else (None, None)
    dx_ref, dgain_ref = refs[:2]
    refs = refs[2:]
    keep_ref, send_ref = refs.pop(0), refs.pop(0)
    later_grad = refs.pop(0) if after_ffn else None
    if kind == "encoder":
        dpre_ref = refs.pop(0)
    elif kind == "cross":
        dsource_ref = refs.pop(0)
    bias_grad = refs.pop(0) if kind != "cross" else None
    held, sems, left, right = refs[:4]
    refs = refs[4:]
    ds_sum = refs.pop(0) if kind != "cross" else None
    weight_grad = refs.pop(0)

    copies = fetch_weights(weights, int(kind == "cross"), held, sems, place, mp_at, ("merge", "rest"))
    d_out = up_ref[...].astype(f32)
    if after_ffn:
        dn = dc_own[...]
        for part in dc_rest:
            dn = dn + part[...].astype(f32)
        d_out = d_out + norm_back(dn, r1_ref[...], later, later_grad)
    g = d_out.astype(bf16)
    rows, width = g.shape
    keys = kv_ref.shape[1]
    stacked = [a_ref[...]] + ([source_ref[...]] if kind == "cross" else []) + [g]
    left[...] = jnp.concatenate(stacked, axis=0).T
    source_at = rows if kind == "cross" else 0
    g_at = left.shape[1] - rows
    right[...] = jnp.zeros(right.shape, bf16)
    same, before = masks(kind, rows, keys)
    grads = []
    for slot in range(4):
        wait_all(copies["merge", slot])
        grads.append(nt(g, slot_rows(held, slot, 3, 4)).astype(bf16))
        right[slot, g_at:, 576:768] = o_ref[slot]
    chances = []
    for slot in range(4):
        scores = nt(stack_heads(q_ref[slot]), kv_ref[slot][:, :192])
        chances.append(softmax_rows(add_bias(kind, scores, rel_ref, slot, same, before)))
    d_scores = []
    for slot in range(4):
        p = chances[slot]
        do_heads = stack_heads(grads[slot])
        dv = tn(p.astype(bf16), do_heads).astype(bf16)
        right[slot, source_at : source_at + keys, 384:576] = dv
        dp = nt(do_heads, kv_ref[slot][:, 192:])
        ds = (p * (dp - jnp.sum(dp * p, axis=-1, keepdims=True))).astype(bf16)
        d_scores.append(ds)
    for slot in range(4):
        ds = d_scores[slot]
        right[slot, 0:rows, 0:192] = join_heads(nn(ds, kv_ref[slot][:, :192])).astype(bf16)
        right[slot, source_at : source_at + keys, 192:384] = tn(ds, stack_heads(q_ref[slot])).astype(bf16)
        if kind != "cross":
            for j in range(3):
                wide = ds[j * rows : (j + 1) * rows, :rows].astype(f32)
                ds_sum[3 * slot + j] = wide[:SEQ] + wide[SEQ:]
    for slot in range(4):
        grad = nn(left[...], right[slot]).astype(bf16)
        weight_grad[...] = grad
        store_blocks(keep_ref, send_ref, place, slot, weight_grad)
    total = None
    source_total = None
    for slot in range(4):
        wait_all(copies["rest", slot])
        if kind == "cross":
            part = nn(right[slot, 0:rows, 0:192], slot_rows(held, slot, 0, 1))
            other = nn(right[slot, rows : rows + keys, 192:576], slot_rows(held, slot, 1, 3))
            source_total = other if slot == 0 else source_total + other
        else:
            part = nn(right[slot, 0:keys, 0:576], slot_rows(held, slot, 0, 3))
        total = part if slot == 0 else total + part
    if kind == "cross":
        dsource_ref[...] = source_total
    if kind == "encoder":
        dpre_ref[...] = total[rows:].astype(bf16)
    dx_ref[...] = d_out + norm_back(total[:rows], x_ref[...].astype(f32), gain, dgain_ref)
    if kind != "cross":
        bucket = bucket_ref[...]
        heads, buckets = bias_grad.shape[:2]

        @pl.loop(0, buckets)
        def _(b):
            chosen = bucket == b
            for head in range(heads):
                part = jnp.where(chosen, ds_sum[head], 0.0)
                bias_grad[head, b] = jnp.sum(part.reshape(SEQ // 8, 8, 2 * SEQ), axis=0)


def ffn_first_kernel(c0, c1, c2, c3, g0, g1, g2, g3, widen, narrow, c_all, g_all, h_ref, du_ref, dc_own, dc_rest):
    tokens = c0.shape[0]
    for i, (c, g) in enumerate(((c0, g0), (c1, g1), (c2, g2), (c3, g3))):
        c_all[i * tokens : (i + 1) * tokens, :] = c[...]
        g_all[i * tokens : (i + 1) * tokens, :] = g[...]
    inner = 0.7978845608028654
    for n in range(widen.shape[1] // 256):
        at = slice(n * 256, (n + 1) * 256)
        u = nn(c_all[...], widen[:, at])
        u2 = u * u
        th = jnp.tanh(inner * (u + 0.044715 * u * u2))
        h_ref[:, at] = (0.5 * u * (1.0 + th)).astype(bf16)
        slope = 0.5 * (1.0 + th) + (0.5 * inner) * u * (1.0 - th * th) * (1.0 + 3 * 0.044715 * u2)
        dh = nt(g_all[...], narrow[at, :])
        du_ref[:, at] = (dh * slope).astype(bf16)
    for n in range(widen.shape[0] // 256):
        at = slice(n * 256, (n + 1) * 256)
        dc = nt(du_ref[...], widen[at, :])
        dc_own[:, at] = dc[:tokens]
        for i in range(3):
            dc_rest[i, :, at] = dc[(i + 1) * tokens : (i + 2) * tokens].astype(bf16)


def ffn_second_kernel(c_all, g_all, h_ref, du_ref, narrow, out_own, out_rest, grad_ref):
    tokens = out_own.shape[0]
    hidden = narrow.shape[0]
    for n in range(narrow.shape[1] // 256):
        at = slice(n * 256, (n + 1) * 256)
        out = nn(h_ref[...], narrow[:, at])
        out_own[:, at] = out[:tokens]
        for i in range(3):
            out_rest[i, :, at] = out[(i + 1) * tokens : (i + 2) * tokens].astype(bf16)
    grad_ref[:, :hidden] = tn(c_all[...], du_ref[...]).astype(bf16)
    grad_ref[:, hidden:] = tn(g_all[...], h_ref[...]).astype(bf16)


def finish_kernel(total_ref, got1, got2, got3, query, key, value, merge):
    total = total_ref[...]
    for got in (got1, got2, got3):
        total = total + got[...].astype(f32)
    width = query.shape[1]
    for i, out in enumerate((query, key, value)):
        out[...] = total[:, i * width : (i + 1) * width]
    merge[...] = total[:, 3 * width :].T


def finish_ffn_kernel(sums, widen, narrow):
    hidden = widen.shape[1]
    widen[...] = sums[:, :hidden].astype(f32)
    narrow[...] = sums[:, hidden:].astype(f32).T


def table_kernel(place_ref, used_ref, out_ref):
    width = out_ref.shape[2]
    rows, entries = used_ref.shape[0], out_ref.shape[0]
    number = used_ref[:, width : width + 128].astype(f32)
    entry = number[:, 0:1] * 32.0 + number[:, 1:2]
    first = (place_ref[2] * entries).astype(f32)
    column = lax.broadcasted_iota(jnp.int32, (rows, entries), 1).astype(f32) + first
    row = lax.broadcasted_iota(jnp.int32, (rows, entries), 0)
    values = used_ref[:, :width]
    for p in range(PREFIX):
        chosen = jnp.logical_and(entry == column, row % PREFIX == p)
        out_ref[:, p, :] = tn(jnp.where(chosen, 1.0, 0.0).astype(bf16), values)


def pack_kernel(place_ref, *refs):
    out = refs[7]
    out[...] = jnp.zeros(out.shape, f32)
    for i in range(2):
        raw = refs[5 + i]
        heads, buckets = raw.shape[:2]
        sums = jnp.sum(jnp.sum(raw[...], axis=2), axis=-1)
        here = lax.broadcasted_iota(jnp.int32, (heads, 128), 0)
        column = lax.broadcasted_iota(jnp.int32, (heads, 128), 1)
        target = (here + place_ref[1] * (heads // 4)) % heads + i * heads
        turn = jnp.where(column == target, 1.0, 0.0)
        out[0:buckets, :] += lax.dot_general(
            sums,
            turn,
            (((0,), (0,)), ((), ())),
            precision=lax.Precision.HIGHEST,
            preferred_element_type=f32,
        )
    for i in range(5):
        for j in range(6):
            out[32 + 6 * i + j : 33 + 6 * i + j, :] = refs[i][:, 128 * j : 128 * (j + 1)]


def call(kernel, name, operands, smem, hbm, outs, scratch, limit=28):
    specs = []
    for i in range(len(operands)):
        if i in smem:
            specs.append(pl.BlockSpec(memory_space=pltpu.SMEM))
        elif i in hbm:
            specs.append(pl.BlockSpec(memory_space=pl.ANY))
        else:
            specs.append(pl.BlockSpec(memory_space=pltpu.VMEM))
    return pl.pallas_call(
        kernel,
        out_shape=[jax.ShapeDtypeStruct(shape, kind) for shape, kind in outs],
        in_specs=specs,
        out_specs=[pl.BlockSpec(memory_space=pltpu.VMEM)] * len(outs),
        scratch_shapes=scratch,
        compiler_params=pltpu.CompilerParams(vmem_limit_bytes=limit * 1024 * 1024),
        cost_estimate=pl.CostEstimate(flops=0, bytes_accessed=1024, transcendentals=0),
        name=name,
    )(*operands)


def weight_blocks(place, groups):
    count = len(groups)
    operands = [place]
    for query, key, value, merge in groups:
        operands += [query.T, key.T, value.T, merge]
    columns, rows = operands[1].shape
    return call(
        functools.partial(blocks_kernel, count),
        "weight_blocks",
        operands,
        (0,),
        range(1, len(operands)),
        [
            ((4 * columns // BLOCKS, rows), bf16),
            ((count - 1, 4 * columns // BLOCKS, rows), bf16),
        ],
        [pltpu.SemaphoreType.DMA((count,))],
        60,
    )


def attention_forward(kind, place, x, extra, gains, rel, weights):
    rows, width = x.shape
    extra_rows = extra.shape[0] if kind == "encoder" else 0
    keys = rows + extra_rows
    operands = [place, x]
    if extra is not None:
        operands.append(extra)
    operands.append(gains)
    if rel is not None:
        operands.append(rel)
    hbm = (len(operands),) if len(weights) == 1 else ()
    operands += weights
    return call(
        functools.partial(attention_forward_kernel, kind, len(weights)),
        kind + "_forward",
        operands,
        (0,),
        hbm,
        [
            ((rows, width), f32),
            ((rows, width), bf16),
            ((keys, width), bf16),
            ((4, rows, 192), bf16),
            ((4, keys, 384), bf16),
            ((4, rows, 192), bf16),
        ],
        [pltpu.VMEM((4, BLOCKS, width // BLOCKS, width), bf16), pltpu.SemaphoreType.DMA((4, 2))],
        56 if len(weights) == 1 else 28,
    )


def attention_backward(kind, place, ffn, upstream, x, gains, stored, source, weights, rel, bucket, buckets):
    rows, width = upstream.shape
    a, q, kv, o = stored
    keys = kv.shape[1]
    operands = [place]
    if ffn is not None:
        dc_own, dc_rest, r1 = ffn
        operands += [dc_own, *dc_rest, upstream, r1]
    else:
        operands += [upstream]
    operands += [x, gains, a]
    if source is not None:
        operands.append(source)
    operands += [q, kv, o]
    hbm = (len(operands),) if len(weights) == 1 else ()
    operands += weights
    if kind != "cross":
        operands += [rel, bucket]
    block = width // BLOCKS
    outs = [
        ((rows, width), f32),
        ((1, width), f32),
    ]
    outs += [((2, 4, 2, block, width), bf16)] * 2
    if ffn is not None:
        outs.append(((1, width), f32))
    if kind == "encoder":
        outs.append(((keys - rows, width), bf16))
    elif kind == "cross":
        outs.append(((rows, width), f32))
    if kind != "cross":
        outs.append(((rel.shape[0], buckets, 8, 2 * SEQ), f32))
    depth = 2 * rows + (keys if kind == "cross" else keys - rows)
    scratch = [
        pltpu.VMEM((4, BLOCKS, block, width), bf16),
        pltpu.SemaphoreType.DMA((4, 2)),
        pltpu.VMEM((width, depth), bf16),
        pltpu.VMEM((4, depth, width), bf16),
    ]
    if kind != "cross":
        scratch.append(pltpu.VMEM((rel.shape[0], SEQ, 2 * SEQ), f32))
    scratch.append(pltpu.VMEM((width, width), bf16))
    return call(
        functools.partial(attention_backward_kernel, kind, len(weights), ffn is not None),
        kind + "_backward",
        operands,
        (0,),
        hbm,
        outs,
        scratch,
        56 if len(weights) == 1 else 28,
    )


def ffn_first(name, c_parts, g_parts, widen, narrow):
    tokens, width = c_parts[0].shape
    hidden = widen.shape[1]
    every = 4 * tokens
    return call(
        ffn_first_kernel,
        name + "_first",
        [*c_parts, *g_parts, widen, narrow],
        (),
        (),
        [
            ((every, width), bf16),
            ((every, width), bf16),
            ((every, hidden), bf16),
            ((every, hidden), bf16),
            ((tokens, width), f32),
            ((3, tokens, width), bf16),
        ],
        [],
    )


def ffn_second(name, c_all, g_all, h, du, narrow):
    every, width = c_all.shape
    hidden = h.shape[1]
    tokens = every // 4
    return call(
        ffn_second_kernel,
        name + "_second",
        [c_all, g_all, h, du, narrow],
        (),
        (),
        [((tokens, width), f32), ((3, tokens, width), bf16), ((width, 2 * hidden), bf16)],
        [],
    )


def gather_tokens(part):
    return [part] + [from_mp(part, step) for step in range(1, 4)]


def return_tokens(rest):
    return [to_mp(rest[step - 1], step) for step in range(1, 4)]


def relative_bias(bucket, table, heads_here):
    twice = jnp.concatenate([bucket, bucket], axis=1)
    onehot = (
        lax.broadcasted_iota(jnp.int32, (table.shape[0], 1), 0) == twice.reshape(1, -1)
    ).astype(f32)
    start = lax.axis_index("mp") * heads_here
    columns = jnp.concatenate([table.T, table.T], axis=0)
    ordered = lax.dynamic_slice_in_dim(columns, start, table.shape[1], 0)
    looked = jnp.dot(ordered, onehot, precision=lax.Precision.HIGHEST)
    return looked.reshape(table.shape[1], SEQ, 2 * SEQ), twice


def shards(
    encoder_input,
    encoder_upstream,
    memory_index,
    memory_table,
    encoder_bucket,
    encoder_bias,
    encoder_gain,
    encoder_query,
    encoder_key,
    encoder_value,
    encoder_merge,
    encoder_later_gain,
    encoder_widen,
    encoder_narrow,
    decoder_input,
    decoder_upstream,
    encoder_states,
    decoder_bucket,
    decoder_bias,
    decoder_gain,
    decoder_query,
    decoder_key,
    decoder_value,
    decoder_merge,
    cross_gain,
    cross_query,
    cross_key,
    cross_value,
    cross_merge,
    decoder_later_gain,
    decoder_widen,
    decoder_narrow,
):
    heads_here = encoder_query.shape[1] // DH
    width = encoder_input.shape[1]
    dp_at = lax.axis_index("dp")
    mp_at = lax.axis_index("mp")
    place = dp_at // (lax.axis_size("dp") // BLOCKS)
    place_in = jnp.stack([place, mp_at, dp_at * lax.axis_size("mp") + mp_at]).astype(jnp.int32)

    encoder_block, decoder_blocks = weight_blocks(
        place_in,
        [
            (encoder_query, encoder_key, encoder_value, encoder_merge),
            (decoder_query, decoder_key, decoder_value, decoder_merge),
            (cross_query, cross_key, cross_value, cross_merge),
        ],
    )
    encoder_others = gather_tokens(encoder_block)[1:]
    decoder_weights = (gather_blocks(decoder_blocks),)

    own_questions = memory_index.shape[0] // lax.axis_size("mp")
    entries = lax.dynamic_slice_in_dim(
        memory_index, mp_at * own_questions, own_questions, 0
    ).reshape(-1)
    prefix = jnp.take(memory_table, entries, axis=0).reshape(-1, width)
    prefix_rows = prefix.shape[0]
    prefix = jnp.pad(prefix, ((0, -prefix_rows % 64), (0, 0)))
    encoder_rel, encoder_twice = relative_bias(encoder_bucket, encoder_bias, heads_here)
    decoder_rel, decoder_twice = relative_bias(decoder_bucket, decoder_bias, heads_here)
    entry_rows = jnp.repeat(entries, PREFIX)
    numbers = jnp.stack([entry_rows // 32, entry_rows % 32], axis=1).astype(bf16)
    numbers = jnp.pad(numbers, ((0, 0), (0, 126)))
    gains = jnp.stack(
        [encoder_gain, encoder_later_gain, decoder_gain, cross_gain, decoder_later_gain]
    )
    small = (prefix, encoder_rel, encoder_twice, decoder_rel, decoder_twice, numbers, gains)
    small = after(small, encoder_block)
    prefix, encoder_rel, encoder_twice, decoder_rel, decoder_twice, numbers, gains = small

    first, second = stack_slots(after(encoder_block, small), encoder_others)
    first_got, second_got = spread_once(first, second)
    encoder_g = gather_tokens(after(encoder_upstream, encoder_others))
    pairs = after(
        (jnp.stack([first, first_got]), jnp.stack([second, second_got])), encoder_g
    )
    fars = spread_twice(*pairs)
    decoder_g = gather_tokens(after(decoder_upstream, encoder_g))
    encoder_own = after(join_places(*pairs, *fars), decoder_g)
    encoder_weights = (encoder_own, swap_cores(encoder_own))

    encoder_r1, encoder_c, *encoder_stored = attention_forward(
        "encoder", place_in, encoder_input, prefix, gains, encoder_rel, encoder_weights
    )
    encoder_c = gather_tokens(encoder_c)
    c_all, g_all, h, du, dc_own, dc_rest = ffn_first(
        "encoder_ffn", encoder_c, encoder_g, encoder_widen, encoder_narrow
    )
    encoder_dc = (dc_own, return_tokens(dc_rest))
    out_own, out_rest, grads = ffn_second("encoder_ffn", c_all, g_all, h, du, encoder_narrow)
    encoder_ffn_sums = reduce_ffn(grads)
    (
        encoder_input_grad,
        encoder_gain_grad,
        keep,
        send,
        encoder_later_grad,
        prefix_grad,
        encoder_bias_raw,
    ) = attention_backward(
        "encoder",
        after(place_in, out_own),
        (*encoder_dc, encoder_r1),
        encoder_upstream,
        encoder_input,
        gains,
        encoder_stored,
        None,
        encoder_weights,
        encoder_rel,
        encoder_twice,
        encoder_bias.shape[0],
    )
    encoder_got = swap_cores(send)
    packed = jnp.concatenate([prefix_grad[:prefix_rows], numbers], axis=1)
    used = lax.all_gather(packed, ("dp", "mp"), axis=0, tiled=True)
    encoder_halves = fold_cores(after(keep, packed), encoder_got)
    encoder_once = send_once(encoder_halves)

    self_r1, _, *self_stored = attention_forward(
        "self", after(place_in, encoder_halves), decoder_input, None, gains, decoder_rel, decoder_weights
    )
    cross_r2, decoder_c, *cross_stored = attention_forward(
        "cross", place_in, self_r1, encoder_states, gains, None, decoder_weights
    )
    decoder_c = gather_tokens(decoder_c)
    encoder_last = fold_once(after(encoder_halves, cross_r2), encoder_once)
    encoder_twice_got = send_twice(encoder_last)
    c_all, g_all, h, du, dc_own, dc_rest = ffn_first(
        "decoder_ffn",
        [after(decoder_c[0], encoder_last), *decoder_c[1:]],
        decoder_g,
        decoder_widen,
        decoder_narrow,
    )
    decoder_dc = (dc_own, return_tokens(after(dc_rest, encoder_twice_got)))
    out_own_d, out_rest_d, grads = ffn_second(
        "decoder_ffn", c_all, g_all, h, du, decoder_narrow
    )
    decoder_ffn_sums = reduce_ffn(grads)
    encoder_sums = fold_twice(
        after(encoder_halves, out_own_d), encoder_once, encoder_twice_got
    )
    encoder_widen_grad, encoder_narrow_grad = two_matrices(after(encoder_ffn_sums, encoder_sums))
    encoder_sent = send_slots(after(encoder_sums, decoder_dc))

    cross_dx, cross_gain_grad, keep, send, decoder_later_grad, states_grad = attention_backward(
        "cross",
        after(place_in, encoder_narrow_grad),
        (*decoder_dc, cross_r2),
        decoder_upstream,
        self_r1,
        gains,
        cross_stored,
        encoder_states,
        decoder_weights,
        None,
        None,
        None,
    )
    cross_got = swap_cores(after(send, encoder_sent))
    cross_halves = fold_cores(keep, cross_got)
    cross_once = send_once(cross_halves)
    encoder_out = return_tokens(after(out_rest, encoder_sent))
    decoder_input_grad, decoder_gain_grad, keep, send, decoder_bias_raw = attention_backward(
        "self",
        after(place_in, cross_halves),
        None,
        cross_dx,
        decoder_input,
        gains,
        self_stored,
        None,
        decoder_weights,
        decoder_rel,
        decoder_twice,
        decoder_bias.shape[0],
    )
    self_got = swap_cores(after(send, cross_once, encoder_out))
    cross_last = fold_once(after(cross_halves, decoder_input_grad), cross_once)
    cross_twice_got = send_twice(cross_last)
    sums = call(
        pack_kernel,
        "pack",
        [
            after(place_in, cross_last),
            encoder_gain_grad,
            encoder_later_grad,
            decoder_gain_grad,
            cross_gain_grad,
            decoder_later_grad,
            encoder_bias_raw,
            decoder_bias_raw,
        ],
        (0,),
        (),
        [((64, 128), f32)],
        [],
    )[0]
    self_halves = fold_cores(keep, after(self_got, sums))
    self_once = send_once(self_halves)
    decoder_out = return_tokens(after(out_rest_d, encoder_out))

    encoder_mats = four_matrices(after(encoder_sums, self_halves), encoder_sent)
    encoder_output = (
        after(encoder_r1, self_halves) + out_own + sum(part.astype(f32) for part in encoder_out)
    ).astype(bf16)
    sums = sum_everywhere(after(sums, self_halves))
    cross_sums = fold_twice(after(cross_halves, encoder_mats), cross_once, cross_twice_got)
    self_last = fold_once(self_halves, after(self_once, cross_sums))
    self_twice_got = send_twice(self_last)
    cross_sent = send_slots(after(cross_sums, self_last, decoder_out))

    table_rows = memory_table.shape[0] // (lax.axis_size("dp") * lax.axis_size("mp"))
    table_grad = call(
        table_kernel,
        "table",
        [after(place_in, self_last), used],
        (0,),
        (),
        [((table_rows, PREFIX, width), f32)],
        [],
    )[0]
    decoder_widen_grad, decoder_narrow_grad = two_matrices(after(decoder_ffn_sums, self_last))
    decoder_output = (
        after(cross_r2, self_last) + out_own_d + sum(part.astype(f32) for part in decoder_out)
    ).astype(bf16)
    self_sums = fold_twice(
        after(self_halves, table_grad, decoder_narrow_grad), self_once, self_twice_got
    )
    self_sent = send_slots(after(self_sums, cross_sent))
    cross_mats = four_matrices(after(cross_sums, self_sums), cross_sent)
    self_mats = four_matrices(self_sums, self_sent)

    gain_sums = [sums[32 + 6 * i : 38 + 6 * i].reshape(-1) for i in range(5)]
    buckets, heads = encoder_bias.shape
    bias_grads = [sums[:buckets, i * heads : (i + 1) * heads] for i in range(2)]
    return (
        encoder_output,
        encoder_input_grad,
        table_grad,
        bias_grads[0],
        gain_sums[0],
        *encoder_mats,
        gain_sums[1],
        encoder_widen_grad,
        encoder_narrow_grad,
        decoder_output,
        decoder_input_grad,
        states_grad,
        bias_grads[1],
        gain_sums[2],
        *self_mats,
        gain_sums[3],
        *cross_mats,
        gain_sums[4],
        decoder_widen_grad,
        decoder_narrow_grad,
    )


def solution(mesh):
    rows = P(("dp", "mp"), None)
    columns = P(None, "mp")
    lines = P("mp", None)
    attention = (columns, columns, columns, lines)
    in_specs = (
        (rows, rows, P("dp", None), P(), P(), P(), P())
        + attention
        + (P(), columns, lines, rows, rows, rows, P(), P(), P())
        + attention
        + (P(),)
        + attention
        + (P(), columns, lines)
    )
    both = P("dp", "mp")
    turned = P("mp", "dp")
    grads = (both, both, both, turned)
    out_specs = (
        (rows, rows, P(("dp", "mp"), None, None), P(), P())
        + grads
        + (P(), both, turned, rows, rows, rows, P(), P())
        + grads
        + (P(),)
        + grads
        + (P(), both, turned)
    )
    return jax.shard_map(shards, mesh=mesh, in_specs=in_specs, out_specs=out_specs, check_vma=False)
```

time: 461 us -> 407 us (0.88)
  waiting for transfers between devices: 115 us -> 147 us
  other arithmetic: 52.3 us -> 23.4 us
  Pallas kernels: 99.9 us -> 75.3 us
  local copies, waits for them, and re-layouts: 37.8 us -> 18.8 us
  starting transfers between devices: 130 us -> 116 us
    ppermute x21 -> x15, waiting for transfers between devices: 15.1 us -> 78.9 us  [from_mp(): lax.ppermute(array, 'mp', [(i, (i - step) % size) for i in range(size)])]
    ppermute x49 -> x23, waiting for transfers between devices: 78 us -> 28 us  [swap_dp(): lax.ppermute(array, 'dp', [(i, i ^ bit) for i in range(lax.axis_size('dp'...]
    pallas_call x10 -> x18, Pallas kernels: 99.9 us -> 75.3 us  [call(): pl.pallas_call(kernel, out_shape=[jax.ShapeDtypeStruct(shape, kind) for s...]
    another operation x40 -> x6, other arithmetic: 20.7 us -> 2.62 us  [the longest x2 1.01 us: shards(): jnp.stack([first, first_got])]
    ppermute x49 -> x23, starting transfers between devices: 44.7 us -> 27.8 us  [swap_dp(): lax.ppermute(array, 'dp', [(i, i ^ bit) for i in range(lax.axis_size('dp'...]
    ppermute x21, waiting for transfers between devices: 17.2 us -> 29.9 us  [to_mp(): lax.ppermute(array, 'mp', [(i, (i + step) % size) for i in range(size)])]
    dynamic_slice x7 -> x0, local copies, waits for them, and re-layouts: 9.83 us -> none  [the longest x5 7.03 us: weight_block(): lax.dynamic_slice_in_dim(w, start, size, 0)]
    all_gather x1, waiting for transfers between devices: 0.01 us -> 6.26 us  [shards(): used = lax.all_gather(packed, ('dp', 'mp'), axis=0, tiled=True)]
  transfers between devices with their start and end apart: 94 -> 65, of which waited for: 31 -> 27; matrix products, arithmetic and copies ran while one was open for 18% -> 8% of each run, Pallas kernels for 22% -> 18%
where the time goes in v2:
time: 407 us; the launch traced here: 399 us
  waiting for transfers between devices  147 us (36%)
  starting transfers between devices  116 us (29%)
  Pallas kernels  75.3 us (19%)
  other arithmetic  23.4 us (6%)
  local copies, waits for them, and re-layouts  18.8 us (5%)
  between operations  17.2 us (4%)
    ppermute x15, waiting for transfers between devices, from_mp(): lax.ppermute(array, 'mp', [(i, (i - step) % size) for i in range(size)])  78.9 us
    pallas_call x18, Pallas kernels, call(): pl.pallas_call(kernel, out_shape=[jax.ShapeDtypeStruct(shape, kind) for s...  75.3 us
    ppermute x15, starting transfers between devices, from_mp(): lax.ppermute(array, 'mp', [(i, (i - step) % size) for i in range(size)])  43.5 us
    ppermute x21, starting transfers between devices, to_mp(): lax.ppermute(array, 'mp', [(i, (i + step) % size) for i in range(size)])  41.2 us
    ppermute x21, waiting for transfers between devices, to_mp(): lax.ppermute(array, 'mp', [(i, (i + step) % size) for i in range(size)])  29.9 us
    ppermute x23, waiting for transfers between devices, swap_dp(): lax.ppermute(array, 'dp', [(i, i ^ bit) for i in range(lax.axis_size('dp'...  28 us
    ppermute x23, starting transfers between devices, swap_dp(): lax.ppermute(array, 'dp', [(i, i ^ bit) for i in range(lax.axis_size('dp'...  27.8 us
    convert_element_type x9, other arithmetic, rounded_sum(): return (left.astype(f32) + right.astype(f32)).astype(bf16)  12.8 us
  transfers between devices with their start and end apart: 65, of which 27 were waited for; matrix products, arithmetic and copies ran while one was open for 8% of the time, Pallas kernels for 18%

profile of v2, /device:TPU:0, one launch (start us, length us, event | category | flops | bytes accessed | tf_op | source)
XLA Modules:
  0.0 399.0 jit_solution(2206213445709300939)
XLA Ops:
  8.7 2.6 weight_blocks.1
  11.4 5.1 %collective-permute-start = (bf16[96,768]{1,0:T(8,128)(2,1)}, bf16[96,768]{1,0:T(8,128)(2,1)}, u32[]{:S(2)}, u32[]{:S(2)}) collective-permute-start(bf16[96,768]{1,0:T(8,128)(2,1)} %get-tuple-element.163), channel_id=1, source_target_pairs={{0,3},{1,0},{2,1},{3,2},{4,7},{5,4},{6,5},{7,6},{8,11},{9,8},{10,9... | collective-permute-start | bytes 442376 | tf_op jit(solution)/shard_map/ppermute | solution.py:35
  25.8 5.7 %collective-permute-done.2 = bf16[96,768]{1,0:T(8,128)(2,1)S(1)} collective-permute-done((bf16[96,768]{1,0:T(8,128)(2,1)}, bf16[96,768]{1,0:T(8,128)(2,1)S(1)}, u32[]{:S(2)}, u32[]{:S(2)}) %collective-permute-start.2) | collective-permute-done | bytes 147488 | tf_op jit(solution)/shard_map/ppermute | solution.py:35
  35.4 12.1 %collective-permute-start.6 = (bf16[128,768]{1,0:T(8,128)(2,1)S(1)}, bf16[128,768]{1,0:T(8,128)(2,1)S(1)}, u32[]{:S(2)}, u32[]{:S(2)}) collective-permute-start(bf16[128,768]{1,0:T(8,128)(2,1)S(1)} %copy-done.13), channel_id=1, source_target_pairs={{0,2},{1,3},{2,0},{3,1},{4,6},{5,7},{6,4},{7,5},{8,10},{9,11},{10,... | collective-permute-start | bytes 589832 | tf_op jit(solution)/shard_map/ppermute | solution.py:35
  49.7 12.9 %collective-permute-done.6.g2 = bf16[128,768]{1,0:T(8,128)(2,1)S(1)} collective-permute-done((bf16[128,768]{1,0:T(8,128)(2,1)S(1)}, bf16[128,768]{1,0:T(8,128)(2,1)S(1)}, u32[]{:S(2)}, u32[]{:S(2)}) %collective-permute-start.6) | collective-permute-done | bytes 196640 | tf_op jit(solution)/shard_map/ppermute | solution.py:35
  62.6 5.6 %collective-permute-done.7.g3 = bf16[128,768]{1,0:T(8,128)(2,1)S(1)} collective-permute-done((bf16[128,768]{1,0:T(8,128)(2,1)S(1)}, bf16[128,768]{1,0:T(8,128)(2,1)S(1)}, u32[]{:S(2)}, u32[]{:S(2)}) %collective-permute-start.7) | collective-permute-done | bytes 196640 | tf_op jit(solution)/shard_map/ppermute | solution.py:35
  68.2 5.8 %collective-permute-start.9 = (bf16[2,2,96,768]{3,2,1,0:T(8,128)(2,1)S(1)}, bf16[2,2,96,768]{3,2,1,0:T(8,128)(2,1)S(1)}, u32[]{:S(2)}, u32[]{:S(2)}) collective-permute-start(bf16[2,2,96,768]{3,2,1,0:T(8,128)(2,1)S(1)} %pad_maximum_fusion.1), channel_id=1, source_target_pairs={{0,8},{4,12},{8,0},{12,4},{16,24},{20,28},{24,16},{28,20},{1,9},{5... | collective-permute-start | bytes 1769480 | tf_op jit(solution)/shard_map/ppermute | solution.py:48
  74.7 8.6 %collective-permute-start.11 = (bf16[128,768]{1,0:T(8,128)(2,1)S(1)}, bf16[128,768]{1,0:T(8,128)(2,1)S(1)}, u32[]{:S(2)}, u32[]{:S(2)}) collective-permute-start(bf16[128,768]{1,0:T(8,128)(2,1)S(1)} %copy-done.14), channel_id=1, source_target_pairs={{0,2},{1,3},{2,0},{3,1},{4,6},{5,7},{6,4},{7,5},{8,10},{9,11},{10,... | collective-permute-start | bytes 589832 | tf_op jit(solution)/shard_map/ppermute | solution.py:35
  85.7 4.4 %collective-permute-done.10.g1 = bf16[128,768]{1,0:T(8,128)(2,1)S(1)} collective-permute-done((bf16[128,768]{1,0:T(8,128)(2,1)S(1)}, bf16[128,768]{1,0:T(8,128)(2,1)S(1)}, u32[]{:S(2)}, u32[]{:S(2)}) %collective-permute-start.10) | collective-permute-done | bytes 196640 | tf_op jit(solution)/shard_map/ppermute | solution.py:35
  90.1 21.7 %collective-permute-done.11.g2 = bf16[128,768]{1,0:T(8,128)(2,1)S(1)} collective-permute-done((bf16[128,768]{1,0:T(8,128)(2,1)S(1)}, bf16[128,768]{1,0:T(8,128)(2,1)S(1)}, u32[]{:S(2)}, u32[]{:S(2)}) %collective-permute-start.11) | collective-permute-done | bytes 196640 | tf_op jit(solution)/shard_map/ppermute | solution.py:35
  111.9 4.5 %collective-permute-done.13.refs_6_.refs_14_ = bf16[4,4,96,768]{3,2,1,0:T(8,128)(2,1)S(1)} collective-permute-done((bf16[4,4,96,768]{3,2,1,0:T(8,128)(2,1)S(1)}, bf16[4,4,96,768]{3,2,1,0:T(8,128)(2,1)S(1)}, u32[]{:S(2)}, u32[]{:S(2)}) %collective-permute-start.13) | collective-permute-done | bytes 2359328 | tf_op jit(solution)/shard_map/ppermute | solution.py:48
  116.5 3.3 encoder_forward.1
  121.9 6.0 %collective-permute-done.14.c1 = bf16[128,768]{1,0:T(8,128)(2,1)S(1)} collective-permute-done((bf16[128,768]{1,0:T(8,128)(2,1)S(1)}, bf16[128,768]{1,0:T(8,128)(2,1)S(1)}, u32[]{:S(2)}, u32[]{:S(2)}) %collective-permute-start.14) | collective-permute-done | bytes 196640 | tf_op jit(solution)/shard_map/ppermute | solution.py:35
  127.9 8.4 %collective-permute-done.15.c2 = bf16[128,768]{1,0:T(8,128)(2,1)S(1)} collective-permute-done((bf16[128,768]{1,0:T(8,128)(2,1)S(1)}, bf16[128,768]{1,0:T(8,128)(2,1)S(1)}, u32[]{:S(2)}, u32[]{:S(2)}) %collective-permute-start.15) | collective-permute-done | bytes 196640 | tf_op jit(solution)/shard_map/ppermute | solution.py:35
  138.7 2.5 collective-permute-start.17
  143.1 3.3 collective-permute-start.19
  148.5 6.7 %collective-permute-done.18.refs_3_ = bf16[128,768]{1,0:T(8,128)(2,1)S(1)} collective-permute-done((bf16[128,768]{1,0:T(8,128)(2,1)S(1)}, bf16[128,768]{1,0:T(8,128)(2,1)S(1)}, u32[]{:S(2)}, u32[]{:S(2)}) %collective-permute-start.18) | collective-permute-done | bytes 196640 | tf_op jit(solution)/shard_map/ppermute | solution.py:40
  155.2 11.6 %encoder_backward.1 = (f32[128,768]{1,0:T(8,128)}, f32[1,768]{1,0:T(1,128)S(1)}, bf16[2,4,2,96,768]{4,3,2,1,0:T(8,128)(2,1)S(1)}, bf16[2,4,2,96,768]{4,3,2,1,0:T...) custom-call(s32[3]{0:T(128)S(1)} %copy-done.36, ...), custom_call_target="tpu_custom_call" | custom-call | bytes 1024 | tf_op jit(solution)/shard_map/encoder_backward/pallas_call | solution.py:607
  169.5 3.5 collective-permute-done.20
  173.0 3.4 fusion.5
  176.4 5.1 %collective-permute-start.22 = (bf16[2,2,96,768]{3,2,1,0:T(8,128)(2,1)}, bf16[2,2,96,768]{3,2,1,0:T(8,128)(2,1)S(1)}, u32[]{:S(2)}, u32[]{:S(2)}) collective-permute-start(bf16[2,2,96,768]{3,2,1,0:T(8,128)(2,1)} %get-tuple-element.376), channel_id=1, source_target_pairs={{0,16},{4,20},{8,24},{12,28},{16,0},{20,4},{24,8},{28,12},{1,17},{... | collective-permute-start | bytes 1769480 | tf_op jit(solution)/shard_map/ppermute | solution.py:48
  181.5 7.0 %self_forward.1 = (f32[128,768]{1,0:T(8,128)}, bf16[128,768]{1,0:T(8,128)(2,1)}, bf16[128,768]{1,0:T(8,128)(2,1)}, bf16[4,128,192]{2,1,0:T(8,128)(2,1)}, bf16[4,...) custom-call(s32[3]{0:T(128)} %pad_add_fusion.2.place_ref.refs_0_, bf16[128,768]{1,0:T(8,128)(2,1)} %refs_2_.3, ...), custom_call_target="tpu_custom_call" | custom-call | bytes 1024 | tf_op jit(solution)/shard_map/self_forward/pallas_call | solution.py:607
  188.6 6.5 %cross_forward.1 = (f32[128,768]{1,0:T(8,128)}, bf16[128,768]{1,0:T(8,128)(2,1)}, bf16[128,768]{1,0:T(8,128)(2,1)}, bf16[4,128,192]{2,1,0:T(8,128)(2,1)}, bf16[4...) custom-call(s32[3]{0:T(128)} %pad_add_fusion.2.place_ref.refs_0_, f32[128,768]{1,0:T(8,128)} %get-tuple-element.190.refs_1_.refs_7_, ...), custom_call_target="tpu_custom_call" | custom-call | bytes 1024 | tf_op jit(solution)/shard_map/cross_forward/pallas_call | solution.py:607
  197.5 8.0 %collective-permute-start.23 = (bf16[128,768]{1,0:T(8,128)(2,1)}, bf16[128,768]{1,0:T(8,128)(2,1)S(1)}, u32[]{:S(2)}, u32[]{:S(2)}) collective-permute-start(bf16[128,768]{1,0:T(8,128)(2,1)} %get-tuple-element.195.c0), channel_id=1, source_target_pairs={{0,3},{1,0},{2,1},{3,2},{4,7},{5,4},{6,5},{7,6},{8,11},{9,8},{10,9... | collective-permute-start | bytes 589832 | tf_op jit(solution)/shard_map/ppermute | solution.py:35
  206.2 5.0 %collective-permute-done.23.c1 = bf16[128,768]{1,0:T(8,128)(2,1)S(1)} collective-permute-done((bf16[128,768]{1,0:T(8,128)(2,1)}, bf16[128,768]{1,0:T(8,128)(2,1)S(1)}, u32[]{:S(2)}, u32[]{:S(2)}) %collective-permute-start.23) | collective-permute-done | bytes 196640 | tf_op jit(solution)/shard_map/ppermute | solution.py:35
  211.2 9.1 %collective-permute-done.24.c2 = bf16[128,768]{1,0:T(8,128)(2,1)S(1)} collective-permute-done((bf16[128,768]{1,0:T(8,128)(2,1)}, bf16[128,768]{1,0:T(8,128)(2,1)S(1)}, u32[]{:S(2)}, u32[]{:S(2)}) %collective-permute-start.24) | collective-permute-done | bytes 196640 | tf_op jit(solution)/shard_map/ppermute | solution.py:35
  223.6 3.5 decoder_ffn_second.1
  228.9 2.8 collective-permute-start.30
  232.1 4.8 %collective-permute-done.28.refs_2_ = bf16[128,768]{1,0:T(8,128)(2,1)S(1)} collective-permute-done((bf16[128,768]{1,0:T(8,128)(2,1)S(1)}, bf16[128,768]{1,0:T(8,128)(2,1)S(1)}, u32[]{:S(2)}, u32[]{:S(2)}) %collective-permute-start.28) | collective-permute-done | bytes 196640 | tf_op jit(solution)/shard_map/ppermute | solution.py:40
  236.8 5.0 %collective-permute-done.29.refs_3_ = bf16[128,768]{1,0:T(8,128)(2,1)S(1)} collective-permute-done((bf16[128,768]{1,0:T(8,128)(2,1)S(1)}, bf16[128,768]{1,0:T(8,128)(2,1)S(1)}, u32[]{:S(2)}, u32[]{:S(2)}) %collective-permute-start.29) | collective-permute-done | bytes 196640 | tf_op jit(solution)/shard_map/ppermute | solution.py:40
  241.9 4.7 %collective-permute-start.31 = (bf16[96,768]{1,0:T(8,128)(2,1)S(1)}, bf16[96,768]{1,0:T(8,128)(2,1)S(1)}, u32[]{:S(2)}, u32[]{:S(2)}) collective-permute-start(bf16[96,768]{1,0:T(8,128)(2,1)S(1)} %slice_bitcast_fusion.12), channel_id=1, source_target_pairs={{0,1},{1,2},{2,3},{3,0},{4,5},{5,6},{6,7},{7,4},{8,9},{9,10},{10,1... | collective-permute-start | bytes 442376 | tf_op jit(solution)/shard_map/ppermute | solution.py:40
  246.5 2.4 collective-permute-start.32
  251.1 12.9 %cross_backward.1 = (f32[128,768]{1,0:T(8,128)}, f32[1,768]{1,0:T(1,128)}, bf16[2,4,2,96,768]{4,3,2,1,0:T(8,128)(2,1)}, bf16[2,4,2,96,768]{4,3,2,1,0:T(8,128)(2,...) custom-call(s32[3]{0:T(128)} %pad_add_fusion.2.place_ref.refs_0_, f32[128,768]{1,0:T(8,128)} %copy-done.20, ...), custom_call_target="tpu_custom_call" | custom-call | bytes 1024 | tf_op jit(solution)/shard_map/cross_backward/pallas_call | solution.py:607
  264.7 4.3 %collective-permute-done.34 = bf16[2,4,2,96,768]{4,3,2,1,0:T(8,128)(2,1)} collective-permute-done((bf16[2,4,2,96,768]{4,3,2,1,0:T(8,128)(2,1)}, bf16[2,4,2,96,768]{4,3,2,1,0:T(8,128)(2,1)}, u32[]{:S(2)}, u32[]{:S(2)}) %collective-permute-start.34) | collective-permute-done | bytes 2359328 | tf_op jit(solution)/shard_map/ppermute | solution.py:48
  269.0 4.4 %fusion.9 = (bf16[2,2,96,768]{3,2,1,0:T(8,128)(2,1)S(1)}, bf16[2,2,96,768]{3,2,1,0:T(8,128)(2,1)}, bf16[2,2,96,768]{3,2,1,0:T(8,128)(2,1)S(1)}, bf16[2,2,96,768]{3,2,1,0:T(8,128)(2,1)}) fusion(bf16[2,4,2,96,768]{4,3,2,1,0:T(8,128)(2,1)} %collective-permute-done.34, bf16[2,4,2,96,768]{4,3,2,1,0:T(8,128)(2,1)} %get-tuple-element.213), kind=kLoop, calls=%fused_computation.25 | loop fusion | flops 4718592 | bytes 7077888 | tf_op jit(solution)/shard_map/convert_element_type | solution.py:63
  277.7 2.8 collective-permute-start.39
  280.5 13.2 %self_backward.1 = (f32[128,768]{1,0:T(8,128)}, f32[1,768]{1,0:T(1,128)}, bf16[2,4,2,96,768]{4,3,2,1,0:T(8,128)(2,1)}, bf16[2,4,2,96,768]{4,3,2,1,0:T(8,128)(2,1)}, f32[12,32,8,128]{3,2,1,0:T(8,128)}) custom-call(s32[3]{0:T(128)} %pad_add_fusion.2.place_ref.refs_0_, f32[128,768]{1,0:T(8,128)} %get-tuple-element.220.refs_1_, bf16[128,768]{1,0:T(8,128)(2,1)} %refs_2_.3, ...), custom_call_target="tpu_custom_call" | custom-call | bytes 1024 | tf_op jit(solution)/shard_map/self_backward/pallas_call | solution.py:607
  297.3 2.6 collective-permute-start.50
  306.8 2.4 fusion.11
  318.0 10.2 %collective-permute-done.46 = f32[64,128]{1,0:T(8,128)S(1)} collective-permute-done((f32[64,128]{1,0:T(8,128)S(1)}, f32[64,128]{1,0:T(8,128)S(1)}, u32[]{:S(2)}, u32[]{:S(2)}) %collective-permute-start.46) | collective-permute-done | bytes 32800 | tf_op jit(solution)/shard_map/ppermute | solution.py:48
  329.7 2.4 collective-permute-done.47
  341.0 3.3 collective-permute-start.52
  352.0 6.3 %all-gather.4.cloned.1.call-done.used_ref = bf16[1280,896]{1,0:T(8,128)(2,1)} async-done(((bf16[40,896]{1,0:T(8,128)(2,1)}), bf16[1280,896]{1,0:T(8,128)(2,1)}) %all-gather.4.cloned.1.call-update) | async-done | bytes 2293776 | tf_op jit(solution)/shard_map/all_gather | solution.py:898
  359.9 2.5 table.1
  368.7 2.6 collective-permute-done.55.got1
  371.3 5.6 %collective-permute-done.56.got2 = bf16[96,768]{1,0:T(8,128)(2,1)S(1)} collective-permute-done((bf16[96,768]{1,0:T(8,128)(2,1)}, bf16[96,768]{1,0:T(8,128)(2,1)S(1)}, u32[]{:S(2)}, u32[]{:S(2)}) %collective-permute-start.56) | collective-permute-done | bytes 147488 | tf_op jit(solution)/shard_map/ppermute | solution.py:40
  376.9 3.2 collective-permute-start.58
  385.2 5.1 %collective-permute-done.59.got2 = bf16[96,768]{1,0:T(8,128)(2,1)S(1)} collective-permute-done((bf16[96,768]{1,0:T(8,128)(2,1)S(1)}, bf16[96,768]{1,0:T(8,128)(2,1)S(1)}, u32[]{:S(2)}, u32[]{:S(2)}) %collective-permute-start.59) | collective-permute-done | bytes 147488 | tf_op jit(solution)/shard_map/ppermute | solution.py:40
  (340 shorter events, 96.0 us)
Async XLA Ops:
  8.1 173.5 %all-gather.6.cloned.1.call-start = ((), (), s32[]{:S(2)}) async-start(), calls=%async_computation.5 | async-start | bytes 9732096 | tf_op jit(solution)/shard_map/all_gather | solution.py:181
  11.4 237.9 %reduce-scatter.3.cloned.1.call-start = ((), (), s32[]{:S(2)}) async-start(), calls=%async_computation.2 | async-start | bytes 2654208 | tf_op jit(solution)/shard_map/reduce_scatter | solution.py:159
  11.4 11.8 %collective-permute-start = (bf16[96,768]{1,0:T(8,128)(2,1)}, bf16[96,768]{1,0:T(8,128)(2,1)}, u32[]{:S(2)}, u32[]{:S(2)}) collective-permute-start(bf16[96,768]{1,0:T(8,128)(2,1)} %get-tuple-element.163), channel_id=1, source_target_pairs={{0,3},{1,0},{2,1},{3,2},{4,7},{5,4},{6,5},{7,6},{8,11},{9,8},{10,9... | collective-permute-start | bytes 442376 | tf_op jit(solution)/shard_map/ppermute | solution.py:35
  16.5 15.0 %collective-permute-start.2 = (bf16[96,768]{1,0:T(8,128)(2,1)}, bf16[96,768]{1,0:T(8,128)(2,1)S(1)}, u32[]{:S(2)}, u32[]{:S(2)}) collective-permute-start(bf16[96,768]{1,0:T(8,128)(2,1)} %get-tuple-element.163), channel_id=1, source_target_pairs={{0,2},{1,3},{2,0},{3,1},{4,6},{5,7},{6,4},{7,5},{8,10},{9,11},{10,... | collective-permute-start | bytes 442376 | tf_op jit(solution)/shard_map/ppermute | solution.py:35
  16.5 15.0 %collective-permute-start.3 = (bf16[96,768]{1,0:T(8,128)(2,1)}, bf16[96,768]{1,0:T(8,128)(2,1)}, u32[]{:S(2)}, u32[]{:S(2)}) collective-permute-start(bf16[96,768]{1,0:T(8,128)(2,1)} %get-tuple-element.163), channel_id=1, source_target_pairs={{0,1},{1,2},{2,3},{3,0},{4,5},{5,6},{6,7},{7,4},{8,9},{9,10},{10,1... | collective-permute-start | bytes 442376 | tf_op jit(solution)/shard_map/ppermute | solution.py:35
  24.2 25.3 %collective-permute-start.1 = (bf16[2,96,768]{2,1,0:T(8,128)(2,1)S(1)}, bf16[2,96,768]{2,1,0:T(8,128)(2,1)S(1)}, u32[]{:S(2)}, u32[]{:S(2)}) collective-permute-start(bf16[2,96,768]{2,1,0:T(8,128)(2,1)S(1)} %get-tuple-element.405), channel_id=1, source_target_pairs={{0,8},{4,12},{8,0},{12,4},{16,24},{20,28},{24,16},{28,20},{1,9},{5... | collective-permute-start | bytes 884744 | tf_op jit(solution)/shard_map/ppermute | solution.py:48
  32.5 17.1 %collective-permute-start.4 = (bf16[2,96,768]{2,1,0:T(8,128)(2,1)S(1)}, bf16[2,96,768]{2,1,0:T(8,128)(2,1)S(1)}, u32[]{:S(2)}, u32[]{:S(2)}) collective-permute-start(bf16[2,96,768]{2,1,0:T(8,128)(2,1)S(1)} %get-tuple-element.403), channel_id=1, source_target_pairs={{0,16},{4,20},{8,24},{12,28},{16,0},{20,4},{24,8},{28,12},{1,17},{... | collective-permute-start | bytes 884744 | tf_op jit(solution)/shard_map/ppermute | solution.py:48
  34.2 15.5 %collective-permute-start.5 = (bf16[128,768]{1,0:T(8,128)(2,1)S(1)}, bf16[128,768]{1,0:T(8,128)(2,1)S(1)}, u32[]{:S(2)}, u32[]{:S(2)}) collective-permute-start(bf16[128,768]{1,0:T(8,128)(2,1)S(1)} %copy-done.13), channel_id=1, source_target_pairs={{0,3},{1,0},{2,1},{3,2},{4,7},{5,4},{6,5},{7,6},{8,11},{9,8},{10,9... | collective-permute-start | bytes 589832 | tf_op jit(solution)/shard_map/ppermute | solution.py:35
  35.4 27.2 %collective-permute-start.6 = (bf16[128,768]{1,0:T(8,128)(2,1)S(1)}, bf16[128,768]{1,0:T(8,128)(2,1)S(1)}, u32[]{:S(2)}, u32[]{:S(2)}) collective-permute-start(bf16[128,768]{1,0:T(8,128)(2,1)S(1)} %copy-done.13), channel_id=1, source_target_pairs={{0,2},{1,3},{2,0},{3,1},{4,6},{5,7},{6,4},{7,5},{8,10},{9,11},{10,... | collective-permute-start | bytes 589832 | tf_op jit(solution)/shard_map/ppermute | solution.py:35
  47.5 20.7 %collective-permute-start.7 = (bf16[128,768]{1,0:T(8,128)(2,1)S(1)}, bf16[128,768]{1,0:T(8,128)(2,1)S(1)}, u32[]{:S(2)}, u32[]{:S(2)}) collective-permute-start(bf16[128,768]{1,0:T(8,128)(2,1)S(1)} %copy-done.13), channel_id=1, source_target_pairs={{0,1},{1,2},{2,3},{3,0},{4,5},{5,6},{6,7},{7,4},{8,9},{9,10},{10,1... | collective-permute-start | bytes 589832 | tf_op jit(solution)/shard_map/ppermute | solution.py:35
  68.2 17.1 %collective-permute-start.9 = (bf16[2,2,96,768]{3,2,1,0:T(8,128)(2,1)S(1)}, bf16[2,2,96,768]{3,2,1,0:T(8,128)(2,1)S(1)}, u32[]{:S(2)}, u32[]{:S(2)}) collective-permute-start(bf16[2,2,96,768]{3,2,1,0:T(8,128)(2,1)S(1)} %pad_maximum_fusion.1), channel_id=1, source_target_pairs={{0,8},{4,12},{8,0},{12,4},{16,24},{20,28},{24,16},{28,20},{1,9},{5... | collective-permute-start | bytes 1769480 | tf_op jit(solution)/shard_map/ppermute | solution.py:48
  74.0 16.1 %collective-permute-start.10 = (bf16[128,768]{1,0:T(8,128)(2,1)S(1)}, bf16[128,768]{1,0:T(8,128)(2,1)S(1)}, u32[]{:S(2)}, u32[]{:S(2)}) collective-permute-start(bf16[128,768]{1,0:T(8,128)(2,1)S(1)} %copy-done.14), channel_id=1, source_target_pairs={{0,3},{1,0},{2,1},{3,2},{4,7},{5,4},{6,5},{7,6},{8,11},{9,8},{10,9... | collective-permute-start | bytes 589832 | tf_op jit(solution)/shard_map/ppermute | solution.py:35
  74.7 37.1 %collective-permute-start.11 = (bf16[128,768]{1,0:T(8,128)(2,1)S(1)}, bf16[128,768]{1,0:T(8,128)(2,1)S(1)}, u32[]{:S(2)}, u32[]{:S(2)}) collective-permute-start(bf16[128,768]{1,0:T(8,128)(2,1)S(1)} %copy-done.14), channel_id=1, source_target_pairs={{0,2},{1,3},{2,0},{3,1},{4,6},{5,7},{6,4},{7,5},{8,10},{9,11},{10,... | collective-permute-start | bytes 589832 | tf_op jit(solution)/shard_map/ppermute | solution.py:35
  83.3 28.6 %collective-permute-start.12 = (bf16[128,768]{1,0:T(8,128)(2,1)S(1)}, bf16[128,768]{1,0:T(8,128)(2,1)S(1)}, u32[]{:S(2)}, u32[]{:S(2)}) collective-permute-start(bf16[128,768]{1,0:T(8,128)(2,1)S(1)} %copy-done.14), channel_id=1, source_target_pairs={{0,1},{1,2},{2,3},{3,0},{4,5},{5,6},{6,7},{7,4},{8,9},{9,10},{10,1... | collective-permute-start | bytes 589832 | tf_op jit(solution)/shard_map/ppermute | solution.py:35
  119.9 16.4 %collective-permute-start.15 = (bf16[128,768]{1,0:T(8,128)(2,1)S(1)}, bf16[128,768]{1,0:T(8,128)(2,1)S(1)}, u32[]{:S(2)}, u32[]{:S(2)}) collective-permute-start(bf16[128,768]{1,0:T(8,128)(2,1)S(1)} %get-tuple-element.170.c0), channel_id=1, source_target_pairs={{0,2},{1,3},{2,0},{3,1},{4,6},{5,7},{6,4},{7,5},{8,10},{9,11},{10,... | collective-permute-start | bytes 589832 | tf_op jit(solution)/shard_map/ppermute | solution.py:35
  120.0 16.4 %collective-permute-start.16 = (bf16[128,768]{1,0:T(8,128)(2,1)S(1)}, bf16[128,768]{1,0:T(8,128)(2,1)S(1)}, u32[]{:S(2)}, u32[]{:S(2)}) collective-permute-start(bf16[128,768]{1,0:T(8,128)(2,1)S(1)} %get-tuple-element.170.c0), channel_id=1, source_target_pairs={{0,1},{1,2},{2,3},{3,0},{4,5},{5,6},{6,7},{7,4},{8,9},{9,10},{10,1... | collective-permute-start | bytes 589832 | tf_op jit(solution)/shard_map/ppermute | solution.py:35
  141.2 14.1 %collective-permute-start.18 = (bf16[128,768]{1,0:T(8,128)(2,1)S(1)}, bf16[128,768]{1,0:T(8,128)(2,1)S(1)}, u32[]{:S(2)}, u32[]{:S(2)}) collective-permute-start(bf16[128,768]{1,0:T(8,128)(2,1)S(1)} %get-tuple-element.390), channel_id=1, source_target_pairs={{0,2},{1,3},{2,0},{3,1},{4,6},{5,7},{6,4},{7,5},{8,10},{9,11},{10,... | collective-permute-start | bytes 589832 | tf_op jit(solution)/shard_map/ppermute | solution.py:40
  143.1 12.1 %collective-permute-start.19 = (bf16[128,768]{1,0:T(8,128)(2,1)S(1)}, bf16[128,768]{1,0:T(8,128)(2,1)S(1)}, u32[]{:S(2)}, u32[]{:S(2)}) collective-permute-start(bf16[128,768]{1,0:T(8,128)(2,1)S(1)} %get-tuple-element.389), channel_id=1, source_target_pairs={{0,3},{1,0},{2,1},{3,2},{4,7},{5,4},{6,5},{7,6},{8,11},{9,8},{10,9... | collective-permute-start | bytes 589832 | tf_op jit(solution)/shard_map/ppermute | solution.py:40
  168.2 181.2 %reduce-scatter.5.cloned.1.call-start = ((), (), s32[]{:S(2)}) async-start(), calls=%async_computation.4 | async-start | bytes 2654208 | tf_op jit(solution)/shard_map/reduce_scatter | solution.py:159
  176.4 19.0 %collective-permute-start.22 = (bf16[2,2,96,768]{3,2,1,0:T(8,128)(2,1)}, bf16[2,2,96,768]{3,2,1,0:T(8,128)(2,1)S(1)}, u32[]{:S(2)}, u32[]{:S(2)}) collective-permute-start(bf16[2,2,96,768]{3,2,1,0:T(8,128)(2,1)} %get-tuple-element.376), channel_id=1, source_target_pairs={{0,16},{4,20},{8,24},{12,28},{16,0},{20,4},{24,8},{28,12},{1,17},{... | collective-permute-start | bytes 1769480 | tf_op jit(solution)/shard_map/ppermute | solution.py:48
  181.5 15.9 %collective-permute-start.21 = (bf16[2,2,96,768]{3,2,1,0:T(8,128)(2,1)}, bf16[2,2,96,768]{3,2,1,0:T(8,128)(2,1)S(1)}, u32[]{:S(2)}, u32[]{:S(2)}) collective-permute-start(bf16[2,2,96,768]{3,2,1,0:T(8,128)(2,1)} %get-tuple-element.378), channel_id=1, source_target_pairs={{0,8},{4,12},{8,0},{12,4},{16,24},{20,28},{24,16},{28,20},{1,9},{5... | collective-permute-start | bytes 1769480 | tf_op jit(solution)/shard_map/ppermute | solution.py:48
  195.4 31.6 %collective-permute-start.27 = (bf16[2,96,768]{2,1,0:T(8,128)(2,1)S(1)}, bf16[2,96,768]{2,1,0:T(8,128)(2,1)S(1)}, u32[]{:S(2)}, u32[]{:S(2)}) collective-permute-start(bf16[2,96,768]{2,1,0:T(8,128)(2,1)S(1)} %fusion.17), channel_id=1, source_target_pairs={{0,8},{4,12},{8,0},{12,4},{16,24},{20,28},{24,16},{28,20},{1,9},{5... | collective-permute-start | bytes 884744 | tf_op jit(solution)/shard_map/ppermute | solution.py:48
  197.5 29.6 %collective-permute-start.26 = (bf16[2,96,768]{2,1,0:T(8,128)(2,1)S(1)}, bf16[2,96,768]{2,1,0:T(8,128)(2,1)S(1)}, u32[]{:S(2)}, u32[]{:S(2)}) collective-permute-start(bf16[2,96,768]{2,1,0:T(8,128)(2,1)S(1)} %fusion.16), channel_id=1, source_target_pairs={{0,16},{4,20},{8,24},{12,28},{16,0},{20,4},{24,8},{28,12},{1,17},{... | collective-permute-start | bytes 884744 | tf_op jit(solution)/shard_map/ppermute | solution.py:48
  197.5 13.7 %collective-permute-start.23 = (bf16[128,768]{1,0:T(8,128)(2,1)}, bf16[128,768]{1,0:T(8,128)(2,1)S(1)}, u32[]{:S(2)}, u32[]{:S(2)}) collective-permute-start(bf16[128,768]{1,0:T(8,128)(2,1)} %get-tuple-element.195.c0), channel_id=1, source_target_pairs={{0,3},{1,0},{2,1},{3,2},{4,7},{5,4},{6,5},{7,6},{8,11},{9,8},{10,9... | collective-permute-start | bytes 589832 | tf_op jit(solution)/shard_map/ppermute | solution.py:35
  205.6 14.8 %collective-permute-start.24 = (bf16[128,768]{1,0:T(8,128)(2,1)}, bf16[128,768]{1,0:T(8,128)(2,1)S(1)}, u32[]{:S(2)}, u32[]{:S(2)}) collective-permute-start(bf16[128,768]{1,0:T(8,128)(2,1)} %get-tuple-element.195.c0), channel_id=1, source_target_pairs={{0,2},{1,3},{2,0},{3,1},{4,6},{5,7},{6,4},{7,5},{8,10},{9,11},{10,... | collective-permute-start | bytes 589832 | tf_op jit(solution)/shard_map/ppermute | solution.py:35
  206.1 14.2 %collective-permute-start.25 = (bf16[128,768]{1,0:T(8,128)(2,1)}, bf16[128,768]{1,0:T(8,128)(2,1)S(1)}, u32[]{:S(2)}, u32[]{:S(2)}) collective-permute-start(bf16[128,768]{1,0:T(8,128)(2,1)} %get-tuple-element.195.c0), channel_id=1, source_target_pairs={{0,1},{1,2},{2,3},{3,0},{4,5},{5,6},{6,7},{7,4},{8,9},{9,10},{10,1... | collective-permute-start | bytes 589832 | tf_op jit(solution)/shard_map/ppermute | solution.py:35
  227.2 14.7 %collective-permute-start.29 = (bf16[128,768]{1,0:T(8,128)(2,1)S(1)}, bf16[128,768]{1,0:T(8,128)(2,1)S(1)}, u32[]{:S(2)}, u32[]{:S(2)}) collective-permute-start(bf16[128,768]{1,0:T(8,128)(2,1)S(1)} %get-tuple-element.387), channel_id=1, source_target_pairs={{0,2},{1,3},{2,0},{3,1},{4,6},{5,7},{6,4},{7,5},{8,10},{9,11},{10,... | collective-permute-start | bytes 589832 | tf_op jit(solution)/shard_map/ppermute | solution.py:40
  228.9 12.9 %collective-permute-start.30 = (bf16[128,768]{1,0:T(8,128)(2,1)S(1)}, bf16[128,768]{1,0:T(8,128)(2,1)S(1)}, u32[]{:S(2)}, u32[]{:S(2)}) collective-permute-start(bf16[128,768]{1,0:T(8,128)(2,1)S(1)} %get-tuple-element.386), channel_id=1, source_target_pairs={{0,3},{1,0},{2,1},{3,2},{4,7},{5,4},{6,5},{7,6},{8,11},{9,8},{10,9... | collective-permute-start | bytes 589832 | tf_op jit(solution)/shard_map/ppermute | solution.py:40
  241.9 22.1 %collective-permute-start.31 = (bf16[96,768]{1,0:T(8,128)(2,1)S(1)}, bf16[96,768]{1,0:T(8,128)(2,1)S(1)}, u32[]{:S(2)}, u32[]{:S(2)}) collective-permute-start(bf16[96,768]{1,0:T(8,128)(2,1)S(1)} %slice_bitcast_fusion.12), channel_id=1, source_target_pairs={{0,1},{1,2},{2,3},{3,0},{4,5},{5,6},{6,7},{7,4},{8,9},{9,10},{10,1... | collective-permute-start | bytes 442376 | tf_op jit(solution)/shard_map/ppermute | solution.py:40
  246.5 17.4 %collective-permute-start.32 = (bf16[96,768]{1,0:T(8,128)(2,1)S(1)}, bf16[96,768]{1,0:T(8,128)(2,1)S(1)}, u32[]{:S(2)}, u32[]{:S(2)}) collective-permute-start(bf16[96,768]{1,0:T(8,128)(2,1)S(1)} %get-tuple-element.216), channel_id=1, source_target_pairs={{0,2},{1,3},{2,0},{3,1},{4,6},{5,7},{6,4},{7,5},{8,10},{9,11},{10,... | collective-permute-start | bytes 442376 | tf_op jit(solution)/shard_map/ppermute | solution.py:40
  249.0 15.0 %collective-permute-start.33 = (bf16[96,768]{1,0:T(8,128)(2,1)S(1)}, bf16[96,768]{1,0:T(8,128)(2,1)S(1)}, u32[]{:S(2)}, u32[]{:S(2)}) collective-permute-start(bf16[96,768]{1,0:T(8,128)(2,1)S(1)} %get-tuple-element.217), channel_id=1, source_target_pairs={{0,3},{1,0},{2,1},{3,2},{4,7},{5,4},{6,5},{7,6},{8,11},{9,8},{10,9... | collective-permute-start | bytes 442376 | tf_op jit(solution)/shard_map/ppermute | solution.py:40
  264.6 93.6 %all-gather.4.cloned.1.call-start = ((), (), s32[]{:S(2)}) async-start(), calls=%async_computation.3 | async-start | bytes 2365440 | tf_op jit(solution)/shard_map/all_gather | solution.py:898
  273.4 20.4 %collective-permute-start.36 = (bf16[2,2,96,768]{3,2,1,0:T(8,128)(2,1)S(1)}, bf16[2,2,96,768]{3,2,1,0:T(8,128)(2,1)}, u32[]{:S(2)}, u32[]{:S(2)}) collective-permute-start(bf16[2,2,96,768]{3,2,1,0:T(8,128)(2,1)S(1)} %get-tuple-element.372), channel_id=1, source_target_pairs={{0,16},{4,20},{8,24},{12,28},{16,0},{20,4},{24,8},{28,12},{1,17},{... | collective-permute-start | bytes 1769480 | tf_op jit(solution)/shard_map/ppermute | solution.py:48
  274.9 19.6 %collective-permute-start.35 = (bf16[2,2,96,768]{3,2,1,0:T(8,128)(2,1)S(1)}, bf16[2,2,96,768]{3,2,1,0:T(8,128)(2,1)S(1)}, u32[]{:S(2)}, u32[]{:S(2)}) collective-permute-start(bf16[2,2,96,768]{3,2,1,0:T(8,128)(2,1)S(1)} %get-tuple-element.374), channel_id=1, source_target_pairs={{0,8},{4,12},{8,0},{12,4},{16,24},{20,28},{24,16},{28,20},{1,9},{5... | collective-permute-start | bytes 1769480 | tf_op jit(solution)/shard_map/ppermute | solution.py:48
  275.5 18.2 %collective-permute-start.37 = (bf16[128,768]{1,0:T(8,128)(2,1)S(1)}, bf16[128,768]{1,0:T(8,128)(2,1)S(1)}, u32[]{:S(2)}, u32[]{:S(2)}) collective-permute-start(bf16[128,768]{1,0:T(8,128)(2,1)S(1)} %get-tuple-element.383), channel_id=1, source_target_pairs={{0,1},{1,2},{2,3},{3,0},{4,5},{5,6},{6,7},{7,4},{8,9},{9,10},{10,1... | collective-permute-start | bytes 589832 | tf_op jit(solution)/shard_map/ppermute | solution.py:40
  277.5 16.2 %collective-permute-start.38 = (bf16[128,768]{1,0:T(8,128)(2,1)S(1)}, bf16[128,768]{1,0:T(8,128)(2,1)S(1)}, u32[]{:S(2)}, u32[]{:S(2)}) collective-permute-start(bf16[128,768]{1,0:T(8,128)(2,1)S(1)} %get-tuple-element.385), channel_id=1, source_target_pairs={{0,2},{1,3},{2,0},{3,1},{4,6},{5,7},{6,4},{7,5},{8,10},{9,11},{10,... | collective-permute-start | bytes 589832 | tf_op jit(solution)/shard_map/ppermute | solution.py:40
  277.7 16.1 %collective-permute-start.39 = (bf16[128,768]{1,0:T(8,128)(2,1)S(1)}, bf16[128,768]{1,0:T(8,128)(2,1)S(1)}, u32[]{:S(2)}, u32[]{:S(2)}) collective-permute-start(bf16[128,768]{1,0:T(8,128)(2,1)S(1)} %get-tuple-element.384), channel_id=1, source_target_pairs={{0,3},{1,0},{2,1},{3,2},{4,7},{5,4},{6,5},{7,6},{8,11},{9,8},{10,9... | collective-permute-start | bytes 589832 | tf_op jit(solution)/shard_map/ppermute | solution.py:40
  297.3 65.1 %collective-permute-start.50 = (bf16[128,768]{1,0:T(8,128)(2,1)}, bf16[128,768]{1,0:T(8,128)(2,1)}, u32[]{:S(2)}, u32[]{:S(2)}) collective-permute-start(bf16[128,768]{1,0:T(8,128)(2,1)} %get-tuple-element.380), channel_id=1, source_target_pairs={{0,1},{1,2},{2,3},{3,0},{4,5},{5,6},{6,7},{7,4},{8,9},{9,10},{10,1... | collective-permute-start | bytes 589832 | tf_op jit(solution)/shard_map/ppermute | solution.py:40
  299.9 62.4 %collective-permute-start.51 = (bf16[128,768]{1,0:T(8,128)(2,1)}, bf16[128,768]{1,0:T(8,128)(2,1)}, u32[]{:S(2)}, u32[]{:S(2)}) collective-permute-start(bf16[128,768]{1,0:T(8,128)(2,1)} %get-tuple-element.382), channel_id=1, source_target_pairs={{0,2},{1,3},{2,0},{3,1},{4,6},{5,7},{6,4},{7,5},{8,10},{9,11},{10,... | collective-permute-start | bytes 589832 | tf_op jit(solution)/shard_map/ppermute | solution.py:40
  302.1 13.1 %collective-permute-start.44 = (bf16[2,96,768]{2,1,0:T(8,128)(2,1)S(1)}, bf16[2,96,768]{2,1,0:T(8,128)(2,1)S(1)}, u32[]{:S(2)}, u32[]{:S(2)}) collective-permute-start(bf16[2,96,768]{2,1,0:T(8,128)(2,1)S(1)} %fusion.19), channel_id=1, source_target_pairs={{0,8},{4,12},{8,0},{12,4},{16,24},{20,28},{24,16},{28,20},{1,9},{5... | collective-permute-start | bytes 884744 | tf_op jit(solution)/shard_map/ppermute | solution.py:48
  309.2 35.2 %collective-permute-start.41 = (bf16[2,2,96,768]{3,2,1,0:T(8,128)(2,1)S(1)}, bf16[2,2,96,768]{3,2,1,0:T(8,128)(2,1)S(1)}, u32[]{:S(2)}, u32[]{:S(2)}) collective-permute-start(bf16[2,2,96,768]{3,2,1,0:T(8,128)(2,1)S(1)} %get-tuple-element.370), channel_id=1, source_target_pairs={{0,8},{4,12},{8,0},{12,4},{16,24},{20,28},{24,16},{28,20},{1,9},{5... | collective-permute-start | bytes 1769480 | tf_op jit(solution)/shard_map/ppermute | solution.py:48
  314.8 29.6 %collective-permute-start.42 = (bf16[2,2,96,768]{3,2,1,0:T(8,128)(2,1)S(1)}, bf16[2,2,96,768]{3,2,1,0:T(8,128)(2,1)S(1)}, u32[]{:S(2)}, u32[]{:S(2)}) collective-permute-start(bf16[2,2,96,768]{3,2,1,0:T(8,128)(2,1)S(1)} %get-tuple-element.368), channel_id=1, source_target_pairs={{0,16},{4,20},{8,24},{12,28},{16,0},{20,4},{24,8},{28,12},{1,17},{... | collective-permute-start | bytes 1769480 | tf_op jit(solution)/shard_map/ppermute | solution.py:48
  315.2 13.0 %collective-permute-start.46 = (f32[64,128]{1,0:T(8,128)S(1)}, f32[64,128]{1,0:T(8,128)S(1)}, u32[]{:S(2)}, u32[]{:S(2)}) collective-permute-start(f32[64,128]{1,0:T(8,128)S(1)} %add.260), channel_id=1, source_target_pairs={{0,8},{4,12},{8,0},{12,4},{16,24},{20,28},{24,16},{28,20},{1,9},{5... | collective-permute-start | bytes 98312 | tf_op jit(solution)/shard_map/ppermute | solution.py:48
  341.0 21.4 %collective-permute-start.52 = (bf16[128,768]{1,0:T(8,128)(2,1)}, bf16[128,768]{1,0:T(8,128)(2,1)S(1)}, u32[]{:S(2)}, u32[]{:S(2)}) collective-permute-start(bf16[128,768]{1,0:T(8,128)(2,1)} %get-tuple-element.381), channel_id=1, source_target_pairs={{0,3},{1,0},{2,1},{3,2},{4,7},{5,4},{6,5},{7,6},{8,11},{9,8},{10,9... | collective-permute-start | bytes 589832 | tf_op jit(solution)/shard_map/ppermute | solution.py:40
  345.2 21.0 %collective-permute-start.53 = (bf16[2,96,768]{2,1,0:T(8,128)(2,1)S(1)}, bf16[2,96,768]{2,1,0:T(8,128)(2,1)}, u32[]{:S(2)}, u32[]{:S(2)}) collective-permute-start(bf16[2,96,768]{2,1,0:T(8,128)(2,1)S(1)} %fusion.20), channel_id=1, source_target_pairs={{0,16},{4,20},{8,24},{12,28},{16,0},{20,4},{24,8},{28,12},{1,17},{... | collective-permute-start | bytes 884744 | tf_op jit(solution)/shard_map/ppermute | solution.py:48
  347.6 19.8 %collective-permute-start.54 = (bf16[2,96,768]{2,1,0:T(8,128)(2,1)S(1)}, bf16[2,96,768]{2,1,0:T(8,128)(2,1)}, u32[]{:S(2)}, u32[]{:S(2)}) collective-permute-start(bf16[2,96,768]{2,1,0:T(8,128)(2,1)S(1)} %fusion.21), channel_id=1, source_target_pairs={{0,8},{4,12},{8,0},{12,4},{16,24},{20,28},{24,16},{28,20},{1,9},{5... | collective-permute-start | bytes 884744 | tf_op jit(solution)/shard_map/ppermute | solution.py:48
  363.2 13.7 %collective-permute-start.56 = (bf16[96,768]{1,0:T(8,128)(2,1)}, bf16[96,768]{1,0:T(8,128)(2,1)S(1)}, u32[]{:S(2)}, u32[]{:S(2)}) collective-permute-start(bf16[96,768]{1,0:T(8,128)(2,1)} %get-tuple-element.266), channel_id=1, source_target_pairs={{0,2},{1,3},{2,0},{3,1},{4,6},{5,7},{6,4},{7,5},{8,10},{9,11},{10,... | collective-permute-start | bytes 442376 | tf_op jit(solution)/shard_map/ppermute | solution.py:40
  365.2 11.8 %collective-permute-start.57 = (bf16[96,768]{1,0:T(8,128)(2,1)}, bf16[96,768]{1,0:T(8,128)(2,1)S(1)}, u32[]{:S(2)}, u32[]{:S(2)}) collective-permute-start(bf16[96,768]{1,0:T(8,128)(2,1)} %get-tuple-element.267), channel_id=1, source_target_pairs={{0,3},{1,0},{2,1},{3,2},{4,7},{5,4},{6,5},{7,6},{8,11},{9,8},{10,9... | collective-permute-start | bytes 442376 | tf_op jit(solution)/shard_map/ppermute | solution.py:40
  (94 other events, 1057.7 us)
Sparse Core Ops, SparseCore 0:
  12.3 108.8 all-gather.5
  295.6 62.5 all-gather.3
Sparse Core Ops, SparseCore 1:
  168.3 52.7 reduce-scatter.2
  264.2 46.0 reduce-scatter.4

commit v3 on v2

--- a/solution.py
+++ b/solution.py
@@ -40,10 +40,6 @@
     return lax.ppermute(array, "mp", [(i, (i + step) % size) for i in range(size)])
 
 
-def swap_mp(array, bit):
-    return lax.ppermute(array, "mp", [(i, i ^ bit) for i in range(lax.axis_size("mp"))])
-
-
 def swap_dp(array, bit):
     return lax.ppermute(array, "dp", [(i, i ^ bit) for i in range(lax.axis_size("dp"))])
 
@@ -63,30 +59,6 @@
     return (left.astype(f32) + right.astype(f32)).astype(bf16)
 
 
-def stack_slots(block, others):
-    return jnp.stack([block, others[0]]), jnp.stack(others[1:])
-
-
-def spread_once(first, second):
-    core, along, across = high_bits()
-    return swap_dp(first, along), swap_dp(second, across)
-
-
-def spread_twice(first_two, second_two):
-    core, along, across = high_bits()
-    return swap_dp(first_two, across), swap_dp(second_two, along)
-
-
-def join_places(first_two, second_two, first_far, second_far):
-    return jnp.concatenate(
-        [
-            jnp.concatenate([first_two, first_far]),
-            jnp.stack([second_two[0], second_far[0], second_two[1], second_far[1]]),
-        ],
-        axis=1,
-    )
-
-
 def swap_cores(array):
     return swap_dp(array, high_bits()[0])
 
@@ -115,7 +87,7 @@
     sums = [
         halves[i][0][0].astype(f32) + got[i][0].astype(f32) + last_got[i].astype(f32) for i in range(2)
     ]
-    return [sums[0][0], sums[0][1], sums[1][0], sums[1][1]]
+    return [sums[0][0], sums[0][1], sums[1][0], sums[1][1]] + [part[i] for i in range(2, sums[0].shape[0]) for part in sums]
 
 
 def send_slots(slots):
@@ -155,82 +127,47 @@
     return parts[0], parts[1], parts[2], parts[3].T
 
 
-def reduce_ffn(grads):
-    return lax.psum_scatter(grads, "dp", scatter_dimension=0, tiled=True)
-
-
-def two_matrices(sums):
-    rows, width = sums.shape
-    if rows % 16:
-        sums = sums.astype(f32)
-        return sums[:, : width // 2], sums[:, width // 2 :].T
-    return call(
-        finish_ffn_kernel,
-        "ffn_matrices",
-        [sums],
-        (),
-        (),
-        [((rows, width // 2), f32), ((width // 2, rows), f32)],
-        [],
-    )
-
-
-def gather_blocks(blocks):
+def two_matrices(widen, narrow):
+    return scatter_rest(widen), scatter_rest(narrow).T
+
+
+def gather_blocks(slots):
     low = lax.axis_size("dp") // BLOCKS
+    groups = [[high * low + i for high in range(BLOCKS)] for i in range(low)]
     if low == 1:
-        every = lax.all_gather(blocks, ("dp", "mp"), axis=0, tiled=False)
-        return every.reshape(BLOCKS, -1, *blocks.shape)
-    groups = [[high * low + i for high in range(BLOCKS)] for i in range(low)]
-    return lax.all_gather(
-        lax.all_gather(blocks, "mp", axis=0, tiled=False),
-        "dp",
-        axis=0,
-        axis_index_groups=groups,
-        tiled=False,
-    )
-
-
-def sum_everywhere(array):
+        groups = None
+    return lax.all_gather(slots, "dp", axis=0, axis_index_groups=groups, tiled=False)
+
+
+def sum_over(axis, array):
+    size = lax.axis_size(axis)
     bit = 1
-    while bit < lax.axis_size("dp"):
-        array = array + swap_dp(array, bit)
-        bit *= 2
-    bit = 1
-    while bit < lax.axis_size("mp"):
-        array = array + swap_mp(array, bit)
+    while bit < size:
+        array = array + lax.ppermute(array, axis, [(i, i ^ bit) for i in range(size)])
         bit *= 2
     return array
 
 
-def fetch_weights(parts, group, held, sems, place, mp_at, order):
-    copies = {(what, slot): [] for what in order for slot in range(4)}
-    if len(parts) == 2:
-        for slot in range(4):
-            for j in range(4):
-                for side in range(2):
-                    held[slot, place ^ (2 * j + side)] = parts[side][j, slot]
-        return copies
+def fetch_weights(weights, group, held, sems, order):
+    copies = {}
     for i, what in enumerate(order):
         blocks = pl.ds(6, 2) if what == "merge" else pl.ds(0, 6)
         for slot in range(4):
-            copy = pltpu.make_async_copy(
-                parts[0].at[blocks, (mp_at + slot) % 4, group],
-                held.at[slot, blocks],
-                sems.at[slot, i],
+            copies[what, slot] = pltpu.make_async_copy(
+                weights.at[blocks, slot, group], held.at[slot, blocks], sems.at[slot, i]
             )
-            copy.start()
-            copies[what, slot].append(copy)
+            copies[what, slot].start()
     return copies
+
+
+def slot_rows(held, slot, first, last):
+    part = held[slot, 2 * first : 2 * last]
+    return part.reshape(part.shape[0] * part.shape[1], part.shape[2])
 
 
 def wait_all(copies):
     for copy in copies:
         copy.wait()
-
-
-def slot_rows(held, slot, first, last):
-    part = held[slot, 2 * first : 2 * last]
-    return part.reshape(part.shape[0] * part.shape[1], part.shape[2])
 
 
 def blocks_kernel(groups, place_ref, *refs):
@@ -317,7 +254,7 @@
     )
 
 
-def attention_forward_kernel(kind, parts, *refs):
+def attention_forward_kernel(kind, *refs):
     refs = list(refs)
     place_ref, x_ref = refs[:2]
     del refs[:2]
@@ -325,9 +262,8 @@
     gains_ref = refs.pop(0)
     gain, later = gain_rows(kind, gains_ref)
     rel_ref = refs.pop(0) if kind != "cross" else None
-    weights = refs[:parts]
-    r1_ref, next_ref, a_ref, q_ref, kv_ref, o_ref, held, sems = refs[parts:]
-    copies = fetch_weights(weights, int(kind == "cross"), held, sems, place_ref[0], place_ref[1], ("rest", "merge"))
+    weights, r1_ref, next_ref, a_ref, q_ref, kv_ref, o_ref, held, sems = refs
+    copies = fetch_weights(weights, int(kind == "cross"), held, sems, ("rest", "merge"))
     r = x_ref[...].astype(f32)
     rows = r.shape[0]
     a = (r * inverse_rms(r) * gain).astype(bf16)
@@ -343,7 +279,7 @@
     queries = []
     sources = []
     for slot in range(4):
-        wait_all(copies["rest", slot])
+        copies["rest", slot].wait()
         if kind == "cross":
             q = nt(a, slot_rows(held, slot, 0, 1)).astype(bf16)
             kv = nt(pre_ref[...], slot_rows(held, slot, 1, 3)).astype(bf16)
@@ -366,7 +302,7 @@
         mixed.append(o)
     acc = r
     for slot in range(4):
-        wait_all(copies["merge", slot])
+        copies["merge", slot].wait()
         acc = acc + nn(mixed[slot], slot_rows(held, slot, 3, 4))
     r1_ref[...] = acc
     next_ref[...] = (acc * inverse_rms(acc) * later).astype(bf16)
@@ -379,31 +315,10 @@
     return t * (scaled - r * (t * t) * jnp.mean(scaled * r, axis=-1, keepdims=True))
 
 
-def store_blocks(keep_ref, send_ref, place, slot, value):
-    size = value.shape[0] // BLOCKS
-    side = place % 2
-    for pair in range(BLOCKS // 2):
-        where = pair ^ (place // 2)
-        if slot // 2 == 0:
-            where = (where % 2) * 2 + where // 2
-        even = value[2 * pair * size : (2 * pair + 1) * size]
-        odd = value[(2 * pair + 1) * size : (2 * pair + 2) * size]
-
-        @pl.when(side == 0)
-        def _():
-            keep_ref[slot // 2, where, slot % 2] = even
-            send_ref[slot // 2, where, slot % 2] = odd
-
-        @pl.when(side == 1)
-        def _():
-            keep_ref[slot // 2, where, slot % 2] = odd
-            send_ref[slot // 2, where, slot % 2] = even
-
-
-def attention_backward_kernel(kind, parts, after_ffn, *refs):
+def attention_backward_kernel(kind, after_ffn, *refs):
     refs = list(refs)
     place_ref = refs.pop(0)
-    place, mp_at = place_ref[0], place_ref[1]
+    place = place_ref[0]
     if after_ffn:
         dc_own, *dc_rest = refs[:4]
         up_ref, r1_ref = refs[4:6]
@@ -415,9 +330,11 @@
     refs = refs[3:]
     source_ref = refs.pop(0) if kind == "cross" else None
     q_ref, kv_ref, o_ref = refs[:3]
-    weights = refs[3 : 3 + parts]
-    refs = refs[3 + parts :]
+    weights = refs[3]
+    refs = refs[4:]
     rel_ref, bucket_ref = (refs.pop(0), refs.pop(0)) if kind != "cross" else (None, None)
+    if kind != "self":
+        refs = refs[2:]
     dx_ref, dgain_ref = refs[:2]
     refs = refs[2:]
     keep_ref, send_ref = refs.pop(0), refs.pop(0)
@@ -430,9 +347,9 @@
     held, sems, left, right = refs[:4]
     refs = refs[4:]
     ds_sum = refs.pop(0) if kind != "cross" else None
-    weight_grad = refs.pop(0)
-
-    copies = fetch_weights(weights, int(kind == "cross"), held, sems, place, mp_at, ("merge", "rest"))
+    stage, out_sems = refs
+    copies = fetch_weights(weights, int(kind == "cross"), held, sems, ("merge", "rest"))
+
     d_out = up_ref[...].astype(f32)
     if after_ffn:
         dn = dc_own[...]
@@ -443,14 +360,19 @@
     rows, width = g.shape
     keys = kv_ref.shape[1]
     stacked = [a_ref[...]] + ([source_ref[...]] if kind == "cross" else []) + [g]
-    left[...] = jnp.concatenate(stacked, axis=0).T
+    turned = jnp.concatenate(stacked, axis=0).T
+    size = width // BLOCKS
+    for d in range(BLOCKS):
+        away = place ^ d
+        at = pl.multiple_of(((away % 2) * 4 + away // 2) * size, size)
+        left[pl.ds(at, size), :] = turned[d * size : (d + 1) * size]
     source_at = rows if kind == "cross" else 0
     g_at = left.shape[1] - rows
     right[...] = jnp.zeros(right.shape, bf16)
     same, before = masks(kind, rows, keys)
     grads = []
     for slot in range(4):
-        wait_all(copies["merge", slot])
+        copies["merge", slot].wait()
         grads.append(nt(g, slot_rows(held, slot, 3, 4)).astype(bf16))
         right[slot, g_at:, 576:768] = o_ref[slot]
     chances = []
@@ -474,14 +396,22 @@
             for j in range(3):
                 wide = ds[j * rows : (j + 1) * rows, :rows].astype(f32)
                 ds_sum[3 * slot + j] = wide[:SEQ] + wide[SEQ:]
+    outgoing = []
     for slot in range(4):
         grad = nn(left[...], right[slot]).astype(bf16)
-        weight_grad[...] = grad
-        store_blocks(keep_ref, send_ref, place, slot, weight_grad)
+        for j in range(BLOCKS):
+            to = (j // 4) * 4 + ((j % 2) * 2 + (j % 4) // 2 if slot // 2 == 0 else j % 4)
+            stage[slot, to] = grad[j * size : (j + 1) * size]
+        for i, out in enumerate((keep_ref, send_ref)):
+            copy = pltpu.make_async_copy(
+                stage.at[slot, pl.ds(4 * i, 4)], out.at[slot // 2, :, slot % 2], out_sems.at[slot, i]
+            )
+            copy.start()
+            outgoing.append(copy)
     total = None
     source_total = None
     for slot in range(4):
-        wait_all(copies["rest", slot])
+        copies["rest", slot].wait()
         if kind == "cross":
             part = nn(right[slot, 0:rows, 0:192], slot_rows(held, slot, 0, 1))
             other = nn(right[slot, rows : rows + keys, 192:576], slot_rows(held, slot, 1, 3))
@@ -504,6 +434,8 @@
             for head in range(heads):
                 part = jnp.where(chosen, ds_sum[head], 0.0)
                 bias_grad[head, b] = jnp.sum(part.reshape(SEQ // 8, 8, 2 * SEQ), axis=0)
+
+    wait_all(outgoing)
 
 
 def ffn_first_kernel(c0, c1, c2, c3, g0, g1, g2, g3, widen, narrow, c_all, g_all, h_ref, du_ref, dc_own, dc_rest):
@@ -529,17 +461,43 @@
             dc_rest[i, :, at] = dc[(i + 1) * tokens : (i + 2) * tokens].astype(bf16)
 
 
-def ffn_second_kernel(c_all, g_all, h_ref, du_ref, narrow, out_own, out_rest, grad_ref):
-    tokens = out_own.shape[0]
-    hidden = narrow.shape[0]
+def ffn_second_kernel(across, place_ref, c_all, g_all, h_ref, du_ref, narrow, *refs):
+    outs = refs[:-4]
+    keep_ref, send_ref, stage, sems = refs[-4:]
+    tokens = c_all.shape[0] // 4
+    place = place_ref[0]
+    copies = []
+    for half, (left, right) in enumerate(((c_all, du_ref), (g_all, h_ref))):
+        grad = tn(left[...], right[...]).astype(bf16)
+        size = grad.shape[0] // BLOCKS
+        for d in range(BLOCKS):
+            away = place ^ d
+            where = away // 2
+            if half == 0:
+                where = (where % 2) * 2 + where // 2
+            stage[half, (away % 2) * 4 + where] = grad[d * size : (d + 1) * size]
+        for i, ref in enumerate((keep_ref, send_ref)):
+            copy = pltpu.make_async_copy(
+                stage.at[half, pl.ds(4 * i, 4)], ref.at[half, :, 2], sems.at[half, i]
+            )
+            copy.start()
+            copies.append(copy)
     for n in range(narrow.shape[1] // 256):
         at = slice(n * 256, (n + 1) * 256)
         out = nn(h_ref[...], narrow[:, at])
-        out_own[:, at] = out[:tokens]
-        for i in range(3):
-            out_rest[i, :, at] = out[(i + 1) * tokens : (i + 2) * tokens].astype(bf16)
-    grad_ref[:, :hidden] = tn(c_all[...], du_ref[...]).astype(bf16)
-    grad_ref[:, hidden:] = tn(g_all[...], h_ref[...]).astype(bf16)
+        for i in range(4):
+            part = out[i * tokens : (i + 1) * tokens]
+            if across:
+                row = pl.multiple_of((place_ref[1] + i) % 4 * tokens, tokens)
+                outs[0][pl.ds(row, tokens), at] = part.astype(bf16)
+            else:
+                outs[i][:, at] = part.astype(outs[i].dtype)
+    wait_all(copies)
+
+
+def gains_kernel(*refs):
+    for i in range(5):
+        refs[5][i : i + 1, :] = refs[i][...].reshape(1, -1)
 
 
 def finish_kernel(total_ref, got1, got2, got3, query, key, value, merge):
@@ -550,12 +508,6 @@
     for i, out in enumerate((query, key, value)):
         out[...] = total[:, i * width : (i + 1) * width]
     merge[...] = total[:, 3 * width :].T
-
-
-def finish_ffn_kernel(sums, widen, narrow):
-    hidden = widen.shape[1]
-    widen[...] = sums[:, :hidden].astype(f32)
-    narrow[...] = sums[:, hidden:].astype(f32).T
 
 
 def table_kernel(place_ref, used_ref, out_ref):
@@ -595,7 +547,7 @@
             out[32 + 6 * i + j : 33 + 6 * i + j, :] = refs[i][:, 128 * j : 128 * (j + 1)]
 
 
-def call(kernel, name, operands, smem, hbm, outs, scratch, limit=28):
+def call(kernel, name, operands, smem, hbm, outs, scratch, limit=28, hbm_outs=(), aliases=None):
     specs = []
     for i in range(len(operands)):
         if i in smem:
@@ -608,8 +560,12 @@
         kernel,
         out_shape=[jax.ShapeDtypeStruct(shape, kind) for shape, kind in outs],
         in_specs=specs,
-        out_specs=[pl.BlockSpec(memory_space=pltpu.VMEM)] * len(outs),
+        out_specs=[
+            pl.BlockSpec(memory_space=pl.ANY if i in hbm_outs else pltpu.VMEM)
+            for i in range(len(outs))
+        ],
         scratch_shapes=scratch,
+        input_output_aliases=aliases or {},
         compiler_params=pltpu.CompilerParams(vmem_limit_bytes=limit * 1024 * 1024),
         cost_estimate=pl.CostEstimate(flops=0, bytes_accessed=1024, transcendentals=0),
         name=name,
@@ -647,10 +603,10 @@
     operands.append(gains)
     if rel is not None:
         operands.append(rel)
-    hbm = (len(operands),) if len(weights) == 1 else ()
-    operands += weights
+    hbm = (len(operands),)
+    operands.append(weights)
     return call(
-        functools.partial(attention_forward_kernel, kind, len(weights)),
+        functools.partial(attention_forward_kernel, kind),
         kind + "_forward",
         operands,
         (0,),
@@ -664,11 +620,13 @@
             ((4, rows, 192), bf16),
         ],
         [pltpu.VMEM((4, BLOCKS, width // BLOCKS, width), bf16), pltpu.SemaphoreType.DMA((4, 2))],
-        56 if len(weights) == 1 else 28,
-    )
-
-
-def attention_backward(kind, place, ffn, upstream, x, gains, stored, source, weights, rel, bucket, buckets):
+        56,
+    )
+
+
+def attention_backward(
+    kind, place, ffn, upstream, x, gains, stored, source, weights, rel, bucket, buckets, grads
+):
     rows, width = upstream.shape
     a, q, kv, o = stored
     keys = kv.shape[1]
@@ -682,16 +640,21 @@
     if source is not None:
         operands.append(source)
     operands += [q, kv, o]
-    hbm = (len(operands),) if len(weights) == 1 else ()
-    operands += weights
+    hbm = (len(operands),)
+    operands.append(weights)
     if kind != "cross":
         operands += [rel, bucket]
+    aliases = None
+    if grads is not None:
+        hbm += (len(operands), len(operands) + 1)
+        aliases = {len(operands): 2, len(operands) + 1: 3}
+        operands += grads
     block = width // BLOCKS
     outs = [
         ((rows, width), f32),
         ((1, width), f32),
     ]
-    outs += [((2, 4, 2, block, width), bf16)] * 2
+    outs += [((2, 4, 2 if grads is None else 3, block, width), bf16)] * 2
     if ffn is not None:
         outs.append(((1, width), f32))
     if kind == "encoder":
@@ -709,16 +672,18 @@
     ]
     if kind != "cross":
         scratch.append(pltpu.VMEM((rel.shape[0], SEQ, 2 * SEQ), f32))
-    scratch.append(pltpu.VMEM((width, width), bf16))
+    scratch += [pltpu.VMEM((4, BLOCKS, block, width), bf16), pltpu.SemaphoreType.DMA((4, 2))]
     return call(
-        functools.partial(attention_backward_kernel, kind, len(weights), ffn is not None),
+        functools.partial(attention_backward_kernel, kind, ffn is not None),
         kind + "_backward",
         operands,
         (0,),
         hbm,
         outs,
         scratch,
-        56 if len(weights) == 1 else 28,
+        56,
+        (2, 3),
+        aliases,
     )
 
 
@@ -744,18 +709,26 @@
     )
 
 
-def ffn_second(name, c_all, g_all, h, du, narrow):
+def ffn_second(name, across, place, c_all, g_all, h, du, narrow):
     every, width = c_all.shape
     hidden = h.shape[1]
     tokens = every // 4
+    block = width // BLOCKS
+    if across:
+        outs = [((every, width), bf16)]
+    else:
+        outs = [((tokens, width), f32)] + [((tokens, width), bf16)] * 3
+    count = len(outs)
     return call(
-        ffn_second_kernel,
+        functools.partial(ffn_second_kernel, across),
         name + "_second",
-        [c_all, g_all, h, du, narrow],
+        [place, c_all, g_all, h, du, narrow],
+        (0,),
         (),
-        (),
-        [((tokens, width), f32), ((3, tokens, width), bf16), ((width, 2 * hidden), bf16)],
-        [],
+        outs + [((2, 4, 3, block, hidden), bf16)] * 2,
+        [pltpu.VMEM((2, BLOCKS, block, hidden), bf16), pltpu.SemaphoreType.DMA((2, 2))],
+        28,
+        (count, count + 1),
     )
 
 
@@ -828,8 +801,9 @@
             (cross_query, cross_key, cross_value, cross_merge),
         ],
     )
-    encoder_others = gather_tokens(encoder_block)[1:]
-    decoder_weights = (gather_blocks(decoder_blocks),)
+    encoder_slots = jnp.stack(gather_tokens(encoder_block))[:, None]
+    encoder_weights = gather_blocks(encoder_slots)
+    encoder_g = gather_tokens(after(encoder_upstream, encoder_slots))
 
     own_questions = memory_index.shape[0] // lax.axis_size("mp")
     entries = lax.dynamic_slice_in_dim(
@@ -843,34 +817,41 @@
     entry_rows = jnp.repeat(entries, PREFIX)
     numbers = jnp.stack([entry_rows // 32, entry_rows % 32], axis=1).astype(bf16)
     numbers = jnp.pad(numbers, ((0, 0), (0, 126)))
-    gains = jnp.stack(
-        [encoder_gain, encoder_later_gain, decoder_gain, cross_gain, decoder_later_gain]
-    )
+    gains = call(
+        gains_kernel,
+        "gains",
+        [encoder_gain, encoder_later_gain, decoder_gain, cross_gain, decoder_later_gain],
+        (),
+        (),
+        [((5, width), f32)],
+        [],
+    )[0]
     small = (prefix, encoder_rel, encoder_twice, decoder_rel, decoder_twice, numbers, gains)
     small = after(small, encoder_block)
     prefix, encoder_rel, encoder_twice, decoder_rel, decoder_twice, numbers, gains = small
-
-    first, second = stack_slots(after(encoder_block, small), encoder_others)
-    first_got, second_got = spread_once(first, second)
-    encoder_g = gather_tokens(after(encoder_upstream, encoder_others))
-    pairs = after(
-        (jnp.stack([first, first_got]), jnp.stack([second, second_got])), encoder_g
-    )
-    fars = spread_twice(*pairs)
-    decoder_g = gather_tokens(after(decoder_upstream, encoder_g))
-    encoder_own = after(join_places(*pairs, *fars), decoder_g)
-    encoder_weights = (encoder_own, swap_cores(encoder_own))
+    decoder_slots = jnp.stack(gather_tokens(after(decoder_blocks, encoder_g, small)))
+    decoder_weights = gather_blocks(decoder_slots)
+
 
     encoder_r1, encoder_c, *encoder_stored = attention_forward(
-        "encoder", place_in, encoder_input, prefix, gains, encoder_rel, encoder_weights
+        "encoder",
+        after(place_in, encoder_g),
+        encoder_input,
+        prefix,
+        gains,
+        encoder_rel,
+        encoder_weights,
     )
     encoder_c = gather_tokens(encoder_c)
     c_all, g_all, h, du, dc_own, dc_rest = ffn_first(
         "encoder_ffn", encoder_c, encoder_g, encoder_widen, encoder_narrow
     )
     encoder_dc = (dc_own, return_tokens(dc_rest))
-    out_own, out_rest, grads = ffn_second("encoder_ffn", c_all, g_all, h, du, encoder_narrow)
-    encoder_ffn_sums = reduce_ffn(grads)
+    out, *grads = ffn_second(
+        "encoder_ffn", True, place_in, c_all, g_all, h, du, encoder_narrow
+    )
+    encoder_out = lax.psum_scatter(out, "mp", scatter_dimension=0, tiled=True)
+    decoder_g = gather_tokens(after(decoder_upstream, encoder_dc))
     (
         encoder_input_grad,
         encoder_gain_grad,
@@ -881,7 +862,7 @@
         encoder_bias_raw,
     ) = attention_backward(
         "encoder",
-        after(place_in, out_own),
+        after(place_in, out),
         (*encoder_dc, encoder_r1),
         encoder_upstream,
         encoder_input,
@@ -892,11 +873,12 @@
         encoder_rel,
         encoder_twice,
         encoder_bias.shape[0],
-    )
-    encoder_got = swap_cores(send)
+        grads,
+    )
+    encoder_got = swap_cores(after(send, decoder_g))
     packed = jnp.concatenate([prefix_grad[:prefix_rows], numbers], axis=1)
     used = lax.all_gather(packed, ("dp", "mp"), axis=0, tiled=True)
-    encoder_halves = fold_cores(after(keep, packed), encoder_got)
+    encoder_halves = fold_cores(keep, encoder_got)
     encoder_once = send_once(encoder_halves)
 
     self_r1, _, *self_stored = attention_forward(
@@ -906,29 +888,28 @@
         "cross", place_in, self_r1, encoder_states, gains, None, decoder_weights
     )
     decoder_c = gather_tokens(decoder_c)
-    encoder_last = fold_once(after(encoder_halves, cross_r2), encoder_once)
-    encoder_twice_got = send_twice(encoder_last)
     c_all, g_all, h, du, dc_own, dc_rest = ffn_first(
         "decoder_ffn",
-        [after(decoder_c[0], encoder_last), *decoder_c[1:]],
+        [after(decoder_c[0], encoder_once, encoder_out), *decoder_c[1:]],
         decoder_g,
         decoder_widen,
         decoder_narrow,
     )
-    decoder_dc = (dc_own, return_tokens(after(dc_rest, encoder_twice_got)))
-    out_own_d, out_rest_d, grads = ffn_second(
-        "decoder_ffn", c_all, g_all, h, du, decoder_narrow
-    )
-    decoder_ffn_sums = reduce_ffn(grads)
+    decoder_dc = (dc_own, return_tokens(dc_rest))
+    encoder_last = fold_once(after(encoder_halves, dc_own), encoder_once)
+    encoder_twice_got = send_twice(encoder_last)
+    out, *rest, keep, send = ffn_second(
+        "decoder_ffn", False, place_in, c_all, g_all, h, du, decoder_narrow
+    )
+    grads = [keep, send]
     encoder_sums = fold_twice(
-        after(encoder_halves, out_own_d), encoder_once, encoder_twice_got
-    )
-    encoder_widen_grad, encoder_narrow_grad = two_matrices(after(encoder_ffn_sums, encoder_sums))
+        after(encoder_halves, out), encoder_once, encoder_twice_got
+    )
     encoder_sent = send_slots(after(encoder_sums, decoder_dc))
 
     cross_dx, cross_gain_grad, keep, send, decoder_later_grad, states_grad = attention_backward(
         "cross",
-        after(place_in, encoder_narrow_grad),
+        after(place_in, encoder_sums),
         (*decoder_dc, cross_r2),
         decoder_upstream,
         self_r1,
@@ -939,11 +920,12 @@
         None,
         None,
         None,
+        grads,
     )
     cross_got = swap_cores(after(send, encoder_sent))
     cross_halves = fold_cores(keep, cross_got)
     cross_once = send_once(cross_halves)
-    encoder_out = return_tokens(after(out_rest, encoder_sent))
+    decoder_out = [to_mp(part, i + 1) for i, part in enumerate(after(rest, cross_halves))]
     decoder_input_grad, decoder_gain_grad, keep, send, decoder_bias_raw = attention_backward(
         "self",
         after(place_in, cross_halves),
@@ -957,8 +939,9 @@
         decoder_rel,
         decoder_twice,
         decoder_bias.shape[0],
-    )
-    self_got = swap_cores(after(send, cross_once, encoder_out))
+        None,
+    )
+    self_got = swap_cores(after(send, cross_once, decoder_out))
     cross_last = fold_once(after(cross_halves, decoder_input_grad), cross_once)
     cross_twice_got = send_twice(cross_last)
     sums = call(
@@ -981,37 +964,36 @@
     )[0]
     self_halves = fold_cores(keep, after(self_got, sums))
     self_once = send_once(self_halves)
-    decoder_out = return_tokens(after(out_rest_d, encoder_out))
-
-    encoder_mats = four_matrices(after(encoder_sums, self_halves), encoder_sent)
-    encoder_output = (
-        after(encoder_r1, self_halves) + out_own + sum(part.astype(f32) for part in encoder_out)
-    ).astype(bf16)
-    sums = sum_everywhere(after(sums, self_halves))
-    cross_sums = fold_twice(after(cross_halves, encoder_mats), cross_once, cross_twice_got)
-    self_last = fold_once(self_halves, after(self_once, cross_sums))
+    cross_sums = fold_twice(after(cross_halves, self_halves), cross_once, cross_twice_got)
+    cross_sent = send_slots(cross_sums)
+    self_last = fold_once(after(self_halves, cross_sent, used), self_once)
     self_twice_got = send_twice(self_last)
-    cross_sent = send_slots(after(cross_sums, self_last, decoder_out))
-
+    sums = sum_over("dp", after(sums, self_halves))
+    self_sums = fold_twice(after(self_halves, sums), self_once, self_twice_got)
+    self_sent = send_slots(self_sums)
+    sums = sum_over("mp", after(sums, self_sums))
+
+    def last(value):
+        return after(value, self_sums)
+
+    cross_mats = four_matrices(last(cross_sums), cross_sent)
+    encoder_mats = four_matrices(last(encoder_sums), encoder_sent)
+    encoder_output = (last(encoder_r1) + encoder_out.astype(f32)).astype(bf16)
+    encoder_widen_grad, encoder_narrow_grad = two_matrices(*last(encoder_sums[4:]))
     table_rows = memory_table.shape[0] // (lax.axis_size("dp") * lax.axis_size("mp"))
     table_grad = call(
         table_kernel,
         "table",
-        [after(place_in, self_last), used],
+        [last(place_in), last(used)],
         (0,),
         (),
         [((table_rows, PREFIX, width), f32)],
         [],
     )[0]
-    decoder_widen_grad, decoder_narrow_grad = two_matrices(after(decoder_ffn_sums, self_last))
     decoder_output = (
-        after(cross_r2, self_last) + out_own_d + sum(part.astype(f32) for part in decoder_out)
+        last(cross_r2) + out + sum(part.astype(f32) for part in decoder_out)
     ).astype(bf16)
-    self_sums = fold_twice(
-        after(self_halves, table_grad, decoder_narrow_grad), self_once, self_twice_got
-    )
-    self_sent = send_slots(after(self_sums, cross_sent))
-    cross_mats = four_matrices(after(cross_sums, self_sums), cross_sent)
+    decoder_widen_grad, decoder_narrow_grad = two_matrices(*last(cross_sums[4:]))
     self_mats = four_matrices(self_sums, self_sent)
 
     gain_sums = [sums[32 + 6 * i : 38 + 6 * i].reshape(-1) for i in range(5)]

time: 407 us -> 381 us (0.936)
  starting transfers between devices: 116 us -> 79.4 us
  other arithmetic: 23.4 us -> 35.1 us
  waiting for transfers between devices: 147 us -> 137 us
  local copies, waits for them, and re-layouts: 18.8 us -> 26.1 us
  Pallas kernels: 75.3 us -> 80 us
    ppermute x15 -> x18, waiting for transfers between devices: 78.9 us -> 62 us  [from_mp(): lax.ppermute(array, 'mp', [(i, (i - step) % size) for i in range(size)])]
    ppermute x2 -> x5, waiting for transfers between devices: 3.94 us -> 19.5 us  [sum_over(): lax.ppermute(array, axis, [(i, i ^ bit) for i in range(size)])]
    ppermute x23 -> x15, starting transfers between devices: 27.8 us -> 13.5 us  [swap_dp(): lax.ppermute(array, 'dp', [(i, i ^ bit) for i in range(lax.axis_size('dp'...]
    ppermute x21 -> x18, starting transfers between devices: 41.2 us -> 28.2 us  [to_mp(): lax.ppermute(array, 'mp', [(i, (i + step) % size) for i in range(size)])]
    ppermute x15 -> x18, starting transfers between devices: 43.5 us -> 34.1 us  [from_mp(): lax.ppermute(array, 'mp', [(i, (i - step) % size) for i in range(size)])]
    ppermute x21 -> x18, waiting for transfers between devices: 29.9 us -> 21.6 us  [to_mp(): lax.ppermute(array, 'mp', [(i, (i + step) % size) for i in range(size)])]
    convert_element_type x9, other arithmetic: 12.8 us -> 18.9 us  [rounded_sum(): return (left.astype(f32) + right.astype(f32)).astype(bf16)]
    pallas_call x18 -> x17, Pallas kernels: 75.3 us -> 80 us  [call(): pl.pallas_call(kernel, out_shape=[jax.ShapeDtypeStruct(shape, kind) for s...]
  transfers between devices with their start and end apart: 65 -> 60, of which waited for: 27 -> 27; matrix products, arithmetic and copies ran while one was open for 8% -> 11% of each run, Pallas kernels for 18% -> 19%
where the time goes in v3:
time: 381 us; the launch traced here: 374 us
  waiting for transfers between devices  137 us (36%)
  Pallas kernels  80 us (21%)
  starting transfers between devices  79.4 us (21%)
  other arithmetic  35.1 us (9%)
  local copies, waits for them, and re-layouts  26.1 us (7%)
  between operations  15.3 us (4%)
    pallas_call x17, Pallas kernels, call(): pl.pallas_call(kernel, out_shape=[jax.ShapeDtypeStruct(shape, kind) for s...  80 us
    ppermute x18, waiting for transfers between devices, from_mp(): lax.ppermute(array, 'mp', [(i, (i - step) % size) for i in range(size)])  62 us
    ppermute x18, starting transfers between devices, from_mp(): lax.ppermute(array, 'mp', [(i, (i - step) % size) for i in range(size)])  34.1 us
    ppermute x18, starting transfers between devices, to_mp(): lax.ppermute(array, 'mp', [(i, (i + step) % size) for i in range(size)])  28.2 us
    ppermute x15, waiting for transfers between devices, swap_dp(): lax.ppermute(array, 'dp', [(i, i ^ bit) for i in range(lax.axis_size('dp'...  27.5 us
    ppermute x18, waiting for transfers between devices, to_mp(): lax.ppermute(array, 'mp', [(i, (i + step) % size) for i in range(size)])  21.6 us
    ppermute x5, waiting for transfers between devices, sum_over(): lax.ppermute(array, axis, [(i, i ^ bit) for i in range(size)])  19.5 us
    convert_element_type x9, other arithmetic, rounded_sum(): return (left.astype(f32) + right.astype(f32)).astype(bf16)  18.9 us
  transfers between devices with their start and end apart: 60, of which 27 were waited for; matrix products, arithmetic and copies ran while one was open for 11% of the time, Pallas kernels for 19%

profile of v3, /device:TPU:0, one launch (start us, length us, event | category | flops | bytes accessed | tf_op | source)
XLA Modules:
  0.0 373.6 jit_solution(216717891072833341)
XLA Ops:
  7.9 2.6 weight_blocks.1
  10.5 3.1 collective-permute-start.5
  13.6 2.6 collective-permute-start.4
  17.6 3.1 collective-permute-done.5
  20.6 5.5 %collective-permute-done.4 = bf16[96,768]{1,0:T(8,128)(2,1)S(1)} collective-permute-done((bf16[96,768]{1,0:T(8,128)(2,1)}, bf16[96,768]{1,0:T(8,128)(2,1)S(1)}, u32[]{:S(2)}, u32[]{:S(2)}) %collective-permute-start.4) | collective-permute-done | bytes 147488 | tf_op jit(solution)/shard_map/ppermute | solution.py:35
  28.0 4.7 %collective-permute-start = (bf16[128,768]{1,0:T(8,128)(2,1)S(1)}, bf16[128,768]{1,0:T(8,128)(2,1)S(1)}, u32[]{:S(2)}, u32[]{:S(2)}) collective-permute-start(bf16[128,768]{1,0:T(8,128)(2,1)S(1)} %copy-done.16), channel_id=1, source_target_pairs={{0,3},{1,0},{2,1},{3,2},{4,7},{5,4},{6,5},{7,6},{8,11},{9,8},{10,9... | collective-permute-start | bytes 589832 | tf_op jit(solution)/shard_map/ppermute | solution.py:35
  47.7 3.0 collective-permute-done.1.g2
  51.9 2.7 collective-permute-start.16
  54.5 8.0 %collective-permute-done.18 = bf16[2,96,768]{2,1,0:T(8,128)(2,1)S(1)} collective-permute-done((bf16[2,96,768]{2,1,0:T(8,128)(2,1)S(1)}, bf16[2,96,768]{2,1,0:T(8,128)(2,1)S(1)}, u32[]{:S(2)}, u32[]{:S(2)}) %collective-permute-start.18) | collective-permute-done | bytes 294944 | tf_op jit(solution)/shard_map/ppermute | solution.py:35
  62.6 10.9 %collective-permute-done.17 = bf16[2,96,768]{2,1,0:T(8,128)(2,1)S(1)} collective-permute-done((bf16[2,96,768]{2,1,0:T(8,128)(2,1)S(1)}, bf16[2,96,768]{2,1,0:T(8,128)(2,1)S(1)}, u32[]{:S(2)}, u32[]{:S(2)}) %collective-permute-start.17) | collective-permute-done | bytes 294944 | tf_op jit(solution)/shard_map/ppermute | solution.py:35
  74.8 7.5 %encoder_forward.1 = (f32[128,768]{1,0:T(8,128)}, bf16[128,768]{1,0:T(8,128)(2,1)}, bf16[192,768]{1,0:T(8,128)(2,1)}, bf16[4,128,192]{2,1,0:T(8,128)(2,1)}, bf16...) custom-call(s32[3]{0:T(128)} %pad_add_fusion.2.place_ref.refs_0_, bf16[128,768]{1,0:T(8,128)(2,1)} %refs_7_.3, ...), custom_call_target="tpu_custom_call" | custom-call | bytes 1024 | tf_op jit(solution)/shard_map/encoder_forward/pallas_call | solution.py:559
  82.3 6.3 %collective-permute-start.6 = (bf16[128,768]{1,0:T(8,128)(2,1)}, bf16[128,768]{1,0:T(8,128)(2,1)S(1)}, u32[]{:S(2)}, u32[]{:S(2)}) collective-permute-start(bf16[128,768]{1,0:T(8,128)(2,1)} %get-tuple-element.155.c0), channel_id=1, source_target_pairs={{0,3},{1,0},{2,1},{3,2},{4,7},{5,4},{6,5},{7,6},{8,11},{9,8},{10,9... | collective-permute-start | bytes 589832 | tf_op jit(solution)/shard_map/ppermute | solution.py:35
  89.8 4.5 %collective-permute-done.6.c1 = bf16[128,768]{1,0:T(8,128)(2,1)S(1)} collective-permute-done((bf16[128,768]{1,0:T(8,128)(2,1)}, bf16[128,768]{1,0:T(8,128)(2,1)S(1)}, u32[]{:S(2)}, u32[]{:S(2)}) %collective-permute-start.6) | collective-permute-done | bytes 196640 | tf_op jit(solution)/shard_map/ppermute | solution.py:35
  94.3 12.2 %collective-permute-done.7.c2 = bf16[128,768]{1,0:T(8,128)(2,1)S(1)} collective-permute-done((bf16[128,768]{1,0:T(8,128)(2,1)}, bf16[128,768]{1,0:T(8,128)(2,1)S(1)}, u32[]{:S(2)}, u32[]{:S(2)}) %collective-permute-start.7) | collective-permute-done | bytes 196640 | tf_op jit(solution)/shard_map/ppermute | solution.py:35
  107.4 3.5 encoder_ffn_first.1
  111.6 3.2 collective-permute-start.11
  114.8 5.9 %collective-permute-done.9.refs_2_ = bf16[128,768]{1,0:T(8,128)(2,1)S(1)} collective-permute-done((bf16[128,768]{1,0:T(8,128)(2,1)S(1)}, bf16[128,768]{1,0:T(8,128)(2,1)S(1)}, u32[]{:S(2)}, u32[]{:S(2)}) %collective-permute-start.9) | collective-permute-done | bytes 196640 | tf_op jit(solution)/shard_map/ppermute | solution.py:40
  120.7 5.8 %collective-permute-done.10.refs_3_ = bf16[128,768]{1,0:T(8,128)(2,1)S(1)} collective-permute-done((bf16[128,768]{1,0:T(8,128)(2,1)S(1)}, bf16[128,768]{1,0:T(8,128)(2,1)S(1)}, u32[]{:S(2)}, u32[]{:S(2)}) %collective-permute-start.10) | collective-permute-done | bytes 196640 | tf_op jit(solution)/shard_map/ppermute | solution.py:40
  126.6 5.0 %collective-permute-start.12 = (bf16[128,768]{1,0:T(8,128)(2,1)S(1)}, bf16[128,768]{1,0:T(8,128)(2,1)S(1)}, u32[]{:S(2)}, u32[]{:S(2)}) collective-permute-start(bf16[128,768]{1,0:T(8,128)(2,1)S(1)} %copy-done.17), channel_id=1, source_target_pairs={{0,3},{1,0},{2,1},{3,2},{4,7},{5,4},{6,5},{7,6},{8,11},{9,8},{10,9... | collective-permute-start | bytes 589832 | tf_op jit(solution)/shard_map/ppermute | solution.py:35
  132.7 4.5 %encoder_ffn_second.1 = (bf16[512,768]{1,0:T(8,128)(2,1)}, bf16[2,4,3,96,768]{4,3,2,1,0:T(8,128)(2,1)S(1)}, bf16[2,4,3,96,768]{4,3,2,1,0:T(8,128)(2,1)S(1)}) custom-call(s32[3]{0:T(128)S(1)} %copy-done.34, bf16[512,768]{1,0:T(8,128)(2,1)S(1)} %get-tuple-element.156.c_all, bf16[512,768]{1,0:T(8,128)(2,1)S(1)} %get-tuple-element.157.g_all, ...), custom_call_target="tpu_custom_call" | custom-call | bytes 1024 | tf_op jit(solution)/shard_map/encoder_ffn_second/pallas_call | solution.py:559
  140.8 12.9 %encoder_backward.1 = (f32[128,768]{1,0:T(8,128)}, f32[1,768]{1,0:T(1,128)}, bf16[2,4,3,96,768]{4,3,2,1,0:T(8,128)(2,1)}, bf16[2,4,3,96,768]{4,3,2,1,0:T(8,128)(...) custom-call(s32[3]{0:T(128)} %pad_add_fusion.2.place_ref.refs_0_, ...), custom_call_target="tpu_custom_call", output_to_operand_aliasing={{2}: (16, {}), {3}: (17, {})} | custom-call | bytes 1024 | tf_op jit(solution)/shard_map/encoder_backward/pallas_call | solution.py:559
  154.1 6.3 %collective-permute-done.15 = bf16[2,4,3,96,768]{4,3,2,1,0:T(8,128)(2,1)} collective-permute-done((bf16[2,4,3,96,768]{4,3,2,1,0:T(8,128)(2,1)}, bf16[2,4,3,96,768]{4,3,2,1,0:T(8,128)(2,1)}, u32[]{:S(2)}, u32[]{:S(2)}) %collective-permute-start.15) | collective-permute-done | bytes 3538976 | tf_op jit(solution)/shard_map/ppermute | solution.py:44
  160.4 5.7 %fusion.5 = (bf16[2,3,96,768]{3,2,1,0:T(8,128)(2,1)}, bf16[2,3,96,768]{3,2,1,0:T(8,128)(2,1)}, bf16[2,3,96,768]{3,2,1,0:T(8,128)(2,1)}, bf16[2,3,96,768]{3,2,1,0:T(8,128)(2,1)}) fusion(bf16[2,4,3,96,768]{4,3,2,1,0:T(8,128)(2,1)} %collective-permute-done.15, bf16[2,4,3,96,768]{4,3,2,1,0:T(8,128)(2,1)} %get-tuple-element.171), kind=kLoop, calls=%fused_computation.21 | loop fusion | flops 7077888 | bytes 10616832 | tf_op jit(solution)/shard_map/convert_element_type | solution.py:59
  169.1 7.0 %self_forward.1 = (f32[128,768]{1,0:T(8,128)}, bf16[128,768]{1,0:T(8,128)(2,1)}, bf16[128,768]{1,0:T(8,128)(2,1)}, bf16[4,128,192]{2,1,0:T(8,128)(2,1)}, bf16[4,...) custom-call(s32[3]{0:T(128)} %pad_add_fusion.2.place_ref.refs_0_, bf16[128,768]{1,0:T(8,128)(2,1)} %refs_2_.5, ...), custom_call_target="tpu_custom_call" | custom-call | bytes 1024 | tf_op jit(solution)/shard_map/self_forward/pallas_call | solution.py:559
  176.1 6.5 %cross_forward.1 = (f32[128,768]{1,0:T(8,128)}, bf16[128,768]{1,0:T(8,128)(2,1)}, bf16[128,768]{1,0:T(8,128)(2,1)}, bf16[4,128,192]{2,1,0:T(8,128)(2,1)}, bf16[4...) custom-call(s32[3]{0:T(128)} %pad_add_fusion.2.place_ref.refs_0_, f32[128,768]{1,0:T(8,128)} %get-tuple-element.181.refs_1_.refs_7_, ...), custom_call_target="tpu_custom_call" | custom-call | bytes 1024 | tf_op jit(solution)/shard_map/cross_forward/pallas_call | solution.py:559
  182.7 3.4 collective-permute-start.21
  189.3 2.5 collective-permute-done.21.c1
  191.8 12.3 %collective-permute-done.22.c2 = bf16[128,768]{1,0:T(8,128)(2,1)S(1)} collective-permute-done((bf16[128,768]{1,0:T(8,128)(2,1)}, bf16[128,768]{1,0:T(8,128)(2,1)S(1)}, u32[]{:S(2)}, u32[]{:S(2)}) %collective-permute-start.22) | collective-permute-done | bytes 196640 | tf_op jit(solution)/shard_map/ppermute | solution.py:35
  205.0 3.3 decoder_ffn_first.1
  212.0 3.6 decoder_ffn_second.1
  219.1 2.8 collective-permute-start.28
  227.2 5.7 %collective-permute-done.27.refs_3_ = bf16[128,768]{1,0:T(8,128)(2,1)S(1)} collective-permute-done((bf16[128,768]{1,0:T(8,128)(2,1)S(1)}, bf16[128,768]{1,0:T(8,128)(2,1)S(1)}, u32[]{:S(2)}, u32[]{:S(2)}) %collective-permute-start.27) | collective-permute-done | bytes 196640 | tf_op jit(solution)/shard_map/ppermute | solution.py:40
  232.9 3.8 %collective-permute-start.29 = (bf16[96,768]{1,0:T(8,128)(2,1)S(1)}, bf16[96,768]{1,0:T(8,128)(2,1)S(1)}, u32[]{:S(2)}, u32[]{:S(2)}) collective-permute-start(bf16[96,768]{1,0:T(8,128)(2,1)S(1)} %slice_bitcast_fusion.14), channel_id=1, source_target_pairs={{0,1},{1,2},{2,3},{3,0},{4,5},{5,6},{6,7},{7,4},{8,9},{9,10},{10,1... | collective-permute-start | bytes 442376 | tf_op jit(solution)/shard_map/ppermute | solution.py:40
  239.2 10.6 %cross_backward.1 = (f32[128,768]{1,0:T(8,128)}, f32[1,768]{1,0:T(1,128)}, bf16[2,4,3,96,768]{4,3,2,1,0:T(8,128)(2,1)}, bf16[2,4,3,96,768]{4,3,2,1,0:T(8,128)(2,...) custom-call(s32[3]{0:T(128)} %pad_add_fusion.2.place_ref.refs_0_, ...), custom_call_target="tpu_custom_call", output_to_operand_aliasing={{2}: (15, {}), {3}: (16, {})} | custom-call | bytes 1024 | tf_op jit(solution)/shard_map/cross_backward/pallas_call | solution.py:559
  249.9 6.4 %collective-permute-done.32 = bf16[2,4,3,96,768]{4,3,2,1,0:T(8,128)(2,1)S(1)} collective-permute-done((bf16[2,4,3,96,768]{4,3,2,1,0:T(8,128)(2,1)}, bf16[2,4,3,96,768]{4,3,2,1,0:T(8,128)(2,1)S(1)}, u32[]{:S(2)}, u32[]{:S(2)}) %collective-permute-start.32) | collective-permute-done | bytes 3538976 | tf_op jit(solution)/shard_map/ppermute | solution.py:44
  256.4 4.5 %fusion.9 = (bf16[2,3,96,768]{3,2,1,0:T(8,128)(2,1)}, bf16[2,3,96,768]{3,2,1,0:T(8,128)(2,1)S(1)}, bf16[2,3,96,768]{3,2,1,0:T(8,128)(2,1)}, bf16[2,3,96,768]{3,2,1,0:T(8,128)(2,1)S(1)}) fusion(bf16[2,4,3,96,768]{4,3,2,1,0:T(8,128)(2,1)S(1)} %collective-permute-done.32, bf16[2,4,3,96,768]{4,3,2,1,0:T(8,128)(2,1)} %get-tuple-element.203), kind=kLoop, calls=%fused_computation.25 | loop fusion | flops 7077888 | bytes 10616832 | tf_op jit(solution)/shard_map/convert_element_type | solution.py:59
  268.8 10.5 %self_backward.1 = (f32[128,768]{1,0:T(8,128)}, f32[1,768]{1,0:T(1,128)}, bf16[2,4,2,96,768]{4,3,2,1,0:T(8,128)(2,1)}, bf16[2,4,2,96,768]{4,3,2,1,0:T(8,128)(2,1)}, f32[12,32,8,128]{3,2,1,0:T(8,128)}) custom-call(s32[3]{0:T(128)} %pad_add_fusion.2.place_ref.refs_0_, f32[128,768]{1,0:T(8,128)} %get-tuple-element.210.refs_1_, bf16[128,768]{1,0:T(8,128)(2,1)} %refs_2_.5, ...), custom_call_target="tpu_custom_call" | custom-call | bytes 1024 | tf_op jit(solution)/shard_map/self_backward/pallas_call | solution.py:559
  279.4 2.7 collective-permute-done.36
  292.1 1.9 fusion.13
  296.1 3.7 %collective-permute-done.43 = bf16[3,96,768]{2,1,0:T(8,128)(2,1)S(1)} collective-permute-done((bf16[3,96,768]{2,1,0:T(8,128)(2,1)S(1)}, bf16[3,96,768]{2,1,0:T(8,128)(2,1)S(1)}, u32[]{:S(2)}, u32[]{:S(2)}) %collective-permute-start.43) | collective-permute-done | bytes 442400 | tf_op jit(solution)/shard_map/ppermute | solution.py:44
  301.0 3.0 collective-permute-start.44
  306.5 12.9 %collective-permute-done.40 = f32[64,128]{1,0:T(8,128)S(1)} collective-permute-done((f32[64,128]{1,0:T(8,128)S(1)}, f32[64,128]{1,0:T(8,128)S(1)}, u32[]{:S(2)}, u32[]{:S(2)}) %collective-permute-start.40) | collective-permute-done | bytes 32800 | tf_op jit(solution)/shard_map/ppermute | solution.py:146
  322.4 6.2 %all-gather.6.cloned.1.call-done.used_ref = bf16[1280,896]{1,0:T(8,128)(2,1)} async-done(((bf16[40,896]{1,0:T(8,128)(2,1)}), bf16[1280,896]{1,0:T(8,128)(2,1)}) %all-gather.6.cloned.1.call-update) | async-done | bytes 2293776 | tf_op jit(solution)/shard_map/all_gather | solution.py:880
  333.6 5.5 %collective-permute-done.48 = bf16[2,96,768]{2,1,0:T(8,128)(2,1)S(1)} collective-permute-done((bf16[2,96,768]{2,1,0:T(8,128)(2,1)S(1)}, bf16[2,96,768]{2,1,0:T(8,128)(2,1)S(1)}, u32[]{:S(2)}, u32[]{:S(2)}) %collective-permute-start.48) | collective-permute-done | bytes 294944 | tf_op jit(solution)/shard_map/ppermute | solution.py:44
  346.4 2.2 collective-permute-start.54
  352.0 2.5 table.1
  356.1 6.5 %collective-permute-done.52 = f32[64,128]{1,0:T(8,128)S(1)} collective-permute-done((f32[64,128]{1,0:T(8,128)S(1)}, f32[64,128]{1,0:T(8,128)S(1)}, u32[]{:S(2)}, u32[]{:S(2)}) %collective-permute-start.52) | collective-permute-done | bytes 32800 | tf_op jit(solution)/shard_map/ppermute | solution.py:146
  364.7 1.9 matrices.4
  (306 shorter events, 96.9 us)
Async XLA Ops:
  7.2 67.6 %all-gather.8.cloned.1.call-start = ((), (), s32[]{:S(2)}) async-start(), calls=%async_computation.3 | async-start | bytes 5308416 | tf_op jit(solution)/shard_map/all_gather | solution.py:139
  10.5 10.1 %collective-permute-start.5 = (bf16[96,768]{1,0:T(8,128)(2,1)}, bf16[96,768]{1,0:T(8,128)(2,1)S(1)}, u32[]{:S(2)}, u32[]{:S(2)}) collective-permute-start(bf16[96,768]{1,0:T(8,128)(2,1)} %get-tuple-element.150), channel_id=1, source_target_pairs={{0,1},{1,2},{2,3},{3,0},{4,5},{5,6},{6,7},{7,4},{8,9},{9,10},{10,1... | collective-permute-start | bytes 442376 | tf_op jit(solution)/shard_map/ppermute | solution.py:35
  13.6 12.5 %collective-permute-start.4 = (bf16[96,768]{1,0:T(8,128)(2,1)}, bf16[96,768]{1,0:T(8,128)(2,1)S(1)}, u32[]{:S(2)}, u32[]{:S(2)}) collective-permute-start(bf16[96,768]{1,0:T(8,128)(2,1)} %get-tuple-element.150), channel_id=1, source_target_pairs={{0,2},{1,3},{2,0},{3,1},{4,6},{5,7},{6,4},{7,5},{8,10},{9,11},{10,... | collective-permute-start | bytes 442376 | tf_op jit(solution)/shard_map/ppermute | solution.py:35
  28.0 141.2 %all-gather.10.cloned.1.call-start = ((), (), s32[]{:S(2)}) async-start(), calls=%async_computation.4 | async-start | bytes 10616832 | tf_op jit(solution)/shard_map/all_gather | solution.py:139
  28.0 19.6 %collective-permute-start = (bf16[128,768]{1,0:T(8,128)(2,1)S(1)}, bf16[128,768]{1,0:T(8,128)(2,1)S(1)}, u32[]{:S(2)}, u32[]{:S(2)}) collective-permute-start(bf16[128,768]{1,0:T(8,128)(2,1)S(1)} %copy-done.16), channel_id=1, source_target_pairs={{0,3},{1,0},{2,1},{3,2},{4,7},{5,4},{6,5},{7,6},{8,11},{9,8},{10,9... | collective-permute-start | bytes 589832 | tf_op jit(solution)/shard_map/ppermute | solution.py:35
  32.8 17.9 %collective-permute-start.1 = (bf16[128,768]{1,0:T(8,128)(2,1)S(1)}, bf16[128,768]{1,0:T(8,128)(2,1)}, u32[]{:S(2)}, u32[]{:S(2)}) collective-permute-start(bf16[128,768]{1,0:T(8,128)(2,1)S(1)} %copy-done.16), channel_id=1, source_target_pairs={{0,2},{1,3},{2,0},{3,1},{4,6},{5,7},{6,4},{7,5},{8,10},{9,11},{10,... | collective-permute-start | bytes 589832 | tf_op jit(solution)/shard_map/ppermute | solution.py:35
  33.2 17.5 %collective-permute-start.2 = (bf16[128,768]{1,0:T(8,128)(2,1)S(1)}, bf16[128,768]{1,0:T(8,128)(2,1)}, u32[]{:S(2)}, u32[]{:S(2)}) collective-permute-start(bf16[128,768]{1,0:T(8,128)(2,1)S(1)} %copy-done.16), channel_id=1, source_target_pairs={{0,1},{1,2},{2,3},{3,0},{4,5},{5,6},{6,7},{7,4},{8,9},{9,10},{10,1... | collective-permute-start | bytes 589832 | tf_op jit(solution)/shard_map/ppermute | solution.py:35
  50.7 11.8 %collective-permute-start.18 = (bf16[2,96,768]{2,1,0:T(8,128)(2,1)S(1)}, bf16[2,96,768]{2,1,0:T(8,128)(2,1)S(1)}, u32[]{:S(2)}, u32[]{:S(2)}) collective-permute-start(bf16[2,96,768]{2,1,0:T(8,128)(2,1)S(1)} %copy-done.54), channel_id=1, source_target_pairs={{0,1},{1,2},{2,3},{3,0},{4,5},{5,6},{6,7},{7,4},{8,9},{9,10},{10,1... | collective-permute-start | bytes 884744 | tf_op jit(solution)/shard_map/ppermute | solution.py:35
  50.7 22.7 %collective-permute-start.17 = (bf16[2,96,768]{2,1,0:T(8,128)(2,1)S(1)}, bf16[2,96,768]{2,1,0:T(8,128)(2,1)S(1)}, u32[]{:S(2)}, u32[]{:S(2)}) collective-permute-start(bf16[2,96,768]{2,1,0:T(8,128)(2,1)S(1)} %copy-done.54), channel_id=1, source_target_pairs={{0,2},{1,3},{2,0},{3,1},{4,6},{5,7},{6,4},{7,5},{8,10},{9,11},{10,... | collective-permute-start | bytes 884744 | tf_op jit(solution)/shard_map/ppermute | solution.py:35
  51.9 21.6 %collective-permute-start.16 = (bf16[2,96,768]{2,1,0:T(8,128)(2,1)S(1)}, bf16[2,96,768]{2,1,0:T(8,128)(2,1)S(1)}, u32[]{:S(2)}, u32[]{:S(2)}) collective-permute-start(bf16[2,96,768]{2,1,0:T(8,128)(2,1)S(1)} %copy-done.54), channel_id=1, source_target_pairs={{0,3},{1,0},{2,1},{3,2},{4,7},{5,4},{6,5},{7,6},{8,11},{9,8},{10,9... | collective-permute-start | bytes 884744 | tf_op jit(solution)/shard_map/ppermute | solution.py:35
  74.7 112.3 %reduce-scatter.2.cloned.1.call-start = ((), (), s32[]{:S(2)}) async-start(), calls=%async_computation.1 | async-start | bytes 983040 | tf_op jit(solution)/shard_map/reduce_scatter | solution.py:853
  82.3 11.9 %collective-permute-start.6 = (bf16[128,768]{1,0:T(8,128)(2,1)}, bf16[128,768]{1,0:T(8,128)(2,1)S(1)}, u32[]{:S(2)}, u32[]{:S(2)}) collective-permute-start(bf16[128,768]{1,0:T(8,128)(2,1)} %get-tuple-element.155.c0), channel_id=1, source_target_pairs={{0,3},{1,0},{2,1},{3,2},{4,7},{5,4},{6,5},{7,6},{8,11},{9,8},{10,9... | collective-permute-start | bytes 589832 | tf_op jit(solution)/shard_map/ppermute | solution.py:35
  88.6 17.9 %collective-permute-start.7 = (bf16[128,768]{1,0:T(8,128)(2,1)}, bf16[128,768]{1,0:T(8,128)(2,1)S(1)}, u32[]{:S(2)}, u32[]{:S(2)}) collective-permute-start(bf16[128,768]{1,0:T(8,128)(2,1)} %get-tuple-element.155.c0), channel_id=1, source_target_pairs={{0,2},{1,3},{2,0},{3,1},{4,6},{5,7},{6,4},{7,5},{8,10},{9,11},{10,... | collective-permute-start | bytes 589832 | tf_op jit(solution)/shard_map/ppermute | solution.py:35
  89.8 16.7 %collective-permute-start.8 = (bf16[128,768]{1,0:T(8,128)(2,1)}, bf16[128,768]{1,0:T(8,128)(2,1)S(1)}, u32[]{:S(2)}, u32[]{:S(2)}) collective-permute-start(bf16[128,768]{1,0:T(8,128)(2,1)} %get-tuple-element.155.c0), channel_id=1, source_target_pairs={{0,1},{1,2},{2,3},{3,0},{4,5},{5,6},{6,7},{7,4},{8,9},{9,10},{10,1... | collective-permute-start | bytes 589832 | tf_op jit(solution)/shard_map/ppermute | solution.py:35
  111.0 15.5 %collective-permute-start.10 = (bf16[128,768]{1,0:T(8,128)(2,1)S(1)}, bf16[128,768]{1,0:T(8,128)(2,1)S(1)}, u32[]{:S(2)}, u32[]{:S(2)}) collective-permute-start(bf16[128,768]{1,0:T(8,128)(2,1)S(1)} %get-tuple-element.382), channel_id=1, source_target_pairs={{0,2},{1,3},{2,0},{3,1},{4,6},{5,7},{6,4},{7,5},{8,10},{9,11},{10,... | collective-permute-start | bytes 589832 | tf_op jit(solution)/shard_map/ppermute | solution.py:40
  111.6 14.9 %collective-permute-start.11 = (bf16[128,768]{1,0:T(8,128)(2,1)S(1)}, bf16[128,768]{1,0:T(8,128)(2,1)S(1)}, u32[]{:S(2)}, u32[]{:S(2)}) collective-permute-start(bf16[128,768]{1,0:T(8,128)(2,1)S(1)} %get-tuple-element.381), channel_id=1, source_target_pairs={{0,3},{1,0},{2,1},{3,2},{4,7},{5,4},{6,5},{7,6},{8,11},{9,8},{10,9... | collective-permute-start | bytes 589832 | tf_op jit(solution)/shard_map/ppermute | solution.py:40
  126.6 27.2 %collective-permute-start.12 = (bf16[128,768]{1,0:T(8,128)(2,1)S(1)}, bf16[128,768]{1,0:T(8,128)(2,1)S(1)}, u32[]{:S(2)}, u32[]{:S(2)}) collective-permute-start(bf16[128,768]{1,0:T(8,128)(2,1)S(1)} %copy-done.17), channel_id=1, source_target_pairs={{0,3},{1,0},{2,1},{3,2},{4,7},{5,4},{6,5},{7,6},{8,11},{9,8},{10,9... | collective-permute-start | bytes 589832 | tf_op jit(solution)/shard_map/ppermute | solution.py:35
  131.6 22.2 %collective-permute-start.13 = (bf16[128,768]{1,0:T(8,128)(2,1)S(1)}, bf16[128,768]{1,0:T(8,128)(2,1)S(1)}, u32[]{:S(2)}, u32[]{:S(2)}) collective-permute-start(bf16[128,768]{1,0:T(8,128)(2,1)S(1)} %copy-done.17), channel_id=1, source_target_pairs={{0,2},{1,3},{2,0},{3,1},{4,6},{5,7},{6,4},{7,5},{8,10},{9,11},{10,... | collective-permute-start | bytes 589832 | tf_op jit(solution)/shard_map/ppermute | solution.py:35
  131.8 21.9 %collective-permute-start.14 = (bf16[128,768]{1,0:T(8,128)(2,1)S(1)}, bf16[128,768]{1,0:T(8,128)(2,1)S(1)}, u32[]{:S(2)}, u32[]{:S(2)}) collective-permute-start(bf16[128,768]{1,0:T(8,128)(2,1)S(1)} %copy-done.17), channel_id=1, source_target_pairs={{0,1},{1,2},{2,3},{3,0},{4,5},{5,6},{6,7},{7,4},{8,9},{9,10},{10,1... | collective-permute-start | bytes 589832 | tf_op jit(solution)/shard_map/ppermute | solution.py:35
  153.9 174.7 %all-gather.6.cloned.1.call-start = ((), (), s32[]{:S(2)}) async-start(), calls=%async_computation.2 | async-start | bytes 2365440 | tf_op jit(solution)/shard_map/all_gather | solution.py:880
  166.1 22.0 %collective-permute-start.19 = (bf16[2,3,96,768]{3,2,1,0:T(8,128)(2,1)}, bf16[2,3,96,768]{3,2,1,0:T(8,128)(2,1)}, u32[]{:S(2)}, u32[]{:S(2)}) collective-permute-start(bf16[2,3,96,768]{3,2,1,0:T(8,128)(2,1)} %get-tuple-element.362), channel_id=1, source_target_pairs={{0,8},{4,12},{8,0},{12,4},{16,24},{20,28},{24,16},{28,20},{1,9},{5... | collective-permute-start | bytes 2654216 | tf_op jit(solution)/shard_map/ppermute | solution.py:44
  167.6 21.7 %collective-permute-start.20 = (bf16[2,3,96,768]{3,2,1,0:T(8,128)(2,1)}, bf16[2,3,96,768]{3,2,1,0:T(8,128)(2,1)}, u32[]{:S(2)}, u32[]{:S(2)}) collective-permute-start(bf16[2,3,96,768]{3,2,1,0:T(8,128)(2,1)} %get-tuple-element.360), channel_id=1, source_target_pairs={{0,16},{4,20},{8,24},{12,28},{16,0},{20,4},{24,8},{28,12},{1,17},{... | collective-permute-start | bytes 2654216 | tf_op jit(solution)/shard_map/ppermute | solution.py:44
  186.1 18.0 %collective-permute-start.22 = (bf16[128,768]{1,0:T(8,128)(2,1)}, bf16[128,768]{1,0:T(8,128)(2,1)S(1)}, u32[]{:S(2)}, u32[]{:S(2)}) collective-permute-start(bf16[128,768]{1,0:T(8,128)(2,1)} %get-tuple-element.183.c0), channel_id=1, source_target_pairs={{0,2},{1,3},{2,0},{3,1},{4,6},{5,7},{6,4},{7,5},{8,10},{9,11},{10,... | collective-permute-start | bytes 589832 | tf_op jit(solution)/shard_map/ppermute | solution.py:35
  186.9 17.2 %collective-permute-start.23 = (bf16[128,768]{1,0:T(8,128)(2,1)}, bf16[128,768]{1,0:T(8,128)(2,1)}, u32[]{:S(2)}, u32[]{:S(2)}) collective-permute-start(bf16[128,768]{1,0:T(8,128)(2,1)} %get-tuple-element.183.c0), channel_id=1, source_target_pairs={{0,1},{1,2},{2,3},{3,0},{4,5},{5,6},{6,7},{7,4},{8,9},{9,10},{10,1... | collective-permute-start | bytes 589832 | tf_op jit(solution)/shard_map/ppermute | solution.py:35
  209.6 12.3 %collective-permute-start.25 = (bf16[3,96,768]{2,1,0:T(8,128)(2,1)S(1)}, bf16[3,96,768]{2,1,0:T(8,128)(2,1)S(1)}, u32[]{:S(2)}, u32[]{:S(2)}) collective-permute-start(bf16[3,96,768]{2,1,0:T(8,128)(2,1)S(1)} %fusion.17), channel_id=1, source_target_pairs={{0,8},{4,12},{8,0},{12,4},{16,24},{20,28},{24,16},{28,20},{1,9},{5... | collective-permute-start | bytes 1327112 | tf_op jit(solution)/shard_map/ppermute | solution.py:44
  211.4 12.5 %collective-permute-start.24 = (bf16[3,96,768]{2,1,0:T(8,128)(2,1)S(1)}, bf16[3,96,768]{2,1,0:T(8,128)(2,1)S(1)}, u32[]{:S(2)}, u32[]{:S(2)}) collective-permute-start(bf16[3,96,768]{2,1,0:T(8,128)(2,1)S(1)} %fusion.16), channel_id=1, source_target_pairs={{0,16},{4,20},{8,24},{12,28},{16,0},{20,4},{24,8},{28,12},{1,17},{... | collective-permute-start | bytes 1327112 | tf_op jit(solution)/shard_map/ppermute | solution.py:44
  217.5 15.4 %collective-permute-start.27 = (bf16[128,768]{1,0:T(8,128)(2,1)S(1)}, bf16[128,768]{1,0:T(8,128)(2,1)S(1)}, u32[]{:S(2)}, u32[]{:S(2)}) collective-permute-start(bf16[128,768]{1,0:T(8,128)(2,1)S(1)} %get-tuple-element.379), channel_id=1, source_target_pairs={{0,2},{1,3},{2,0},{3,1},{4,6},{5,7},{6,4},{7,5},{8,10},{9,11},{10,... | collective-permute-start | bytes 589832 | tf_op jit(solution)/shard_map/ppermute | solution.py:40
  219.1 13.8 %collective-permute-start.28 = (bf16[128,768]{1,0:T(8,128)(2,1)S(1)}, bf16[128,768]{1,0:T(8,128)(2,1)S(1)}, u32[]{:S(2)}, u32[]{:S(2)}) collective-permute-start(bf16[128,768]{1,0:T(8,128)(2,1)S(1)} %get-tuple-element.378), channel_id=1, source_target_pairs={{0,3},{1,0},{2,1},{3,2},{4,7},{5,4},{6,5},{7,6},{8,11},{9,8},{10,9... | collective-permute-start | bytes 589832 | tf_op jit(solution)/shard_map/ppermute | solution.py:40
  232.9 16.9 %collective-permute-start.29 = (bf16[96,768]{1,0:T(8,128)(2,1)S(1)}, bf16[96,768]{1,0:T(8,128)(2,1)S(1)}, u32[]{:S(2)}, u32[]{:S(2)}) collective-permute-start(bf16[96,768]{1,0:T(8,128)(2,1)S(1)} %slice_bitcast_fusion.14), channel_id=1, source_target_pairs={{0,1},{1,2},{2,3},{3,0},{4,5},{5,6},{6,7},{7,4},{8,9},{9,10},{10,1... | collective-permute-start | bytes 442376 | tf_op jit(solution)/shard_map/ppermute | solution.py:40
  236.7 13.2 %collective-permute-start.30 = (bf16[96,768]{1,0:T(8,128)(2,1)S(1)}, bf16[96,768]{1,0:T(8,128)(2,1)S(1)}, u32[]{:S(2)}, u32[]{:S(2)}) collective-permute-start(bf16[96,768]{1,0:T(8,128)(2,1)S(1)} %get-tuple-element.206), channel_id=1, source_target_pairs={{0,2},{1,3},{2,0},{3,1},{4,6},{5,7},{6,4},{7,5},{8,10},{9,11},{10,... | collective-permute-start | bytes 442376 | tf_op jit(solution)/shard_map/ppermute | solution.py:40
  238.5 11.3 %collective-permute-start.31 = (bf16[96,768]{1,0:T(8,128)(2,1)S(1)}, bf16[96,768]{1,0:T(8,128)(2,1)S(1)}, u32[]{:S(2)}, u32[]{:S(2)}) collective-permute-start(bf16[96,768]{1,0:T(8,128)(2,1)S(1)} %get-tuple-element.207), channel_id=1, source_target_pairs={{0,3},{1,0},{2,1},{3,2},{4,7},{5,4},{6,5},{7,6},{8,11},{9,8},{10,9... | collective-permute-start | bytes 442376 | tf_op jit(solution)/shard_map/ppermute | solution.py:40
  260.8 22.6 %collective-permute-start.33 = (bf16[2,3,96,768]{3,2,1,0:T(8,128)(2,1)}, bf16[2,3,96,768]{3,2,1,0:T(8,128)(2,1)}, u32[]{:S(2)}, u32[]{:S(2)}) collective-permute-start(bf16[2,3,96,768]{3,2,1,0:T(8,128)(2,1)} %get-tuple-element.358), channel_id=1, source_target_pairs={{0,8},{4,12},{8,0},{12,4},{16,24},{20,28},{24,16},{28,20},{1,9},{5... | collective-permute-start | bytes 2654216 | tf_op jit(solution)/shard_map/ppermute | solution.py:44
  262.4 22.2 %collective-permute-start.34 = (bf16[2,3,96,768]{3,2,1,0:T(8,128)(2,1)}, bf16[2,3,96,768]{3,2,1,0:T(8,128)(2,1)}, u32[]{:S(2)}, u32[]{:S(2)}) collective-permute-start(bf16[2,3,96,768]{3,2,1,0:T(8,128)(2,1)} %get-tuple-element.356), channel_id=1, source_target_pairs={{0,16},{4,20},{8,24},{12,28},{16,0},{20,4},{24,8},{28,12},{1,17},{... | collective-permute-start | bytes 2654216 | tf_op jit(solution)/shard_map/ppermute | solution.py:44
  264.6 14.9 %collective-permute-start.35 = (bf16[128,768]{1,0:T(8,128)(2,1)S(1)}, bf16[128,768]{1,0:T(8,128)(2,1)S(1)}, u32[]{:S(2)}, u32[]{:S(2)}) collective-permute-start(bf16[128,768]{1,0:T(8,128)(2,1)S(1)} %get-tuple-element.220), channel_id=1, source_target_pairs={{0,1},{1,2},{2,3},{3,0},{4,5},{5,6},{6,7},{7,4},{8,9},{9,10},{10,1... | collective-permute-start | bytes 589832 | tf_op jit(solution)/shard_map/ppermute | solution.py:40
  266.2 16.0 %collective-permute-start.36 = (bf16[128,768]{1,0:T(8,128)(2,1)S(1)}, bf16[128,768]{1,0:T(8,128)(2,1)S(1)}, u32[]{:S(2)}, u32[]{:S(2)}) collective-permute-start(bf16[128,768]{1,0:T(8,128)(2,1)S(1)} %get-tuple-element.221), channel_id=1, source_target_pairs={{0,2},{1,3},{2,0},{3,1},{4,6},{5,7},{6,4},{7,5},{8,10},{9,11},{10,... | collective-permute-start | bytes 589832 | tf_op jit(solution)/shard_map/ppermute | solution.py:40
  267.2 15.1 %collective-permute-start.37 = (bf16[128,768]{1,0:T(8,128)(2,1)S(1)}, bf16[128,768]{1,0:T(8,128)(2,1)S(1)}, u32[]{:S(2)}, u32[]{:S(2)}) collective-permute-start(bf16[128,768]{1,0:T(8,128)(2,1)S(1)} %get-tuple-element.222), channel_id=1, source_target_pairs={{0,3},{1,0},{2,1},{3,2},{4,7},{5,4},{6,5},{7,6},{8,11},{9,8},{10,9... | collective-permute-start | bytes 589832 | tf_op jit(solution)/shard_map/ppermute | solution.py:40
  285.7 14.1 %collective-permute-start.43 = (bf16[3,96,768]{2,1,0:T(8,128)(2,1)S(1)}, bf16[3,96,768]{2,1,0:T(8,128)(2,1)S(1)}, u32[]{:S(2)}, u32[]{:S(2)}) collective-permute-start(bf16[3,96,768]{2,1,0:T(8,128)(2,1)S(1)} %fusion.18), channel_id=1, source_target_pairs={{0,16},{4,20},{8,24},{12,28},{16,0},{20,4},{24,8},{28,12},{1,17},{... | collective-permute-start | bytes 1327112 | tf_op jit(solution)/shard_map/ppermute | solution.py:44
  288.4 15.6 %collective-permute-start.45 = (bf16[3,96,768]{2,1,0:T(8,128)(2,1)S(1)}, bf16[3,96,768]{2,1,0:T(8,128)(2,1)S(1)}, u32[]{:S(2)}, u32[]{:S(2)}) collective-permute-start(bf16[3,96,768]{2,1,0:T(8,128)(2,1)S(1)} %fusion.19), channel_id=1, source_target_pairs={{0,8},{4,12},{8,0},{12,4},{16,24},{20,28},{24,16},{28,20},{1,9},{5... | collective-permute-start | bytes 1327112 | tf_op jit(solution)/shard_map/ppermute | solution.py:44
  294.1 34.6 %collective-permute-start.42 = (bf16[2,2,96,768]{3,2,1,0:T(8,128)(2,1)}, bf16[2,2,96,768]{3,2,1,0:T(8,128)(2,1)}, u32[]{:S(2)}, u32[]{:S(2)}) collective-permute-start(bf16[2,2,96,768]{3,2,1,0:T(8,128)(2,1)} %get-tuple-element.366), channel_id=1, source_target_pairs={{0,8},{4,12},{8,0},{12,4},{16,24},{20,28},{24,16},{28,20},{1,9},{5... | collective-permute-start | bytes 1769480 | tf_op jit(solution)/shard_map/ppermute | solution.py:44
  295.6 36.2 %collective-permute-start.49 = (bf16[2,2,96,768]{3,2,1,0:T(8,128)(2,1)}, bf16[2,2,96,768]{3,2,1,0:T(8,128)(2,1)}, u32[]{:S(2)}, u32[]{:S(2)}) collective-permute-start(bf16[2,2,96,768]{3,2,1,0:T(8,128)(2,1)} %get-tuple-element.364), channel_id=1, source_target_pairs={{0,16},{4,20},{8,24},{12,28},{16,0},{20,4},{24,8},{28,12},{1,17},{... | collective-permute-start | bytes 1769480 | tf_op jit(solution)/shard_map/ppermute | solution.py:44
  301.0 19.9 %collective-permute-start.44 = (bf16[96,768]{1,0:T(8,128)(2,1)S(1)}, bf16[96,768]{1,0:T(8,128)(2,1)S(1)}, u32[]{:S(2)}, u32[]{:S(2)}) collective-permute-start(bf16[96,768]{1,0:T(8,128)(2,1)S(1)} %fusion.35), channel_id=1, source_target_pairs={{0,1},{1,2},{2,3},{3,0},{4,5},{5,6},{6,7},{7,4},{8,9},{9,10},{10,1... | collective-permute-start | bytes 442376 | tf_op jit(solution)/shard_map/ppermute | solution.py:40
  305.3 14.1 %collective-permute-start.40 = (f32[64,128]{1,0:T(8,128)S(1)}, f32[64,128]{1,0:T(8,128)S(1)}, u32[]{:S(2)}, u32[]{:S(2)}) collective-permute-start(f32[64,128]{1,0:T(8,128)S(1)} %add.237), channel_id=1, source_target_pairs={{0,8},{4,12},{8,0},{12,4},{16,24},{20,28},{24,16},{28,20},{1,9},{5... | collective-permute-start | bytes 98312 | tf_op jit(solution)/shard_map/ppermute | solution.py:146
  305.9 22.8 %collective-permute-start.46 = (bf16[96,768]{1,0:T(8,128)(2,1)S(1)}, bf16[96,768]{1,0:T(8,128)(2,1)S(1)}, u32[]{:S(2)}, u32[]{:S(2)}) collective-permute-start(bf16[96,768]{1,0:T(8,128)(2,1)S(1)} %get-tuple-element.371), channel_id=1, source_target_pairs={{0,2},{1,3},{2,0},{3,1},{4,6},{5,7},{6,4},{7,5},{8,10},{9,11},{10,... | collective-permute-start | bytes 442376 | tf_op jit(solution)/shard_map/ppermute | solution.py:40
  321.6 10.1 %collective-permute-start.41 = (f32[64,128]{1,0:T(8,128)S(1)}, f32[64,128]{1,0:T(8,128)S(1)}, u32[]{:S(2)}, u32[]{:S(2)}) collective-permute-start(f32[64,128]{1,0:T(8,128)S(1)} %add.238), channel_id=1, source_target_pairs={{0,16},{4,20},{8,24},{12,28},{16,0},{20,4},{24,8},{28,12},{1,17},{... | collective-permute-start | bytes 98312 | tf_op jit(solution)/shard_map/ppermute | solution.py:146
  345.2 19.5 %collective-permute-start.53 = (bf16[96,768]{1,0:T(8,128)(2,1)}, bf16[96,768]{1,0:T(8,128)(2,1)}, u32[]{:S(2)}, u32[]{:S(2)}) collective-permute-start(bf16[96,768]{1,0:T(8,128)(2,1)} %fusion.38), channel_id=1, source_target_pairs={{0,1},{1,2},{2,3},{3,0},{4,5},{5,6},{6,7},{7,4},{8,9},{9,10},{10,1... | collective-permute-start | bytes 442376 | tf_op jit(solution)/shard_map/ppermute | solution.py:40
  346.4 18.3 %collective-permute-start.54 = (bf16[96,768]{1,0:T(8,128)(2,1)}, bf16[96,768]{1,0:T(8,128)(2,1)}, u32[]{:S(2)}, u32[]{:S(2)}) collective-permute-start(bf16[96,768]{1,0:T(8,128)(2,1)} %get-tuple-element.385), channel_id=1, source_target_pairs={{0,2},{1,3},{2,0},{3,1},{4,6},{5,7},{6,4},{7,5},{8,10},{9,11},{10,... | collective-permute-start | bytes 442376 | tf_op jit(solution)/shard_map/ppermute | solution.py:40
  348.5 16.2 %collective-permute-start.55 = (bf16[96,768]{1,0:T(8,128)(2,1)}, bf16[96,768]{1,0:T(8,128)(2,1)}, u32[]{:S(2)}, u32[]{:S(2)}) collective-permute-start(bf16[96,768]{1,0:T(8,128)(2,1)} %get-tuple-element.384), channel_id=1, source_target_pairs={{0,3},{1,0},{2,1},{3,2},{4,7},{5,4},{6,5},{7,6},{8,11},{9,8},{10,9... | collective-permute-start | bytes 442376 | tf_op jit(solution)/shard_map/ppermute | solution.py:40
  350.2 12.5 %collective-permute-start.52 = (f32[64,128]{1,0:T(8,128)S(1)}, f32[64,128]{1,0:T(8,128)S(1)}, u32[]{:S(2)}, u32[]{:S(2)}) collective-permute-start(f32[64,128]{1,0:T(8,128)S(1)} %add.255), channel_id=1, source_target_pairs={{0,2},{1,3},{2,0},{3,1},{4,6},{5,7},{6,4},{7,5},{8,10},{9,11},{10,... | collective-permute-start | bytes 98312 | tf_op jit(solution)/shard_map/ppermute | solution.py:146
  (84 other events, 888.3 us)
Sparse Core Ops, SparseCore 0:
  28.1 41.2 all-gather.7
  74.8 62.7 all-gather.9
  154.0 24.4 reduce-scatter.1
  264.7 63.8 all-gather.5

commit v4 on v3

--- a/solution.py
+++ b/solution.py
@@ -139,10 +139,9 @@
     return lax.all_gather(slots, "dp", axis=0, axis_index_groups=groups, tiled=False)
 
 
-def sum_over(axis, array):
+def sum_bits(axis, array, bit, end):
     size = lax.axis_size(axis)
-    bit = 1
-    while bit < size:
+    while bit < end:
         array = array + lax.ppermute(array, axis, [(i, i ^ bit) for i in range(size)])
         bit *= 2
     return array
@@ -465,6 +464,10 @@
     outs = refs[:-4]
     keep_ref, send_ref, stage, sems = refs[-4:]
     tokens = c_all.shape[0] // 4
+    if not across:
+        packed, *outs = outs
+        for out in outs[1:]:
+            out[tokens:, :] = packed[...]
     place = place_ref[0]
     copies = []
     for half, (left, right) in enumerate(((c_all, du_ref), (g_all, h_ref))):
@@ -491,7 +494,7 @@
                 row = pl.multiple_of((place_ref[1] + i) % 4 * tokens, tokens)
                 outs[0][pl.ds(row, tokens), at] = part.astype(bf16)
             else:
-                outs[i][:, at] = part.astype(outs[i].dtype)
+                outs[i][0:tokens, at] = part.astype(outs[i].dtype)
     wait_all(copies)
 
 
@@ -510,18 +513,22 @@
     merge[...] = total[:, 3 * width :].T
 
 
-def table_kernel(place_ref, used_ref, out_ref):
-    width = out_ref.shape[2]
-    rows, entries = used_ref.shape[0], out_ref.shape[0]
-    number = used_ref[:, width : width + 128].astype(f32)
-    entry = number[:, 0:1] * 32.0 + number[:, 1:2]
+def table_kernel(rows, place_ref, used_ref, out_ref):
+    entries = out_ref.shape[0]
+    size = used_ref.shape[1]
     first = (place_ref[2] * entries).astype(f32)
-    column = lax.broadcasted_iota(jnp.int32, (rows, entries), 1).astype(f32) + first
-    row = lax.broadcasted_iota(jnp.int32, (rows, entries), 0)
-    values = used_ref[:, :width]
+    row = lax.broadcasted_iota(jnp.int32, (PREFIX * entries, size), 0)
+    column = lax.broadcasted_iota(jnp.int32, (PREFIX * entries, size), 1)
+    wanted = (row % entries).astype(f32) + first
+    fits = jnp.logical_and(column % PREFIX == row // entries, column < rows)
+    total = jnp.zeros((PREFIX * entries, used_ref.shape[2]), f32)
+    for i in range(used_ref.shape[0]):
+        number = used_ref[i, :, 0:128].astype(f32)
+        entry = number[rows : rows + 1, :size] * 32.0 + number[rows + 1 : rows + 2, :size]
+        chosen = jnp.logical_and(entry == wanted, fits)
+        total = total + nn(jnp.where(chosen, 1.0, 0.0).astype(bf16), used_ref[i])
     for p in range(PREFIX):
-        chosen = jnp.logical_and(entry == column, row % PREFIX == p)
-        out_ref[:, p, :] = tn(jnp.where(chosen, 1.0, 0.0).astype(bf16), values)
+        out_ref[:, p, :] = total[p * entries : (p + 1) * entries]
 
 
 def pack_kernel(place_ref, *refs):
@@ -709,20 +716,23 @@
     )
 
 
-def ffn_second(name, across, place, c_all, g_all, h, du, narrow):
+def ffn_second(name, packed, place, c_all, g_all, h, du, narrow):
     every, width = c_all.shape
     hidden = h.shape[1]
     tokens = every // 4
     block = width // BLOCKS
+    across = packed is None
+    operands = [place, c_all, g_all, h, du, narrow]
     if across:
         outs = [((every, width), bf16)]
     else:
-        outs = [((tokens, width), f32)] + [((tokens, width), bf16)] * 3
+        operands.append(packed)
+        outs = [((tokens, width), f32)] + [((tokens + packed.shape[0], width), bf16)] * 3
     count = len(outs)
     return call(
         functools.partial(ffn_second_kernel, across),
         name + "_second",
-        [place, c_all, g_all, h, du, narrow],
+        operands,
         (0,),
         (),
         outs + [((2, 4, 3, block, hidden), bf16)] * 2,
@@ -815,8 +825,8 @@
     encoder_rel, encoder_twice = relative_bias(encoder_bucket, encoder_bias, heads_here)
     decoder_rel, decoder_twice = relative_bias(decoder_bucket, decoder_bias, heads_here)
     entry_rows = jnp.repeat(entries, PREFIX)
-    numbers = jnp.stack([entry_rows // 32, entry_rows % 32], axis=1).astype(bf16)
-    numbers = jnp.pad(numbers, ((0, 0), (0, 126)))
+    numbers = jnp.stack([entry_rows // 32, entry_rows % 32]).astype(bf16)
+    numbers = jnp.pad(numbers, ((0, -(prefix_rows + 2) % 16), (0, width - prefix_rows)))
     gains = call(
         gains_kernel,
         "gains",
@@ -848,7 +858,7 @@
     )
     encoder_dc = (dc_own, return_tokens(dc_rest))
     out, *grads = ffn_second(
-        "encoder_ffn", True, place_in, c_all, g_all, h, du, encoder_narrow
+        "encoder_ffn", None, after(place_in, encoder_dc[1][0]), c_all, g_all, h, du, encoder_narrow
     )
     encoder_out = lax.psum_scatter(out, "mp", scatter_dimension=0, tiled=True)
     decoder_g = gather_tokens(after(decoder_upstream, encoder_dc))
@@ -876,32 +886,32 @@
         grads,
     )
     encoder_got = swap_cores(after(send, decoder_g))
-    packed = jnp.concatenate([prefix_grad[:prefix_rows], numbers], axis=1)
-    used = lax.all_gather(packed, ("dp", "mp"), axis=0, tiled=True)
-    encoder_halves = fold_cores(keep, encoder_got)
+    packed = jnp.concatenate([prefix_grad[:prefix_rows], numbers])
+
+    self_r1, _, *self_stored = attention_forward(
+        "self", after(place_in, encoder_input_grad), decoder_input, None, gains, decoder_rel, decoder_weights
+    )
+    encoder_halves = fold_cores(after(keep, self_r1), encoder_got)
     encoder_once = send_once(encoder_halves)
-
-    self_r1, _, *self_stored = attention_forward(
-        "self", after(place_in, encoder_halves), decoder_input, None, gains, decoder_rel, decoder_weights
-    )
     cross_r2, decoder_c, *cross_stored = attention_forward(
-        "cross", place_in, self_r1, encoder_states, gains, None, decoder_weights
+        "cross", after(place_in, encoder_halves), self_r1, encoder_states, gains, None, decoder_weights
     )
     decoder_c = gather_tokens(decoder_c)
     c_all, g_all, h, du, dc_own, dc_rest = ffn_first(
         "decoder_ffn",
-        [after(decoder_c[0], encoder_once, encoder_out), *decoder_c[1:]],
+        [after(decoder_c[0], encoder_out), *decoder_c[1:]],
         decoder_g,
         decoder_widen,
         decoder_narrow,
     )
     decoder_dc = (dc_own, return_tokens(dc_rest))
-    encoder_last = fold_once(after(encoder_halves, dc_own), encoder_once)
+    encoder_last = fold_once(after(encoder_halves, decoder_dc[1][0]), encoder_once)
     encoder_twice_got = send_twice(encoder_last)
     out, *rest, keep, send = ffn_second(
-        "decoder_ffn", False, place_in, c_all, g_all, h, du, decoder_narrow
+        "decoder_ffn", packed, after(place_in, encoder_last), c_all, g_all, h, du, decoder_narrow
     )
     grads = [keep, send]
+
     encoder_sums = fold_twice(
         after(encoder_halves, out), encoder_once, encoder_twice_got
     )
@@ -926,6 +936,9 @@
     cross_halves = fold_cores(keep, cross_got)
     cross_once = send_once(cross_halves)
     decoder_out = [to_mp(part, i + 1) for i, part in enumerate(after(rest, cross_halves))]
+    tokens = cross_r2.shape[0]
+    used = jnp.stack([packed] + [part[tokens:] for part in decoder_out])
+    used = lax.all_gather(used, "dp", axis=0, tiled=False).reshape(-1, *packed.shape)
     decoder_input_grad, decoder_gain_grad, keep, send, decoder_bias_raw = attention_backward(
         "self",
         after(place_in, cross_halves),
@@ -948,7 +961,7 @@
         pack_kernel,
         "pack",
         [
-            after(place_in, cross_last),
+            place_in,
             encoder_gain_grad,
             encoder_later_grad,
             decoder_gain_grad,
@@ -962,16 +975,17 @@
         [((64, 128), f32)],
         [],
     )[0]
-    self_halves = fold_cores(keep, after(self_got, sums))
+    sums = sum_bits("mp", sums, 1, lax.axis_size("mp"))
+    self_halves = fold_cores(keep, after(self_got, sums, cross_last))
     self_once = send_once(self_halves)
     cross_sums = fold_twice(after(cross_halves, self_halves), cross_once, cross_twice_got)
     cross_sent = send_slots(cross_sums)
-    self_last = fold_once(after(self_halves, cross_sent, used), self_once)
+    sums = sum_bits("dp", after(sums, self_halves), 1, 2)
+    self_last = fold_once(after(self_halves, cross_sums), self_once)
     self_twice_got = send_twice(self_last)
-    sums = sum_over("dp", after(sums, self_halves))
-    self_sums = fold_twice(after(self_halves, sums), self_once, self_twice_got)
+    self_sums = fold_twice(after(self_halves, sums, cross_sent), self_once, self_twice_got)
     self_sent = send_slots(self_sums)
-    sums = sum_over("mp", after(sums, self_sums))
+    sums = sum_bits("dp", after(sums, self_sums), 2, lax.axis_size("dp"))
 
     def last(value):
         return after(value, self_sums)
@@ -982,7 +996,7 @@
     encoder_widen_grad, encoder_narrow_grad = two_matrices(*last(encoder_sums[4:]))
     table_rows = memory_table.shape[0] // (lax.axis_size("dp") * lax.axis_size("mp"))
     table_grad = call(
-        table_kernel,
+        functools.partial(table_kernel, prefix_rows),
         "table",
         [last(place_in), last(used)],
         (0,),
@@ -991,7 +1005,7 @@
         [],
     )[0]
     decoder_output = (
-        last(cross_r2) + out + sum(part.astype(f32) for part in decoder_out)
+        last(cross_r2) + out + sum(part[:tokens].astype(f32) for part in decoder_out)
     ).astype(bf16)
     decoder_widen_grad, decoder_narrow_grad = two_matrices(*last(cross_sums[4:]))
     self_mats = four_matrices(self_sums, self_sent)

time: 381 us -> 372 us (0.976)
  other arithmetic: 35.1 us -> 29 us
  waiting for transfers between devices: 137 us -> 132 us
    ppermute x5, waiting for transfers between devices: 19.5 us -> 5.71 us  [sum_bits(): lax.ppermute(array, axis, [(i, i ^ bit) for i in range(size)])]
    ppermute x18, waiting for transfers between devices: 21.6 us -> 30 us  [to_mp(): lax.ppermute(array, 'mp', [(i, (i + step) % size) for i in range(size)])]
    ppermute x18, starting transfers between devices: 28.2 us -> 21.2 us  [to_mp(): lax.ppermute(array, 'mp', [(i, (i + step) % size) for i in range(size)])]
    ppermute x5, starting transfers between devices: 3.15 us -> 9.6 us  [sum_bits(): lax.ppermute(array, axis, [(i, i ^ bit) for i in range(size)])]
    all_gather x1, waiting for transfers between devices: 6.18 us -> 0.01 us  [shards(): lax.all_gather(used, 'dp', axis=0, tiled=False).reshape(-1, *packed.shape)]
    ppermute x15, waiting for transfers between devices: 27.5 us -> 33.6 us  [swap_dp(): lax.ppermute(array, 'dp', [(i, i ^ bit) for i in range(lax.axis_size('dp'...]
    unnamed x148 -> x126, local copies, waits for them, and re-layouts: 11.8 us -> 14 us
  transfers between devices with their start and end apart: 60 -> 60, of which waited for: 27 -> 25; matrix products, arithmetic and copies ran while one was open for 11% -> 11% of each run, Pallas kernels for 19% -> 21%
where the time goes in v4:
time: 372 us; the launch traced here: 365 us
  waiting for transfers between devices  132 us (35%)
  Pallas kernels  79.9 us (21%)
  starting transfers between devices  78.6 us (21%)
  other arithmetic  29 us (8%)
  local copies, waits for them, and re-layouts  28.6 us (8%)
  between operations  15.3 us (4%)
    pallas_call x17, Pallas kernels, call(): pl.pallas_call(kernel, out_shape=[jax.ShapeDtypeStruct(shape, kind) for s...  79.9 us
    ppermute x18, waiting for transfers between devices, from_mp(): lax.ppermute(array, 'mp', [(i, (i - step) % size) for i in range(size)])  63 us
    ppermute x18, starting transfers between devices, from_mp(): lax.ppermute(array, 'mp', [(i, (i - step) % size) for i in range(size)])  34.1 us
    ppermute x15, waiting for transfers between devices, swap_dp(): lax.ppermute(array, 'dp', [(i, i ^ bit) for i in range(lax.axis_size('dp'...  33.6 us
    ppermute x18, waiting for transfers between devices, to_mp(): lax.ppermute(array, 'mp', [(i, (i + step) % size) for i in range(size)])  30 us
    ppermute x18, starting transfers between devices, to_mp(): lax.ppermute(array, 'mp', [(i, (i + step) % size) for i in range(size)])  21.2 us
    convert_element_type x9, other arithmetic, rounded_sum(): return (left.astype(f32) + right.astype(f32)).astype(bf16)  16.3 us
    unnamed x126, local copies, waits for them, and re-layouts  14 us
  transfers between devices with their start and end apart: 60, of which 25 were waited for; matrix products, arithmetic and copies ran while one was open for 11% of the time, Pallas kernels for 21%

profile of v4, /device:TPU:0, one launch (start us, length us, event | category | flops | bytes accessed | tf_op | source)
XLA Modules:
  0.0 364.7 jit_solution(1450479299673525829)
XLA Ops:
  7.9 2.6 weight_blocks.1
  10.5 3.1 collective-permute-start.5
  13.6 2.6 collective-permute-start.4
  17.6 3.1 collective-permute-done.5
  20.6 5.5 %collective-permute-done.4 = bf16[96,768]{1,0:T(8,128)(2,1)S(1)} collective-permute-done((bf16[96,768]{1,0:T(8,128)(2,1)}, bf16[96,768]{1,0:T(8,128)(2,1)S(1)}, u32[]{:S(2)}, u32[]{:S(2)}) %collective-permute-start.4) | collective-permute-done | bytes 147488 | tf_op jit(solution)/shard_map/ppermute | solution.py:35
  28.0 4.7 %collective-permute-start = (bf16[128,768]{1,0:T(8,128)(2,1)S(1)}, bf16[128,768]{1,0:T(8,128)(2,1)S(1)}, u32[]{:S(2)}, u32[]{:S(2)}) collective-permute-start(bf16[128,768]{1,0:T(8,128)(2,1)S(1)} %copy-done.15), channel_id=1, source_target_pairs={{0,3},{1,0},{2,1},{3,2},{4,7},{5,4},{6,5},{7,6},{8,11},{9,8},{10,9... | collective-permute-start | bytes 589832 | tf_op jit(solution)/shard_map/ppermute | solution.py:35
  48.2 2.5 collective-permute-done.1.g2
  52.4 2.1 collective-permute-start.12
  54.5 8.0 %collective-permute-done.14 = bf16[2,96,768]{2,1,0:T(8,128)(2,1)S(1)} collective-permute-done((bf16[2,96,768]{2,1,0:T(8,128)(2,1)S(1)}, bf16[2,96,768]{2,1,0:T(8,128)(2,1)S(1)}, u32[]{:S(2)}, u32[]{:S(2)}) %collective-permute-start.14) | collective-permute-done | bytes 294944 | tf_op jit(solution)/shard_map/ppermute | solution.py:35
  62.5 10.9 %collective-permute-done.13 = bf16[2,96,768]{2,1,0:T(8,128)(2,1)S(1)} collective-permute-done((bf16[2,96,768]{2,1,0:T(8,128)(2,1)S(1)}, bf16[2,96,768]{2,1,0:T(8,128)(2,1)S(1)}, u32[]{:S(2)}, u32[]{:S(2)}) %collective-permute-start.13) | collective-permute-done | bytes 294944 | tf_op jit(solution)/shard_map/ppermute | solution.py:35
  74.8 7.5 %encoder_forward.1 = (f32[128,768]{1,0:T(8,128)}, bf16[128,768]{1,0:T(8,128)(2,1)}, bf16[192,768]{1,0:T(8,128)(2,1)}, bf16[4,128,192]{2,1,0:T(8,128)(2,1)}, bf16...) custom-call(s32[3]{0:T(128)} %pad_add_fusion.2.place_ref.refs_0_, bf16[128,768]{1,0:T(8,128)(2,1)} %refs_7_.3, ...), custom_call_target="tpu_custom_call" | custom-call | bytes 1024 | tf_op jit(solution)/shard_map/encoder_forward/pallas_call | solution.py:566
  82.3 6.3 %collective-permute-start.6 = (bf16[128,768]{1,0:T(8,128)(2,1)}, bf16[128,768]{1,0:T(8,128)(2,1)S(1)}, u32[]{:S(2)}, u32[]{:S(2)}) collective-permute-start(bf16[128,768]{1,0:T(8,128)(2,1)} %get-tuple-element.158.c0), channel_id=1, source_target_pairs={{0,3},{1,0},{2,1},{3,2},{4,7},{5,4},{6,5},{7,6},{8,11},{9,8},{10,9... | collective-permute-start | bytes 589832 | tf_op jit(solution)/shard_map/ppermute | solution.py:35
  89.7 4.5 %collective-permute-done.6.c1 = bf16[128,768]{1,0:T(8,128)(2,1)S(1)} collective-permute-done((bf16[128,768]{1,0:T(8,128)(2,1)}, bf16[128,768]{1,0:T(8,128)(2,1)S(1)}, u32[]{:S(2)}, u32[]{:S(2)}) %collective-permute-start.6) | collective-permute-done | bytes 196640 | tf_op jit(solution)/shard_map/ppermute | solution.py:35
  94.3 12.2 %collective-permute-done.7.c2 = bf16[128,768]{1,0:T(8,128)(2,1)S(1)} collective-permute-done((bf16[128,768]{1,0:T(8,128)(2,1)}, bf16[128,768]{1,0:T(8,128)(2,1)S(1)}, u32[]{:S(2)}, u32[]{:S(2)}) %collective-permute-start.7) | collective-permute-done | bytes 196640 | tf_op jit(solution)/shard_map/ppermute | solution.py:35
  107.4 3.5 encoder_ffn_first.1
  111.6 3.2 collective-permute-start.11
  114.8 5.9 %collective-permute-done.9.refs_2_ = bf16[128,768]{1,0:T(8,128)(2,1)S(1)} collective-permute-done((bf16[128,768]{1,0:T(8,128)(2,1)S(1)}, bf16[128,768]{1,0:T(8,128)(2,1)S(1)}, u32[]{:S(2)}, u32[]{:S(2)}) %collective-permute-start.9) | collective-permute-done | bytes 196640 | tf_op jit(solution)/shard_map/ppermute | solution.py:40
  120.8 5.8 %collective-permute-done.10.refs_3_ = bf16[128,768]{1,0:T(8,128)(2,1)S(1)} collective-permute-done((bf16[128,768]{1,0:T(8,128)(2,1)S(1)}, bf16[128,768]{1,0:T(8,128)(2,1)S(1)}, u32[]{:S(2)}, u32[]{:S(2)}) %collective-permute-start.10) | collective-permute-done | bytes 196640 | tf_op jit(solution)/shard_map/ppermute | solution.py:40
  126.6 5.0 %collective-permute-start.15 = (bf16[128,768]{1,0:T(8,128)(2,1)S(1)}, bf16[128,768]{1,0:T(8,128)(2,1)S(1)}, u32[]{:S(2)}, u32[]{:S(2)}) collective-permute-start(bf16[128,768]{1,0:T(8,128)(2,1)S(1)} %copy-done.16), channel_id=1, source_target_pairs={{0,3},{1,0},{2,1},{3,2},{4,7},{5,4},{6,5},{7,6},{8,11},{9,8},{10,9... | collective-permute-start | bytes 589832 | tf_op jit(solution)/shard_map/ppermute | solution.py:35
  132.7 4.5 %encoder_ffn_second.1 = (bf16[512,768]{1,0:T(8,128)(2,1)}, bf16[2,4,3,96,768]{4,3,2,1,0:T(8,128)(2,1)S(1)}, bf16[2,4,3,96,768]{4,3,2,1,0:T(8,128)(2,1)S(1)}) custom-call(s32[3]{0:T(128)S(1)} %copy-done.21, bf16[512,768]{1,0:T(8,128)(2,1)S(1)} %get-tuple-element.161.c_all, bf16[512,768]{1,0:T(8,128)(2,1)S(1)} %get-tuple-element.162.g_all, ...), custom_call_target="tpu_custom_call" | custom-call | bytes 1024 | tf_op jit(solution)/shard_map/encoder_ffn_second/pallas_call | solution.py:566
  140.8 12.9 %encoder_backward.1 = (f32[128,768]{1,0:T(8,128)}, f32[1,768]{1,0:T(1,128)}, bf16[2,4,3,96,768]{4,3,2,1,0:T(8,128)(2,1)}, bf16[2,4,3,96,768]{4,3,2,1,0:T(8,128)(...) custom-call(s32[3]{0:T(128)} %pad_add_fusion.2.place_ref.refs_0_, ...), custom_call_target="tpu_custom_call", output_to_operand_aliasing={{2}: (16, {}), {3}: (17, {})} | custom-call | bytes 1024 | tf_op jit(solution)/shard_map/encoder_backward/pallas_call | solution.py:566
  154.1 7.1 %self_forward.1 = (f32[128,768]{1,0:T(8,128)}, bf16[128,768]{1,0:T(8,128)(2,1)}, bf16[128,768]{1,0:T(8,128)(2,1)}, bf16[4,128,192]{2,1,0:T(8,128)(2,1)}, bf16[4,...) custom-call(s32[3]{0:T(128)} %pad_add_fusion.2.place_ref.refs_0_, bf16[128,768]{1,0:T(8,128)(2,1)} %refs_2_.5, ...), custom_call_target="tpu_custom_call" | custom-call | bytes 1024 | tf_op jit(solution)/shard_map/self_forward/pallas_call | solution.py:566
  161.2 4.5 %fusion.5 = (bf16[2,3,96,768]{3,2,1,0:T(8,128)(2,1)}, bf16[2,3,96,768]{3,2,1,0:T(8,128)(2,1)}, bf16[2,3,96,768]{3,2,1,0:T(8,128)(2,1)}, bf16[2,3,96,768]{3,2,1,0:T(8,128)(2,1)}) fusion(bf16[2,4,3,96,768]{4,3,2,1,0:T(8,128)(2,1)} %collective-permute-done.18, bf16[2,4,3,96,768]{4,3,2,1,0:T(8,128)(2,1)S(1)} %copy-done.3), kind=kLoop, calls=%fused_computation.21 | loop fusion | flops 7077888 | bytes 10616832 | tf_op jit(solution)/shard_map/convert_element_type | solution.py:59
  167.2 6.5 %cross_forward.1 = (f32[128,768]{1,0:T(8,128)}, bf16[128,768]{1,0:T(8,128)(2,1)}, bf16[128,768]{1,0:T(8,128)(2,1)}, bf16[4,128,192]{2,1,0:T(8,128)(2,1)}, bf16[4...) custom-call(s32[3]{0:T(128)} %pad_add_fusion.2.place_ref.refs_0_, f32[128,768]{1,0:T(8,128)} %get-tuple-element.183.refs_1_.refs_7_, ...), custom_call_target="tpu_custom_call" | custom-call | bytes 1024 | tf_op jit(solution)/shard_map/cross_forward/pallas_call | solution.py:566
  173.8 3.5 collective-permute-start.19
  179.7 3.2 collective-permute-done.19.c1
  182.9 13.0 %collective-permute-done.20.c2 = bf16[128,768]{1,0:T(8,128)(2,1)S(1)} collective-permute-done((bf16[128,768]{1,0:T(8,128)(2,1)}, bf16[128,768]{1,0:T(8,128)(2,1)S(1)}, u32[]{:S(2)}, u32[]{:S(2)}) %collective-permute-start.20) | collective-permute-done | bytes 196640 | tf_op jit(solution)/shard_map/ppermute | solution.py:35
  196.9 3.3 decoder_ffn_first.1
  200.3 8.0 %collective-permute-done.22.refs_2_ = bf16[128,768]{1,0:T(8,128)(2,1)S(1)} collective-permute-done((bf16[128,768]{1,0:T(8,128)(2,1)S(1)}, bf16[128,768]{1,0:T(8,128)(2,1)S(1)}, u32[]{:S(2)}, u32[]{:S(2)}) %collective-permute-start.22) | collective-permute-done | bytes 196640 | tf_op jit(solution)/shard_map/ppermute | solution.py:40
  213.9 3.6 decoder_ffn_second.1
  226.7 2.6 collective-permute-start.30
  230.6 10.6 %cross_backward.1 = (f32[128,768]{1,0:T(8,128)}, f32[1,768]{1,0:T(1,128)}, bf16[2,4,3,96,768]{4,3,2,1,0:T(8,128)(2,1)}, bf16[2,4,3,96,768]{4,3,2,1,0:T(8,128)(2,...) custom-call(s32[3]{0:T(128)} %pad_add_fusion.2.place_ref.refs_0_, ...), custom_call_target="tpu_custom_call", output_to_operand_aliasing={{2}: (15, {}), {3}: (16, {})} | custom-call | bytes 1024 | tf_op jit(solution)/shard_map/cross_backward/pallas_call | solution.py:566
  241.3 6.4 %collective-permute-done.32 = bf16[2,4,3,96,768]{4,3,2,1,0:T(8,128)(2,1)S(1)} collective-permute-done((bf16[2,4,3,96,768]{4,3,2,1,0:T(8,128)(2,1)}, bf16[2,4,3,96,768]{4,3,2,1,0:T(8,128)(2,1)S(1)}, u32[]{:S(2)}, u32[]{:S(2)}) %collective-permute-start.32) | collective-permute-done | bytes 3538976 | tf_op jit(solution)/shard_map/ppermute | solution.py:44
  247.7 4.3 %fusion.9 = (bf16[2,3,96,768]{3,2,1,0:T(8,128)(2,1)S(1)}, bf16[2,3,96,768]{3,2,1,0:T(8,128)(2,1)}, bf16[2,3,96,768]{3,2,1,0:T(8,128)(2,1)}, bf16[2,3,96,768]{3,2,1,0:T(8,128)(2,1)S(1)}) fusion(bf16[2,4,3,96,768]{4,3,2,1,0:T(8,128)(2,1)S(1)} %collective-permute-done.32, bf16[2,4,3,96,768]{4,3,2,1,0:T(8,128)(2,1)} %get-tuple-element.212), kind=kLoop, calls=%fused_computation.25 | loop fusion | flops 7077888 | bytes 10616832 | tf_op jit(solution)/shard_map/convert_element_type | solution.py:59
  254.1 2.9 collective-permute-start.37
  257.1 10.6 %self_backward.1 = (f32[128,768]{1,0:T(8,128)}, f32[1,768]{1,0:T(1,128)}, bf16[2,4,2,96,768]{4,3,2,1,0:T(8,128)(2,1)}, bf16[2,4,2,96,768]{4,3,2,1,0:T(8,128)(2,1)}, f32[12,32,8,128]{3,2,1,0:T(8,128)}) custom-call(s32[3]{0:T(128)} %pad_add_fusion.2.place_ref.refs_0_, f32[128,768]{1,0:T(8,128)} %get-tuple-element.219.refs_1_, bf16[128,768]{1,0:T(8,128)(2,1)} %refs_2_.5, ...), custom_call_target="tpu_custom_call" | custom-call | bytes 1024 | tf_op jit(solution)/shard_map/self_backward/pallas_call | solution.py:566
  267.8 6.8 %collective-permute-done.36 = bf16[176,768]{1,0:T(8,128)(2,1)S(1)} collective-permute-done((bf16[176,768]{1,0:T(8,128)(2,1)S(1)}, bf16[176,768]{1,0:T(8,128)(2,1)S(1)}, u32[]{:S(2)}, u32[]{:S(2)}) %collective-permute-start.36) | collective-permute-done | bytes 270368 | tf_op jit(solution)/shard_map/ppermute | solution.py:40
  274.7 2.1 copy-done.11
  278.9 5.9 %collective-permute-start.39 = (f32[64,128]{1,0:T(8,128)S(1)}, f32[64,128]{1,0:T(8,128)S(1)}, u32[]{:S(2)}, u32[]{:S(2)}) collective-permute-start(f32[64,128]{1,0:T(8,128)S(1)} %pack.1), channel_id=1, source_target_pairs={{0,1},{1,0},{2,3},{3,2},{4,5},{5,4},{6,7},{7,6},{8,9},{9,8},{10,11... | collective-permute-start | bytes 98312 | tf_op jit(solution)/shard_map/ppermute | solution.py:145
  287.7 3.8 %collective-permute-done.40 = f32[64,128]{1,0:T(8,128)S(1)} collective-permute-done((f32[64,128]{1,0:T(8,128)S(1)}, f32[64,128]{1,0:T(8,128)S(1)}, u32[]{:S(2)}, u32[]{:S(2)}) %collective-permute-start.40) | collective-permute-done | bytes 32800 | tf_op jit(solution)/shard_map/ppermute | solution.py:145
  298.2 2.5 fusion.13
  301.6 8.5 %collective-permute-done.44 = bf16[3,96,768]{2,1,0:T(8,128)(2,1)S(1)} collective-permute-done((bf16[3,96,768]{2,1,0:T(8,128)(2,1)S(1)}, bf16[3,96,768]{2,1,0:T(8,128)(2,1)S(1)}, u32[]{:S(2)}, u32[]{:S(2)}) %collective-permute-start.44) | collective-permute-done | bytes 442400 | tf_op jit(solution)/shard_map/ppermute | solution.py:44
  313.1 2.1 collective-permute-start.43
  316.7 8.4 %collective-permute-done.47 = bf16[2,2,96,768]{3,2,1,0:T(8,128)(2,1)S(1)} collective-permute-done((bf16[2,2,96,768]{3,2,1,0:T(8,128)(2,1)S(1)}, bf16[2,2,96,768]{3,2,1,0:T(8,128)(2,1)S(1)}, u32[]{:S(2)}, u32[]{:S(2)}) %collective-permute-start.47) | collective-permute-done | bytes 589856 | tf_op jit(solution)/shard_map/ppermute | solution.py:44
  326.9 3.5 collective-permute-done.46.got3
  332.9 1.9 collective-permute-done.48
  335.6 3.3 collective-permute-done.50
  355.5 2.2 table.1
  (286 shorter events, 91.9 us)
Async XLA Ops:
  7.2 67.6 %all-gather.7.cloned.1.call-start = ((), (), s32[]{:S(2)}) async-start(), calls=%async_computation.2 | async-start | bytes 5308416 | tf_op jit(solution)/shard_map/all_gather | solution.py:139
  10.5 10.1 %collective-permute-start.5 = (bf16[96,768]{1,0:T(8,128)(2,1)}, bf16[96,768]{1,0:T(8,128)(2,1)S(1)}, u32[]{:S(2)}, u32[]{:S(2)}) collective-permute-start(bf16[96,768]{1,0:T(8,128)(2,1)} %get-tuple-element.153), channel_id=1, source_target_pairs={{0,1},{1,2},{2,3},{3,0},{4,5},{5,6},{6,7},{7,4},{8,9},{9,10},{10,1... | collective-permute-start | bytes 442376 | tf_op jit(solution)/shard_map/ppermute | solution.py:35
  13.6 12.5 %collective-permute-start.4 = (bf16[96,768]{1,0:T(8,128)(2,1)}, bf16[96,768]{1,0:T(8,128)(2,1)S(1)}, u32[]{:S(2)}, u32[]{:S(2)}) collective-permute-start(bf16[96,768]{1,0:T(8,128)(2,1)} %get-tuple-element.153), channel_id=1, source_target_pairs={{0,2},{1,3},{2,0},{3,1},{4,6},{5,7},{6,4},{7,5},{8,10},{9,11},{10,... | collective-permute-start | bytes 442376 | tf_op jit(solution)/shard_map/ppermute | solution.py:35
  16.2 9.9 %collective-permute-start.3 = (bf16[96,768]{1,0:T(8,128)(2,1)}, bf16[96,768]{1,0:T(8,128)(2,1)S(1)}, u32[]{:S(2)}, u32[]{:S(2)}) collective-permute-start(bf16[96,768]{1,0:T(8,128)(2,1)} %get-tuple-element.153), channel_id=1, source_target_pairs={{0,3},{1,0},{2,1},{3,2},{4,7},{5,4},{6,5},{7,6},{8,11},{9,8},{10,9... | collective-permute-start | bytes 442376 | tf_op jit(solution)/shard_map/ppermute | solution.py:35
  28.0 126.1 %all-gather.9.cloned.1.call-start = ((), (), s32[]{:S(2)}) async-start(), calls=%async_computation.3 | async-start | bytes 10616832 | tf_op jit(solution)/shard_map/all_gather | solution.py:139
  28.0 20.2 %collective-permute-start = (bf16[128,768]{1,0:T(8,128)(2,1)S(1)}, bf16[128,768]{1,0:T(8,128)(2,1)S(1)}, u32[]{:S(2)}, u32[]{:S(2)}) collective-permute-start(bf16[128,768]{1,0:T(8,128)(2,1)S(1)} %copy-done.15), channel_id=1, source_target_pairs={{0,3},{1,0},{2,1},{3,2},{4,7},{5,4},{6,5},{7,6},{8,11},{9,8},{10,9... | collective-permute-start | bytes 589832 | tf_op jit(solution)/shard_map/ppermute | solution.py:35
  32.8 17.9 %collective-permute-start.1 = (bf16[128,768]{1,0:T(8,128)(2,1)S(1)}, bf16[128,768]{1,0:T(8,128)(2,1)}, u32[]{:S(2)}, u32[]{:S(2)}) collective-permute-start(bf16[128,768]{1,0:T(8,128)(2,1)S(1)} %copy-done.15), channel_id=1, source_target_pairs={{0,2},{1,3},{2,0},{3,1},{4,6},{5,7},{6,4},{7,5},{8,10},{9,11},{10,... | collective-permute-start | bytes 589832 | tf_op jit(solution)/shard_map/ppermute | solution.py:35
  33.2 17.5 %collective-permute-start.2 = (bf16[128,768]{1,0:T(8,128)(2,1)S(1)}, bf16[128,768]{1,0:T(8,128)(2,1)}, u32[]{:S(2)}, u32[]{:S(2)}) collective-permute-start(bf16[128,768]{1,0:T(8,128)(2,1)S(1)} %copy-done.15), channel_id=1, source_target_pairs={{0,1},{1,2},{2,3},{3,0},{4,5},{5,6},{6,7},{7,4},{8,9},{9,10},{10,1... | collective-permute-start | bytes 589832 | tf_op jit(solution)/shard_map/ppermute | solution.py:35
  50.7 11.8 %collective-permute-start.14 = (bf16[2,96,768]{2,1,0:T(8,128)(2,1)S(1)}, bf16[2,96,768]{2,1,0:T(8,128)(2,1)S(1)}, u32[]{:S(2)}, u32[]{:S(2)}) collective-permute-start(bf16[2,96,768]{2,1,0:T(8,128)(2,1)S(1)} %copy-done.44), channel_id=1, source_target_pairs={{0,1},{1,2},{2,3},{3,0},{4,5},{5,6},{6,7},{7,4},{8,9},{9,10},{10,1... | collective-permute-start | bytes 884744 | tf_op jit(solution)/shard_map/ppermute | solution.py:35
  51.1 22.3 %collective-permute-start.13 = (bf16[2,96,768]{2,1,0:T(8,128)(2,1)S(1)}, bf16[2,96,768]{2,1,0:T(8,128)(2,1)S(1)}, u32[]{:S(2)}, u32[]{:S(2)}) collective-permute-start(bf16[2,96,768]{2,1,0:T(8,128)(2,1)S(1)} %copy-done.44), channel_id=1, source_target_pairs={{0,2},{1,3},{2,0},{3,1},{4,6},{5,7},{6,4},{7,5},{8,10},{9,11},{10,... | collective-permute-start | bytes 884744 | tf_op jit(solution)/shard_map/ppermute | solution.py:35
  52.4 21.0 %collective-permute-start.12 = (bf16[2,96,768]{2,1,0:T(8,128)(2,1)S(1)}, bf16[2,96,768]{2,1,0:T(8,128)(2,1)S(1)}, u32[]{:S(2)}, u32[]{:S(2)}) collective-permute-start(bf16[2,96,768]{2,1,0:T(8,128)(2,1)S(1)} %copy-done.44), channel_id=1, source_target_pairs={{0,3},{1,0},{2,1},{3,2},{4,7},{5,4},{6,5},{7,6},{8,11},{9,8},{10,9... | collective-permute-start | bytes 884744 | tf_op jit(solution)/shard_map/ppermute | solution.py:35
  74.7 105.0 %reduce-scatter.2.cloned.1.call-start = ((), (), s32[]{:S(2)}) async-start(), calls=%async_computation.1 | async-start | bytes 983040 | tf_op jit(solution)/shard_map/reduce_scatter | solution.py:863
  82.3 11.9 %collective-permute-start.6 = (bf16[128,768]{1,0:T(8,128)(2,1)}, bf16[128,768]{1,0:T(8,128)(2,1)S(1)}, u32[]{:S(2)}, u32[]{:S(2)}) collective-permute-start(bf16[128,768]{1,0:T(8,128)(2,1)} %get-tuple-element.158.c0), channel_id=1, source_target_pairs={{0,3},{1,0},{2,1},{3,2},{4,7},{5,4},{6,5},{7,6},{8,11},{9,8},{10,9... | collective-permute-start | bytes 589832 | tf_op jit(solution)/shard_map/ppermute | solution.py:35
  88.6 17.9 %collective-permute-start.7 = (bf16[128,768]{1,0:T(8,128)(2,1)}, bf16[128,768]{1,0:T(8,128)(2,1)S(1)}, u32[]{:S(2)}, u32[]{:S(2)}) collective-permute-start(bf16[128,768]{1,0:T(8,128)(2,1)} %get-tuple-element.158.c0), channel_id=1, source_target_pairs={{0,2},{1,3},{2,0},{3,1},{4,6},{5,7},{6,4},{7,5},{8,10},{9,11},{10,... | collective-permute-start | bytes 589832 | tf_op jit(solution)/shard_map/ppermute | solution.py:35
  89.7 16.8 %collective-permute-start.8 = (bf16[128,768]{1,0:T(8,128)(2,1)}, bf16[128,768]{1,0:T(8,128)(2,1)S(1)}, u32[]{:S(2)}, u32[]{:S(2)}) collective-permute-start(bf16[128,768]{1,0:T(8,128)(2,1)} %get-tuple-element.158.c0), channel_id=1, source_target_pairs={{0,1},{1,2},{2,3},{3,0},{4,5},{5,6},{6,7},{7,4},{8,9},{9,10},{10,1... | collective-permute-start | bytes 589832 | tf_op jit(solution)/shard_map/ppermute | solution.py:35
  111.0 9.8 %collective-permute-start.9 = (bf16[128,768]{1,0:T(8,128)(2,1)S(1)}, bf16[128,768]{1,0:T(8,128)(2,1)S(1)}, u32[]{:S(2)}, u32[]{:S(2)}) collective-permute-start(bf16[128,768]{1,0:T(8,128)(2,1)S(1)} %get-tuple-element.393), channel_id=1, source_target_pairs={{0,1},{1,2},{2,3},{3,0},{4,5},{5,6},{6,7},{7,4},{8,9},{9,10},{10,1... | collective-permute-start | bytes 589832 | tf_op jit(solution)/shard_map/ppermute | solution.py:40
  111.0 15.6 %collective-permute-start.10 = (bf16[128,768]{1,0:T(8,128)(2,1)S(1)}, bf16[128,768]{1,0:T(8,128)(2,1)S(1)}, u32[]{:S(2)}, u32[]{:S(2)}) collective-permute-start(bf16[128,768]{1,0:T(8,128)(2,1)S(1)} %get-tuple-element.392), channel_id=1, source_target_pairs={{0,2},{1,3},{2,0},{3,1},{4,6},{5,7},{6,4},{7,5},{8,10},{9,11},{10,... | collective-permute-start | bytes 589832 | tf_op jit(solution)/shard_map/ppermute | solution.py:40
  111.6 15.0 %collective-permute-start.11 = (bf16[128,768]{1,0:T(8,128)(2,1)S(1)}, bf16[128,768]{1,0:T(8,128)(2,1)S(1)}, u32[]{:S(2)}, u32[]{:S(2)}) collective-permute-start(bf16[128,768]{1,0:T(8,128)(2,1)S(1)} %get-tuple-element.391), channel_id=1, source_target_pairs={{0,3},{1,0},{2,1},{3,2},{4,7},{5,4},{6,5},{7,6},{8,11},{9,8},{10,9... | collective-permute-start | bytes 589832 | tf_op jit(solution)/shard_map/ppermute | solution.py:40
  126.6 27.1 %collective-permute-start.15 = (bf16[128,768]{1,0:T(8,128)(2,1)S(1)}, bf16[128,768]{1,0:T(8,128)(2,1)S(1)}, u32[]{:S(2)}, u32[]{:S(2)}) collective-permute-start(bf16[128,768]{1,0:T(8,128)(2,1)S(1)} %copy-done.16), channel_id=1, source_target_pairs={{0,3},{1,0},{2,1},{3,2},{4,7},{5,4},{6,5},{7,6},{8,11},{9,8},{10,9... | collective-permute-start | bytes 589832 | tf_op jit(solution)/shard_map/ppermute | solution.py:35
  131.6 22.1 %collective-permute-start.16 = (bf16[128,768]{1,0:T(8,128)(2,1)S(1)}, bf16[128,768]{1,0:T(8,128)(2,1)S(1)}, u32[]{:S(2)}, u32[]{:S(2)}) collective-permute-start(bf16[128,768]{1,0:T(8,128)(2,1)S(1)} %copy-done.16), channel_id=1, source_target_pairs={{0,2},{1,3},{2,0},{3,1},{4,6},{5,7},{6,4},{7,5},{8,10},{9,11},{10,... | collective-permute-start | bytes 589832 | tf_op jit(solution)/shard_map/ppermute | solution.py:35
  131.9 21.8 %collective-permute-start.17 = (bf16[128,768]{1,0:T(8,128)(2,1)S(1)}, bf16[128,768]{1,0:T(8,128)(2,1)S(1)}, u32[]{:S(2)}, u32[]{:S(2)}) collective-permute-start(bf16[128,768]{1,0:T(8,128)(2,1)S(1)} %copy-done.16), channel_id=1, source_target_pairs={{0,1},{1,2},{2,3},{3,0},{4,5},{5,6},{6,7},{7,4},{8,9},{9,10},{10,1... | collective-permute-start | bytes 589832 | tf_op jit(solution)/shard_map/ppermute | solution.py:35
  153.8 200.0 %all-gather.11.cloned.1.call-start = ((), (), s32[]{:S(2)}) async-start(), calls=%async_computation.4 | async-start | bytes 2654208 | tf_op jit(solution)/shard_map/all_gather | solution.py:941
  165.7 42.7 %collective-permute-start.24 = (bf16[2,3,96,768]{3,2,1,0:T(8,128)(2,1)}, bf16[2,3,96,768]{3,2,1,0:T(8,128)(2,1)}, u32[]{:S(2)}, u32[]{:S(2)}) collective-permute-start(bf16[2,3,96,768]{3,2,1,0:T(8,128)(2,1)} %get-tuple-element.366), channel_id=1, source_target_pairs={{0,16},{4,20},{8,24},{12,28},{16,0},{20,4},{24,8},{28,12},{1,17},{... | collective-permute-start | bytes 2654216 | tf_op jit(solution)/shard_map/ppermute | solution.py:44
  177.3 18.7 %collective-permute-start.20 = (bf16[128,768]{1,0:T(8,128)(2,1)}, bf16[128,768]{1,0:T(8,128)(2,1)S(1)}, u32[]{:S(2)}, u32[]{:S(2)}) collective-permute-start(bf16[128,768]{1,0:T(8,128)(2,1)} %get-tuple-element.190.c0), channel_id=1, source_target_pairs={{0,2},{1,3},{2,0},{3,1},{4,6},{5,7},{6,4},{7,5},{8,10},{9,11},{10,... | collective-permute-start | bytes 589832 | tf_op jit(solution)/shard_map/ppermute | solution.py:35
  178.1 17.9 %collective-permute-start.21 = (bf16[128,768]{1,0:T(8,128)(2,1)}, bf16[128,768]{1,0:T(8,128)(2,1)}, u32[]{:S(2)}, u32[]{:S(2)}) collective-permute-start(bf16[128,768]{1,0:T(8,128)(2,1)} %get-tuple-element.190.c0), channel_id=1, source_target_pairs={{0,1},{1,2},{2,3},{3,0},{4,5},{5,6},{6,7},{7,4},{8,9},{9,10},{10,1... | collective-permute-start | bytes 589832 | tf_op jit(solution)/shard_map/ppermute | solution.py:35
  178.2 34.0 %collective-permute-start.23 = (bf16[2,3,96,768]{3,2,1,0:T(8,128)(2,1)}, bf16[2,3,96,768]{3,2,1,0:T(8,128)(2,1)}, u32[]{:S(2)}, u32[]{:S(2)}) collective-permute-start(bf16[2,3,96,768]{3,2,1,0:T(8,128)(2,1)} %get-tuple-element.368), channel_id=1, source_target_pairs={{0,8},{4,12},{8,0},{12,4},{16,24},{20,28},{24,16},{28,20},{1,9},{5... | collective-permute-start | bytes 2654216 | tf_op jit(solution)/shard_map/ppermute | solution.py:44
  209.6 10.6 %collective-permute-start.26 = (bf16[3,96,768]{2,1,0:T(8,128)(2,1)S(1)}, bf16[3,96,768]{2,1,0:T(8,128)(2,1)S(1)}, u32[]{:S(2)}, u32[]{:S(2)}) collective-permute-start(bf16[3,96,768]{2,1,0:T(8,128)(2,1)S(1)} %fusion.17), channel_id=1, source_target_pairs={{0,8},{4,12},{8,0},{12,4},{16,24},{20,28},{24,16},{28,20},{1,9},{5... | collective-permute-start | bytes 1327112 | tf_op jit(solution)/shard_map/ppermute | solution.py:44
  211.2 14.1 %collective-permute-start.27 = (bf16[128,768]{1,0:T(8,128)(2,1)S(1)}, bf16[128,768]{1,0:T(8,128)(2,1)S(1)}, u32[]{:S(2)}, u32[]{:S(2)}) collective-permute-start(bf16[128,768]{1,0:T(8,128)(2,1)S(1)} %get-tuple-element.389), channel_id=1, source_target_pairs={{0,2},{1,3},{2,0},{3,1},{4,6},{5,7},{6,4},{7,5},{8,10},{9,11},{10,... | collective-permute-start | bytes 589832 | tf_op jit(solution)/shard_map/ppermute | solution.py:40
  211.3 14.1 %collective-permute-start.28 = (bf16[128,768]{1,0:T(8,128)(2,1)S(1)}, bf16[128,768]{1,0:T(8,128)(2,1)S(1)}, u32[]{:S(2)}, u32[]{:S(2)}) collective-permute-start(bf16[128,768]{1,0:T(8,128)(2,1)S(1)} %get-tuple-element.388), channel_id=1, source_target_pairs={{0,3},{1,0},{2,1},{3,2},{4,7},{5,4},{6,5},{7,6},{8,11},{9,8},{10,9... | collective-permute-start | bytes 589832 | tf_op jit(solution)/shard_map/ppermute | solution.py:40
  213.3 10.1 %collective-permute-start.25 = (bf16[3,96,768]{2,1,0:T(8,128)(2,1)S(1)}, bf16[3,96,768]{2,1,0:T(8,128)(2,1)S(1)}, u32[]{:S(2)}, u32[]{:S(2)}) collective-permute-start(bf16[3,96,768]{2,1,0:T(8,128)(2,1)S(1)} %fusion.16), channel_id=1, source_target_pairs={{0,16},{4,20},{8,24},{12,28},{16,0},{20,4},{24,8},{28,12},{1,17},{... | collective-permute-start | bytes 1327112 | tf_op jit(solution)/shard_map/ppermute | solution.py:44
  225.4 15.8 %collective-permute-start.29 = (bf16[96,768]{1,0:T(8,128)(2,1)S(1)}, bf16[96,768]{1,0:T(8,128)(2,1)S(1)}, u32[]{:S(2)}, u32[]{:S(2)}) collective-permute-start(bf16[96,768]{1,0:T(8,128)(2,1)S(1)} %slice_bitcast_fusion.14), channel_id=1, source_target_pairs={{0,1},{1,2},{2,3},{3,0},{4,5},{5,6},{6,7},{7,4},{8,9},{9,10},{10,1... | collective-permute-start | bytes 442376 | tf_op jit(solution)/shard_map/ppermute | solution.py:40
  226.7 14.5 %collective-permute-start.30 = (bf16[96,768]{1,0:T(8,128)(2,1)S(1)}, bf16[96,768]{1,0:T(8,128)(2,1)S(1)}, u32[]{:S(2)}, u32[]{:S(2)}) collective-permute-start(bf16[96,768]{1,0:T(8,128)(2,1)S(1)} %get-tuple-element.215), channel_id=1, source_target_pairs={{0,2},{1,3},{2,0},{3,1},{4,6},{5,7},{6,4},{7,5},{8,10},{9,11},{10,... | collective-permute-start | bytes 442376 | tf_op jit(solution)/shard_map/ppermute | solution.py:40
  229.3 12.0 %collective-permute-start.31 = (bf16[96,768]{1,0:T(8,128)(2,1)S(1)}, bf16[96,768]{1,0:T(8,128)(2,1)S(1)}, u32[]{:S(2)}, u32[]{:S(2)}) collective-permute-start(bf16[96,768]{1,0:T(8,128)(2,1)S(1)} %get-tuple-element.216), channel_id=1, source_target_pairs={{0,3},{1,0},{2,1},{3,2},{4,7},{5,4},{6,5},{7,6},{8,11},{9,8},{10,9... | collective-permute-start | bytes 442376 | tf_op jit(solution)/shard_map/ppermute | solution.py:40
  252.0 22.5 %collective-permute-start.33 = (bf16[2,3,96,768]{3,2,1,0:T(8,128)(2,1)}, bf16[2,3,96,768]{3,2,1,0:T(8,128)(2,1)S(1)}, u32[]{:S(2)}, u32[]{:S(2)}) collective-permute-start(bf16[2,3,96,768]{3,2,1,0:T(8,128)(2,1)} %get-tuple-element.364), channel_id=1, source_target_pairs={{0,8},{4,12},{8,0},{12,4},{16,24},{20,28},{24,16},{28,20},{1,9},{5... | collective-permute-start | bytes 2654216 | tf_op jit(solution)/shard_map/ppermute | solution.py:44
  252.5 22.0 %collective-permute-start.34 = (bf16[2,3,96,768]{3,2,1,0:T(8,128)(2,1)S(1)}, bf16[2,3,96,768]{3,2,1,0:T(8,128)(2,1)S(1)}, u32[]{:S(2)}, u32[]{:S(2)}) collective-permute-start(bf16[2,3,96,768]{3,2,1,0:T(8,128)(2,1)S(1)} %get-tuple-element.362), channel_id=1, source_target_pairs={{0,16},{4,20},{8,24},{12,28},{16,0},{20,4},{24,8},{28,12},{1,17},{... | collective-permute-start | bytes 2654216 | tf_op jit(solution)/shard_map/ppermute | solution.py:44
  253.0 14.8 %collective-permute-start.35 = (bf16[176,768]{1,0:T(8,128)(2,1)S(1)}, bf16[176,768]{1,0:T(8,128)(2,1)S(1)}, u32[]{:S(2)}, u32[]{:S(2)}) collective-permute-start(bf16[176,768]{1,0:T(8,128)(2,1)S(1)} %get-tuple-element.229), channel_id=1, source_target_pairs={{0,1},{1,2},{2,3},{3,0},{4,5},{5,6},{6,7},{7,4},{8,9},{9,10},{10,1... | collective-permute-start | bytes 811016 | tf_op jit(solution)/shard_map/ppermute | solution.py:40
  253.8 20.7 %collective-permute-start.36 = (bf16[176,768]{1,0:T(8,128)(2,1)S(1)}, bf16[176,768]{1,0:T(8,128)(2,1)S(1)}, u32[]{:S(2)}, u32[]{:S(2)}) collective-permute-start(bf16[176,768]{1,0:T(8,128)(2,1)S(1)} %get-tuple-element.230), channel_id=1, source_target_pairs={{0,2},{1,3},{2,0},{3,1},{4,6},{5,7},{6,4},{7,5},{8,10},{9,11},{10,... | collective-permute-start | bytes 811016 | tf_op jit(solution)/shard_map/ppermute | solution.py:40
  254.1 20.4 %collective-permute-start.37 = (bf16[176,768]{1,0:T(8,128)(2,1)S(1)}, bf16[176,768]{1,0:T(8,128)(2,1)S(1)}, u32[]{:S(2)}, u32[]{:S(2)}) collective-permute-start(bf16[176,768]{1,0:T(8,128)(2,1)S(1)} %get-tuple-element.231), channel_id=1, source_target_pairs={{0,3},{1,0},{2,1},{3,2},{4,7},{5,4},{6,5},{7,6},{8,11},{9,8},{10,9... | collective-permute-start | bytes 811016 | tf_op jit(solution)/shard_map/ppermute | solution.py:40
  274.6 23.7 %collective-permute-start.38 = (bf16[2,4,2,96,768]{4,3,2,1,0:T(8,128)(2,1)}, bf16[2,4,2,96,768]{4,3,2,1,0:T(8,128)(2,1)}, u32[]{:S(2)}, u32[]{:S(2)}) collective-permute-start(bf16[2,4,2,96,768]{4,3,2,1,0:T(8,128)(2,1)} %get-tuple-element.232), channel_id=1, source_target_pairs={{0,4},{4,0},{8,12},{12,8},{16,20},{20,16},{24,28},{28,24},{1,5},{5... | collective-permute-start | bytes 7077896 | tf_op jit(solution)/shard_map/ppermute | solution.py:44
  293.8 16.3 %collective-permute-start.44 = (bf16[3,96,768]{2,1,0:T(8,128)(2,1)S(1)}, bf16[3,96,768]{2,1,0:T(8,128)(2,1)S(1)}, u32[]{:S(2)}, u32[]{:S(2)}) collective-permute-start(bf16[3,96,768]{2,1,0:T(8,128)(2,1)S(1)} %fusion.19), channel_id=1, source_target_pairs={{0,8},{4,12},{8,0},{12,4},{16,24},{20,28},{24,16},{28,20},{1,9},{5... | collective-permute-start | bytes 1327112 | tf_op jit(solution)/shard_map/ppermute | solution.py:44
  296.6 16.3 %collective-permute-start.42 = (bf16[3,96,768]{2,1,0:T(8,128)(2,1)S(1)}, bf16[3,96,768]{2,1,0:T(8,128)(2,1)S(1)}, u32[]{:S(2)}, u32[]{:S(2)}) collective-permute-start(bf16[3,96,768]{2,1,0:T(8,128)(2,1)S(1)} %fusion.18), channel_id=1, source_target_pairs={{0,16},{4,20},{8,24},{12,28},{16,0},{20,4},{24,8},{28,12},{1,17},{... | collective-permute-start | bytes 1327112 | tf_op jit(solution)/shard_map/ppermute | solution.py:44
  300.7 24.3 %collective-permute-start.47 = (bf16[2,2,96,768]{3,2,1,0:T(8,128)(2,1)S(1)}, bf16[2,2,96,768]{3,2,1,0:T(8,128)(2,1)S(1)}, u32[]{:S(2)}, u32[]{:S(2)}) collective-permute-start(bf16[2,2,96,768]{3,2,1,0:T(8,128)(2,1)S(1)} %get-tuple-element.372), channel_id=1, source_target_pairs={{0,8},{4,12},{8,0},{12,4},{16,24},{20,28},{24,16},{28,20},{1,9},{5... | collective-permute-start | bytes 1769480 | tf_op jit(solution)/shard_map/ppermute | solution.py:44
  301.2 30.4 %collective-permute-start.49 = (bf16[2,2,96,768]{3,2,1,0:T(8,128)(2,1)S(1)}, bf16[2,2,96,768]{3,2,1,0:T(8,128)(2,1)S(1)}, u32[]{:S(2)}, u32[]{:S(2)}) collective-permute-start(bf16[2,2,96,768]{3,2,1,0:T(8,128)(2,1)S(1)} %get-tuple-element.370), channel_id=1, source_target_pairs={{0,16},{4,20},{8,24},{12,28},{16,0},{20,4},{24,8},{28,12},{1,17},{... | collective-permute-start | bytes 1769480 | tf_op jit(solution)/shard_map/ppermute | solution.py:44
  313.1 13.8 %collective-permute-start.43 = (bf16[96,768]{1,0:T(8,128)(2,1)S(1)}, bf16[96,768]{1,0:T(8,128)(2,1)S(1)}, u32[]{:S(2)}, u32[]{:S(2)}) collective-permute-start(bf16[96,768]{1,0:T(8,128)(2,1)S(1)} %fusion.41), channel_id=1, source_target_pairs={{0,1},{1,2},{2,3},{3,0},{4,5},{5,6},{6,7},{7,4},{8,9},{9,10},{10,1... | collective-permute-start | bytes 442376 | tf_op jit(solution)/shard_map/ppermute | solution.py:40
  316.0 11.0 %collective-permute-start.45 = (bf16[96,768]{1,0:T(8,128)(2,1)S(1)}, bf16[96,768]{1,0:T(8,128)(2,1)S(1)}, u32[]{:S(2)}, u32[]{:S(2)}) collective-permute-start(bf16[96,768]{1,0:T(8,128)(2,1)S(1)} %get-tuple-element.375), channel_id=1, source_target_pairs={{0,2},{1,3},{2,0},{3,1},{4,6},{5,7},{6,4},{7,5},{8,10},{9,11},{10,... | collective-permute-start | bytes 442376 | tf_op jit(solution)/shard_map/ppermute | solution.py:40
  325.1 9.6 %collective-permute-start.48 = (bf16[2,96,768]{2,1,0:T(8,128)(2,1)S(1)}, bf16[2,96,768]{2,1,0:T(8,128)(2,1)S(1)}, u32[]{:S(2)}, u32[]{:S(2)}) collective-permute-start(bf16[2,96,768]{2,1,0:T(8,128)(2,1)S(1)} %fusion.20), channel_id=1, source_target_pairs={{0,16},{4,20},{8,24},{12,28},{16,0},{20,4},{24,8},{28,12},{1,17},{... | collective-permute-start | bytes 884744 | tf_op jit(solution)/shard_map/ppermute | solution.py:44
  339.7 12.2 %collective-permute-start.53 = (bf16[96,768]{1,0:T(8,128)(2,1)}, bf16[96,768]{1,0:T(8,128)(2,1)}, u32[]{:S(2)}, u32[]{:S(2)}) collective-permute-start(bf16[96,768]{1,0:T(8,128)(2,1)} %fusion.44), channel_id=1, source_target_pairs={{0,1},{1,2},{2,3},{3,0},{4,5},{5,6},{6,7},{7,4},{8,9},{9,10},{10,1... | collective-permute-start | bytes 442376 | tf_op jit(solution)/shard_map/ppermute | solution.py:40
  342.6 9.3 %collective-permute-start.54 = (bf16[96,768]{1,0:T(8,128)(2,1)}, bf16[96,768]{1,0:T(8,128)(2,1)}, u32[]{:S(2)}, u32[]{:S(2)}) collective-permute-start(bf16[96,768]{1,0:T(8,128)(2,1)} %get-tuple-element.395), channel_id=1, source_target_pairs={{0,2},{1,3},{2,0},{3,1},{4,6},{5,7},{6,4},{7,5},{8,10},{9,11},{10,... | collective-permute-start | bytes 442376 | tf_op jit(solution)/shard_map/ppermute | solution.py:40
  (73 other events, 917.2 us)
Sparse Core Ops, SparseCore 0:
  28.1 41.2 all-gather.6
  74.8 62.7 all-gather.8
  153.9 24.5 reduce-scatter.1
  292.5 38.4 all-gather.10
